TPU v7x, 128 devices: a whole 4x4x4 slice. The times are simulated.
128 devices in a mesh: space: 4 (over y_hi, core), chan: 32 (over y_lo, x, z).
Axes of the slice: x: 4, y: 4 (y_hi: 2, y_lo: 2; y = y_hi * 2 + y_lo), z: 4, core: 2. Of those that a mesh axis runs over, the one named last changes fastest.
Arguments:
- point_feats: bfloat16 [262144, 256], P(('space', 'chan')), may hold values from -6 to 6
- send_slots: int32 [4, 32, 4, 1024], P('space', 'chan'), may hold values from 0 to 2047
- send_counts: int32 [4, 32, 4], P('space', 'chan'), may hold values from 1 to 1024, as said below
- neighbors: int32 [16, 32, 32, 128], P('space', 'chan'), may hold values from 0 to 4095, as said below
- tile_fill: int32 [16, 32, 32], P('space', 'chan'), may hold values from 16 to 128
- offsets: float32 [16, 32, 32, 3, 128], P('space', 'chan'), may hold values from -2.5 to 2.5
- weight: bfloat16 [256, 27, 256], P('chan'), may hold values from -0.078125 to 0.078125
- conv_bias: bfloat16 [256], replicated, may hold values from -3 to 3
- cotangent: bfloat16 [16, 128, 128, 256], P('space', 'chan'), may hold values from -6 to 6
Outputs:
- activated: bfloat16 [16, 128, 128, 256], P('space', 'chan')
- weight_grad: float32 [256, 27, 256], P('chan')
Inputs may be any that keep to these rules, and one draw needn't show every extreme that they name: `send_counts`: at most 1024 per device and owner; for every index of chan, one owner receives exactly 1024 from every source. `neighbors`: entry (z, a, b, s) is src * 1024 + j for a source index src of space and a slot j < send_counts[src, c, z // 4], with c the tile's index of chan.
All inputs are finite; a program needn't handle non-finite values.
Results may differ from a plain program's by a relative error of at most 0.0059.
Values may be sent and summed in bfloat16 or wider, within the bound.
No kernel may reach another device: no remote copies, remote signals or barrier semaphores. Data moves between devices by JAX's collectives and lax.ppermute only.
A program may use at most 192 MiB of HBM per device.

v0:
```python
import math

import jax
import jax.numpy as jnp
from jax import lax
from jax.sharding import PartitionSpec as P


def padded_2(block, sides, width):
    for axis, dim in sides:
        count = lax.axis_size(axis)
        forward = [(i, i + 1) for i in range(count - 1)]
        backward = [(target, source) for source, target in forward]
        low = lax.ppermute(
            lax.slice_in_dim(block, block.shape[dim] - width, None, axis=dim), axis, forward
        )
        high = lax.ppermute(lax.slice_in_dim(block, 0, width, axis=dim), axis, backward)
        block = jnp.concatenate([low, block, high], axis=dim)
    return block


def kernel_weights(offsets, fill_count):
    centres = jnp.arange(4, dtype=jnp.float32) - 1.5
    along_x = offsets[..., 0, :][..., None, None, :] - centres[:, None, None]
    along_y = offsets[..., 1, :][..., None, None, :] - centres[None, :, None]
    along_z = offsets[..., 2, :][..., None, None, :]
    values = jnp.exp(-0.5 * (along_x * along_x + along_y * along_y + along_z * along_z))
    in_use = jnp.arange(offsets.shape[-1], dtype=jnp.int32) < fill_count[..., None]
    return jnp.where(in_use[..., None, None, :], values, jnp.zeros((), values.dtype))


def conv_part(padded, weights):
    planes = padded.shape[0] - 2
    width_x = padded.shape[1] - 2
    width_y = padded.shape[2] - 2
    running = jnp.zeros((planes, width_x, width_y, weights.shape[2]), jnp.float32)
    for position in range(27):
        shift_z, shift_x, shift_y = (position // 9, position // 3 % 3, position % 3)
        window = padded[
            shift_z : shift_z + planes, shift_x : shift_x + width_x, shift_y : shift_y + width_y, :
        ]
        running = running + jnp.einsum(
            "zxyi,io->zxyo", window, weights[:, position, :], preferred_element_type=jnp.float32
        )
    return running


def grad_part(padded, grad_pre):
    planes = padded.shape[0] - 2
    width_x = padded.shape[1] - 2
    width_y = padded.shape[2] - 2
    term_list = []
    for position in range(27):
        shift_z, shift_x, shift_y = (position // 9, position // 3 % 3, position % 3)
        window = padded[
            shift_z : shift_z + planes, shift_x : shift_x + width_x, shift_y : shift_y + width_y, :
        ]
        term_list.append(
            jnp.einsum("zxyi,zxyo->io", window, grad_pre, preferred_element_type=jnp.float32)
        )
    return jnp.stack(term_list, 1)


def activate(pre_act, cotangent):
    activated = jax.nn.gelu(pre_act).astype(jnp.bfloat16)
    _, backward = jax.vjp(jax.nn.gelu, pre_act)
    grad_pre = backward(cotangent.astype(jnp.float32))[0].astype(jnp.bfloat16)
    return (activated, grad_pre)


def on_device(
    point_feats,
    send_slots,
    send_counts,
    neighbors,
    tile_fill,
    offsets,
    weight,
    conv_bias,
    cotangent,
):
    spaces = send_slots.shape[2]
    capacity = send_slots.shape[3]
    planes = cotangent.shape[0]
    rows_x = cotangent.shape[1]
    width_y = cotangent.shape[2]
    channels = cotangent.shape[3]
    slot_list = send_slots[0, 0]
    usable = jnp.arange(capacity, dtype=jnp.int32)[None, :] < send_counts[0, 0][:, None]
    outgoing = jnp.where(usable[..., None], point_feats[slot_list], jnp.zeros((), jnp.bfloat16))
    incoming = lax.all_to_all(outgoing, "space", split_axis=0, concat_axis=0, tiled=True)
    point_table = incoming.reshape(spaces * capacity, channels)
    picked = point_table[neighbors]
    kernel = kernel_weights(offsets, tile_fill)
    denominator = 1.0 + jnp.sum(kernel, axis=-1)
    kernel_half = kernel.astype(jnp.bfloat16)
    summed = jnp.einsum(
        "zabuvs,zabsk->zabuvk", kernel_half, picked, preferred_element_type=jnp.float32
    )
    tile_sums = (summed / denominator[..., None]).astype(jnp.bfloat16)
    latent = tile_sums.transpose(0, 1, 3, 2, 4, 5).reshape(planes, rows_x, width_y, channels)
    with_rims = padded_2(latent, (("space", 0), ("chan", 1)), 1)
    padded = jnp.pad(with_rims, ((0, 0), (0, 0), (1, 1), (0, 0)))
    bias_wide = conv_bias.astype(jnp.float32)
    full_weight = lax.all_gather(weight, "chan", axis=0, tiled=True)
    pre_act = conv_part(padded, full_weight) + bias_wide
    activated, grad_pre = activate(pre_act, cotangent)
    row_count = weight.shape[0]
    scaling = 1.0 / math.sqrt(
        planes * lax.axis_size("space") * rows_x * lax.axis_size("chan") * width_y
    )
    summed_all = lax.psum(grad_part(padded, grad_pre), ("space", "chan"))
    own_rows = lax.dynamic_slice_in_dim(
        summed_all, lax.axis_index("chan") * row_count, row_count, 0
    )
    return (activated, own_rows * scaling)


def solution(mesh):
    return jax.shard_map(
        on_device,
        mesh=mesh,
        in_specs=(
            P(("space", "chan"), None),
            P("space", "chan", None, None),
            P("space", "chan", None),
            P("space", "chan", None, None),
            P("space", "chan", None),
            P("space", "chan", None, None, None),
            P("chan", None, None),
            P(),
            P("space", "chan", None, None),
        ),
        out_specs=(P("space", "chan", None, None), P("chan", None, None)),
        check_vma=False,
    )
```

profile of v0, /device:TPU:1, one launch (start us, length us, event | category | flops | bytes accessed | tf_op | source)
XLA Modules:
  0.0 454.3 jit_solution(3659133097962273879)
XLA Ops:
  8.7 14.6 %gather_fusion = bf16[4096,256]{1,0:T(8,128)(2,1)S(1)} fusion(bf16[2048,256]{1,0:T(8,128)(2,1)S(1)} %copy-done, s32[4096]{0:T(1024)S(1)} %bitcast_clamp_fusion), kind=kCustom, calls=%fused_computation | custom fusion | bytes 4210688 | tf_op jit(solution)/shard_map/gather | solution.py:90
  23.4 1.7 broadcast_select_fusion
  25.1 6.1 %all-to-all-start = ((bf16[4,1024,256]{2,1,0:T(8,128)(2,1)}), bf16[4,1024,256]{2,1,0:T(8,128)(2,1)S(1)}, u32[]{:S(2)}, u32[]{:S(2)}) async-start(bf16[4,1024,256]{2,1,0:T(8,128)(2,1)} %broadcast_select_fusion), calls=%async_computation | async-start | bytes 4194304 | tf_op jit(solution)/shard_map/all_to_all | solution.py:91
  32.6 24.9 %all-to-all-done = bf16[4,1024,256]{2,1,0:T(8,128)(2,1)S(1)} async-done(((bf16[4,1024,256]{2,1,0:T(8,128)(2,1)}), bf16[4,1024,256]{2,1,0:T(8,128)(2,1)S(1)}, u32[]{:S(2)}, u32[]{:S(2)}) %all-to-all-start) | async-done | bytes 2097184 | tf_op jit(solution)/shard_map/all_to_all | solution.py:91
  57.5 65.2 %gather_fusion.1 = bf16[16384,256]{1,0:T(8,128)(2,1)} fusion(bf16[4096,256]{1,0:T(8,128)(2,1)S(1)} %bitcast.442, s32[16384]{0:T(1024)S(1)} %broadcast_clamp_fusion), kind=kCustom, calls=%fused_computation.1 | custom fusion | bytes 16842752 | tf_op jit(solution)/shard_map/gather | solution.py:93
  122.7 5.3 %fusion.16 = bf16[4,1,4,32,4,256]{5,4,2,3,0,1:T(4,128)(2,1)S(1)} fusion(bf16[4,32,128,256,1]{3,2,4,1,0:T(8,128)(2,1)} %bitcast.447, f32[4,32,4,4]{3,2,1,0:T(4,128)S(1)} %copy.130, f32[4,32,128]{2,1,0:T(8,128)S(1)} %get-tuple-element.43, f32[4,32,4,128]{3,2,1,0:T(4,128)S(1)} %copy.129, f32[4,32,4,128]{3,2,1,0:T(4,128)S(1)} %copy.128, ...), kind=kOutput, calls=%fused_computation.42 | convolution fusion | flops 136577024 | bytes 10051584 | tf_op jit(solution)/shard_map/zabuvs,zabsk->zabuvk/dot_general | solution.py:97
  128.3 2.7 collective-permute-start
  131.7 1.9 collective-permute-start.1
  134.7 6.5 %collective-permute-done.1 = bf16[1,4,128,256]{3,2,1,0:T(8,128)(2,1)S(1)} collective-permute-done((bf16[1,4,128,256]{3,2,1,0:T(8,128)(2,1)S(1)}, bf16[1,4,128,256]{3,2,1,0:T(8,128)(2,1)S(1)}, u32[]{:S(2)}, u32[]{:S(2)}) %collective-permute-start.1) | collective-permute-done | bytes 262176 | tf_op jit(solution)/shard_map/ppermute | solution.py:17
  141.4 1.3 collective-permute-start.3
  142.7 4.0 collective-permute-start.2
  147.3 2.6 collective-permute-done.3
  149.9 1.5 collective-permute-done.2
  151.4 2.8 fusion.46
  154.2 1.2 fusion.5
  155.4 9.0 %fusion.165 = (bf16[4,4,128,256]{3,2,1,0:T(8,128)(2,1)}, bf16[4,4,128,256]{3,2,1,0:T(8,128)(2,1)}, bf16[4,4,128,256]{3,2,1,0:T(8,128)(2,1)}, bf16[4,4,128,256]{3...) fusion(bf16[6,6,130,256]{3,2,1,0:T(8,128)(2,1)S(1)} %fusion.5), kind=kLoop, calls=%fused_computation.268 | loop fusion | bytes 37748736 | tf_op jit(solution)/shard_map/slice | solution.py:39
  164.4 3.0 fusion.79
  167.5 2.8 fusion.82
  170.3 1.7 fusion.83
  172.1 1.8 fusion.80
  173.9 1.7 fusion.84
  175.6 1.8 fusion.100
  177.4 1.7 fusion.101
  179.2 1.8 fusion.102
  181.0 1.8 fusion.103
  182.8 1.8 fusion.104
  184.6 1.7 fusion.105
  186.3 1.8 fusion.106
  188.1 1.7 fusion.108
  189.9 1.8 fusion.109
  191.7 1.7 fusion.110
  193.5 1.8 fusion.92
  195.2 1.8 fusion.93
  197.1 1.7 fusion.95
  198.8 1.8 fusion.96
  200.6 1.8 fusion.97
  202.4 1.8 fusion.98
  204.2 1.8 fusion.99
  206.0 1.8 fusion.81
  207.8 1.8 fusion.77
  209.5 1.8 fusion.94
  211.3 1.7 fusion.107
  213.1 19.9 %fusion.8 = (bf16[4,4,128,256]{3,2,1,0:T(8,128)(2,1)}, bf16[4,4,128,256]{3,2,1,0:T(8,128)(2,1)}) fusion(bf16[4,4,128,256]{3,2,1,0:T(8,128)(2,1)S(1)} %copy-done.14, f32[256]{0:T(256)} %convert_element_type.29, bf16[256,27,256]{2,0,1:T(8,128)(2,1)} %all-gather.2.cloned.1.call-done, bf16[6,6,130,256]{3,2,1,0:T(8,128)(2,1)S(1)} %fusion.5, ...), kind=kOutput, calls=%fused_computation.24 | convolution fusion | flops 294649856 | bytes 58852352 | tf_op jit(solution)/shard_map/zxyi,io->zxyo/dot_general | solution.py:42
  233.0 2.9 fusion.43
  239.6 1.2 fusion.39
  244.4 1.2 fusion.35
  267.5 178.3 %all-reduce.3.cloned.1.call-done = f32[256,27,256]{2,0,1:T(8,128)} async-done(((f32[256,27,256]{2,0,1:T(8,128)}), f32[256,27,256]{2,0,1:T(8,128)}) %all-reduce.3.cloned.1.call-update) | async-done | bytes 7077904 | tf_op jit(solution)/shard_map/psum | solution.py:112
  445.8 1.6 dynamic-slice_multiply_fusion
  (143 shorter events, 34.7 us)
Async XLA Ops:
  7.2 1.5 copy-start
  7.2 157.2 %all-gather.2.cloned.1.call-start = ((), (), s32[]{:S(2)}) async-start(), calls=%async_computation.1 | async-start | bytes 3649536 | tf_op jit(solution)/shard_map/all_gather | solution.py:105
  8.7 14.6 %copy-start.42 = (s32[1,1,4]{2,1,0:T(1,128)S(1)}, s32[1,1,4]{2,1,0:T(1,128)}, u32[]{:S(2)}) copy-start(s32[1,1,4]{2,1,0:T(1,128)} %param.11) | copy-start | bytes 52
  25.1 6.1 %copy-start.39 = (f32[4,1,32,3,128]{4,2,3,1,0:T(8,128)S(1)}, f32[4,1,32,3,128]{4,2,3,1,0:T(8,128)}, u32[]{:S(2)}) copy-start(f32[4,1,32,3,128]{4,2,3,1,0:T(8,128)} %param.14) | copy-start | bytes 589828
  25.1 32.4 %all-to-all-start = ((bf16[4,1024,256]{2,1,0:T(8,128)(2,1)}), bf16[4,1024,256]{2,1,0:T(8,128)(2,1)S(1)}, u32[]{:S(2)}, u32[]{:S(2)}) async-start(bf16[4,1024,256]{2,1,0:T(8,128)(2,1)} %broadcast_select_fusion), calls=%async_computation | async-start | bytes 4194304 | tf_op jit(solution)/shard_map/all_to_all | solution.py:91
  31.2 1.4 copy-start.40
  31.2 414.6 %all-reduce.3.cloned.1.call-start = ((), (), s32[]{:S(2)}) async-start(), calls=%async_computation.2 | async-start | bytes 14155776 | tf_op jit(solution)/shard_map/psum | solution.py:112
  128.3 6.0 %collective-permute-start = (bf16[1,4,128,256]{3,2,1,0:T(8,128)(2,1)S(1)}, bf16[1,4,128,256]{3,2,1,0:T(8,128)(2,1)S(1)}, u32[]{:S(2)}, u32[]{:S(2)}) collective-permute-start(bf16[1,4,128,256]{3,2,1,0:T(8,128)(2,1)S(1)} %copy.132), channel_id=1, source_target_pairs={{0,32},{32,64},{64,96},{1,33},{33,65},{65,97},{2,34},{34,66},{66,9... | collective-permute-start | bytes 786440 | tf_op jit(solution)/shard_map/ppermute | solution.py:14
  131.5 3.2 copy-start.4
  131.7 9.6 %collective-permute-start.1 = (bf16[1,4,128,256]{3,2,1,0:T(8,128)(2,1)S(1)}, bf16[1,4,128,256]{3,2,1,0:T(8,128)(2,1)S(1)}, u32[]{:S(2)}, u32[]{:S(2)}) collective-permute-start(bf16[1,4,128,256]{3,2,1,0:T(8,128)(2,1)S(1)} %copy.135), channel_id=1, source_target_pairs={{32,0},{64,32},{96,64},{33,1},{65,33},{97,65},{34,2},{66,34},{98,6... | collective-permute-start | bytes 786440 | tf_op jit(solution)/shard_map/ppermute | solution.py:17
  134.7 15.2 %copy-start.11 = (bf16[5,4,128,256]{3,2,1,0:T(8,128)(2,1)}, bf16[5,4,128,256]{3,2,1,0:T(8,128)(2,1)S(1)}, u32[]{:S(2)}) copy-start(bf16[5,4,128,256]{3,2,1,0:T(8,128)(2,1)S(1)} %get-tuple-element.33) | copy-start | bytes 3932164
  134.7 12.0 %copy-start.43 = (bf16[256]{0:T(256)(128)(2,1)S(1)}, bf16[256]{0:T(256)(128)(2,1)}, u32[]{:S(2)}) copy-start(bf16[256]{0:T(256)(128)(2,1)} %param.16) | copy-start | bytes 1540
  141.3 8.6 %copy-start.7 = (bf16[5,4,128,256]{3,2,1,0:T(8,128)(2,1)}, bf16[5,4,128,256]{3,2,1,0:T(8,128)(2,1)S(1)}, u32[]{:S(2)}) copy-start(bf16[5,4,128,256]{3,2,1,0:T(8,128)(2,1)S(1)} %get-tuple-element.40) | copy-start | bytes 3932164
  141.3 12.9 %copy-start.2 = (bf16[6,4,128,256]{3,2,1,0:T(8,128)(2,1)}, bf16[6,4,128,256]{3,2,1,0:T(8,128)(2,1)S(1)}, u32[]{:S(2)}) copy-start(bf16[6,4,128,256]{3,2,1,0:T(8,128)(2,1)S(1)} %get-tuple-element.41) | copy-start | bytes 4718596
  141.4 8.5 %collective-permute-start.3 = (bf16[6,1,128,256]{3,2,1,0:T(8,128)(2,1)S(1)}, bf16[6,1,128,256]{3,2,1,0:T(8,128)(2,1)S(1)}, u32[]{:S(2)}, u32[]{:S(2)}) collective-permute-start(bf16[6,1,128,256]{3,2,1,0:T(8,128)(2,1)S(1)} %get-tuple-element.32), channel_id=1, source_target_pairs={{1,0},{2,1},{3,2},{4,3},{5,4},{6,5},{7,6},{8,7},{9,8},{10,9},{11,1... | collective-permute-start | bytes 1179656 | tf_op jit(solution)/shard_map/ppermute | solution.py:17
  142.7 8.7 %collective-permute-start.2 = (bf16[6,1,128,256]{3,2,1,0:T(8,128)(2,1)S(1)}, bf16[6,1,128,256]{3,2,1,0:T(8,128)(2,1)S(1)}, u32[]{:S(2)}, u32[]{:S(2)}) collective-permute-start(bf16[6,1,128,256]{3,2,1,0:T(8,128)(2,1)S(1)} %get-tuple-element.31), channel_id=1, source_target_pairs={{0,1},{1,2},{2,3},{3,4},{4,5},{5,6},{6,7},{7,8},{8,9},{9,10},{10,1... | collective-permute-start | bytes 1179656 | tf_op jit(solution)/shard_map/ppermute | solution.py:14
  164.4 3.1 copy-start.3
  167.5 2.8 copy-start.10
  206.0 1.8 copy-start.5
  207.8 1.8 copy-start.8
  209.5 1.8 copy-start.12
  211.3 1.8 copy-start.14
  233.0 2.9 copy-start.15
  233.0 2.9 copy-start.36
  235.8 1.2 copy-start.38
  237.0 1.2 copy-start.37
  238.2 1.3 copy-start.13
  239.6 1.2 copy-start.35
  240.8 1.2 copy-start.34
  242.0 1.2 copy-start.29
  243.2 1.2 copy-start.33
  244.4 1.2 copy-start.32
  245.6 1.2 copy-start.26
  246.8 1.2 copy-start.31
  248.0 1.2 copy-start.30
  249.2 1.2 copy-start.6
  250.5 1.2 copy-start.28
  251.6 1.2 copy-start.27
  252.9 1.2 copy-start.21
  254.1 1.2 copy-start.25
  255.3 1.2 copy-start.24
  256.5 1.2 copy-start.18
  257.7 1.2 copy-start.23
  258.9 1.2 copy-start.22
  260.1 1.3 copy-start.9
  262.6 1.2 copy-start.19
  265.0 1.2 copy-start.17
  267.4 180.0 %copy-start.1 = (bf16[2048,256]{1,0:T(8,128)(2,1)S(1)}, bf16[2048,256]{1,0:T(8,128)(2,1)}, u32[]{:S(2)}) copy-start(bf16[2048,256]{1,0:T(8,128)(2,1)} %param.9) | copy-start | bytes 3145732
  (3 other events, 3.1 us)
Sparse Core Ops, SparseCore 0:
  9.6 119.8 all-gather.1
  267.6 178.1 all-reduce.2
where the time goes:
time: 455 us; the launch traced here: 454 us
  waiting for transfers between devices  215 us (47%)
  matrix products  107 us (24%)
  local copies, waits for them, and re-layouts  91.7 us (20%)
  starting transfers between devices  16.1 us (4%)
  between operations  14.4 us (3%)
  other arithmetic  9.33 us (2%)
    psum x1, waiting for transfers between devices, on_device(): summed_all = lax.psum(grad_part(padded, grad_pre), ('space', 'chan'))  178 us
    dot_general x27, matrix products, conv_part(): jnp.einsum('zxyi,io->zxyo', window, weights[:, position, :], preferred_el...  68.5 us
    gather x1, local copies, waits for them, and re-layouts, on_device(): picked = point_table[neighbors]  65.2 us
    dot_general x27, matrix products, grad_part(): jnp.einsum('zxyi,zxyo->io', window, grad_pre, preferred_element_type=jnp....  33.6 us
    all_to_all x1, waiting for transfers between devices, on_device(): lax.all_to_all(outgoing, 'space', split_axis=0, concat_axis=0, tiled=True)  24.9 us
    gather x1, local copies, waits for them, and re-layouts, on_device(): point_feats[slot_list]  14.6 us
    ppermute x2, waiting for transfers between devices, padded_2(): lax.ppermute(lax.slice_in_dim(block, 0, width, axis=dim), axis, backward)  9.14 us
  transfers between devices with their start and end apart: 7, of which 6 were waited for; matrix products, arithmetic and copies ran while one was open for 23% of the time, Pallas kernels for 0%

commit v1 on v0

v1 whole, which is shorter than its diff:
```python
import math

import jax
import jax.numpy as jnp
from jax import lax
from jax.experimental import pallas as pl
from jax.experimental.pallas import tpu as pltpu
from jax.sharding import PartitionSpec as P

BF = jnp.bfloat16
F32 = jnp.float32


def send_kernel(slots_ref, counts_ref, feats_ref, out_ref):
    owner = pl.program_id(0)
    points = feats_ref.shape[0]
    slots = slots_ref[0]
    position = lax.broadcasted_iota(jnp.int32, slots.shape, 0) * 128 + lax.broadcasted_iota(
        jnp.int32, slots.shape, 1
    )
    slots = jnp.where(position < counts_ref[owner], slots, -1)
    columns = slots.T
    point_ids = lax.broadcasted_iota(jnp.int32, (128, points), 1)
    for half in range(2):
        hot = [
            jnp.where(point_ids == columns[:, r : r + 1], 1.0, 0.0).astype(BF)
            for r in range(half * 4, half * 4 + 4)
        ]
        rows = jnp.dot(
            jnp.concatenate(hot, axis=0), feats_ref[...], preferred_element_type=F32
        )
        out_ref[0, half * 512 : half * 512 + 512, :] = rows.astype(BF)


def gather_listed(feats, slots, counts):
    owners, capacity = slots.shape
    points, channels = feats.shape
    return pl.pallas_call(
        send_kernel,
        grid=(owners,),
        in_specs=[
            pl.BlockSpec((1, capacity // 128, 128), lambda t: (t, 0, 0)),
            pl.BlockSpec(memory_space=pltpu.SMEM),
            pl.BlockSpec((points, channels), lambda t: (0, 0)),
        ],
        out_specs=pl.BlockSpec((1, capacity, channels), lambda t: (t, 0, 0)),
        out_shape=jax.ShapeDtypeStruct((owners, capacity, channels), BF),
        compiler_params=pltpu.CompilerParams(vmem_limit_bytes=40 << 20),
    )(slots.reshape(owners, capacity // 128, 128), counts, feats)


def latent_kernel(fill_ref, near_ref, place_ref, table_ref, out_ref, spread, total, order, denom):
    plane = pl.program_id(0)
    tiles = near_ref.shape[1]
    slots = near_ref.shape[2]
    rows = table_ref.shape[0]
    channels = table_ref.shape[1]
    groups = rows // 256
    cell = lax.broadcasted_iota(jnp.int32, (16, slots), 0)
    centre_x = (cell // 4).astype(F32) - 1.5
    centre_y = (cell % 4).astype(F32) - 1.5
    lane = lax.broadcasted_iota(jnp.int32, (16, slots), 1)
    low_ids = lax.broadcasted_iota(jnp.int32, (256, slots), 0)

    def one_tile(tile, carry):
        near = near_ref[0, pl.ds(tile, 1), :]
        along_x = place_ref[0, 0, pl.ds(tile, 1), :] - centre_x
        along_y = place_ref[0, 1, pl.ds(tile, 1), :] - centre_y
        along_z = place_ref[0, 2, pl.ds(tile, 1), :]
        values = jnp.exp(-0.5 * (along_x * along_x + along_y * along_y + along_z * along_z))
        values = jnp.where(lane < fill_ref[plane, tile], values, 0.0)
        start = pl.multiple_of(tile * 16, 16)
        denom[pl.ds(start, 16), :] = 1.0 + jnp.sum(values, axis=1, keepdims=True)
        half = values.astype(BF).astype(F32)
        high = jnp.broadcast_to(near >> 8, (16, slots))
        low = near & 255
        stacked = jnp.concatenate(
            [jnp.where(high == g, half, 0.0).astype(BF) for g in range(groups)], axis=0
        )
        hot = jnp.where(low_ids == low, 1.0, 0.0).astype(BF)
        block = lax.dot_general(
            stacked, hot, (((1,), (1,)), ((), ())), preferred_element_type=F32
        ).astype(BF)
        for g in range(groups):
            spread[pl.ds(start, 16), g * 256 : g * 256 + 256] = block[g * 16 : g * 16 + 16, :]
        return carry

    lax.fori_loop(0, tiles, one_tile, 0, unroll=4)
    summed = jnp.dot(spread[...], table_ref[...], preferred_element_type=F32)
    summed = summed / denom[...]
    for lanes in range(0, channels, 128):
        total[...] = summed[:, lanes : lanes + 128]
        for u in range(4):
            for v in range(4):
                order[pl.ds(v, tiles, stride=4), :] = total[
                    pl.ds(u * 4 + v, tiles, stride=16), :
                ]
            out_ref[0, u, :, lanes : lanes + 128] = order[...].astype(BF)


def latent_block(table, near, fill, place):
    planes, tiles, slots = near.shape
    rows, channels = table.shape
    return pl.pallas_call(
        latent_kernel,
        grid=(planes,),
        in_specs=[
            pl.BlockSpec(memory_space=pltpu.SMEM),
            pl.BlockSpec((1, tiles, slots), lambda z: (z, 0, 0)),
            pl.BlockSpec((1, 3, tiles, slots), lambda z: (z, 0, 0, 0)),
            pl.BlockSpec((rows, channels), lambda z: (0, 0)),
        ],
        out_specs=pl.BlockSpec((1, 4, tiles * 4, channels), lambda z: (z, 0, 0, 0)),
        out_shape=jax.ShapeDtypeStruct((planes, 4, tiles * 4, channels), BF),
        scratch_shapes=[
            pltpu.VMEM((tiles * 16, rows), BF),
            pltpu.VMEM((tiles * 16, 128), F32),
            pltpu.VMEM((tiles * 4, 128), F32),
            pltpu.VMEM((tiles * 16, 1), F32),
        ],
        compiler_params=pltpu.CompilerParams(vmem_limit_bytes=40 << 20),
    )(fill, near, place, table)


def conv_kernel(
    latent_ref, below_ref, above_ref, left_ref, right_ref, left_rim_ref, right_rim_ref,
    weight_ref, bias_ref, cotangent_ref, act_ref, grad_ref, padded, turned, taps, shifted,
):
    planes, rows_x, width, channels = latent_ref.shape
    flat = rows_x * width
    padded[1 : planes + 1, 1 : rows_x + 1] = latent_ref[...]
    padded[0:1, 1 : rows_x + 1] = below_ref[...]
    padded[planes + 1 : planes + 2, 1 : rows_x + 1] = above_ref[...]
    padded[1 : planes + 1, 0:1] = left_ref[...]
    padded[1 : planes + 1, rows_x + 1 : rows_x + 2] = right_ref[...]
    for rim in range(2):
        z = rim * (planes + 1)
        padded[z : z + 1, 0:1] = left_rim_ref[rim : rim + 1]
        padded[z : z + 1, rows_x + 1 : rows_x + 2] = right_rim_ref[rim : rim + 1]
    y_ids = lax.broadcasted_iota(jnp.int32, (width, channels), 0)
    root = math.sqrt(2.0 / math.pi)

    def turn(z, carry):
        block = padded[z].reshape((rows_x + 2) * width, channels)
        turned[z] = block.T
        return carry

    lax.fori_loop(0, planes + 2, turn, 0)

    def conv_plane(z, carry):
        pieces = [
            padded[z + dz, dx : dx + rows_x].reshape(flat, channels)
            for dz in range(3)
            for dx in range(3)
        ]
        taps[...] = jnp.dot(
            jnp.concatenate(pieces, axis=1), weight_ref[...], preferred_element_type=F32
        )
        for x in range(rows_x):
            rows = slice(x * width, (x + 1) * width)
            low = jnp.where(y_ids == 0, 0.0, pltpu.roll(taps[rows, 0:channels], 1, 0))
            high = jnp.where(
                y_ids == width - 1, 0.0, pltpu.roll(taps[rows, 2 * channels :], width - 1, 0)
            )
            pre = low + taps[rows, channels : 2 * channels] + high + bias_ref[...]
            square = pre * pre
            inner = root * (pre + 0.044715 * (square * pre))
            bent = jnp.tanh(inner)
            gate = 0.5 * (1.0 + bent)
            act_ref[z, x] = (pre * gate).astype(BF)
            slope = gate + 0.5 * pre * (1.0 - bent * bent) * (
                root * (1.0 + 3.0 * 0.044715 * square)
            )
            grad = (cotangent_ref[z, x].astype(F32) * slope).astype(BF).astype(F32)
            start = pl.multiple_of(z * flat + x * width, width)
            shifted[pl.ds(start, width), 0:channels] = jnp.where(
                y_ids == width - 1, 0.0, pltpu.roll(grad, width - 1, 0)
            ).astype(BF)
            shifted[pl.ds(start, width), channels : 2 * channels] = grad.astype(BF)
            shifted[pl.ds(start, width), 2 * channels :] = jnp.where(
                y_ids == 0, 0.0, pltpu.roll(grad, 1, 0)
            ).astype(BF)
        return carry

    lax.fori_loop(0, planes, conv_plane, 0)

    def grad_taps(tap, carry):
        dz = tap // 3
        start = pl.multiple_of((tap % 3) * width, width)
        pieces = [turned[z + dz, :, pl.ds(start, flat)] for z in range(planes)]
        sums = jnp.dot(
            jnp.concatenate(pieces, axis=1), shifted[...], preferred_element_type=F32
        )
        for dy in range(3):
            part = sums[:, dy * channels : (dy + 1) * channels]
            both = jnp.concatenate(
                [
                    part[:, :128].reshape(channels // 8, 8, 128),
                    part[:, 128:].reshape(channels // 8, 8, 128),
                ],
                axis=1,
            )
            grad_ref[:, tap * 3 + dy] = both.astype(BF)
        return carry

    lax.fori_loop(0, 9, grad_taps, 0)


def conv_block(
    latent, below, above, left, right, left_rim, right_rim, weight, bias, cotangent
):
    planes, rows_x, width, channels = latent.shape
    flat = rows_x * width
    whole = pl.BlockSpec(memory_space=pltpu.VMEM)
    return pl.pallas_call(
        conv_kernel,
        in_specs=[whole] * 10,
        out_specs=[whole] * 2,
        out_shape=[
            jax.ShapeDtypeStruct(latent.shape, BF),
            jax.ShapeDtypeStruct((channels // 8, 27, 16, 128), BF),
        ],
        scratch_shapes=[
            pltpu.VMEM((planes + 2, rows_x + 2, width, channels), BF),
            pltpu.VMEM((planes + 2, channels, (rows_x + 2) * width), BF),
            pltpu.VMEM((flat, 3 * channels), F32),
            pltpu.VMEM((planes * flat, 3 * channels), BF),
        ],
        compiler_params=pltpu.CompilerParams(vmem_limit_bytes=52 << 20),
    )(latent, below, above, left, right, left_rim, right_rim, weight, bias, cotangent)


def in_order(core, own, other):
    low = jnp.where(core == 0, own, other)
    high = jnp.where(core == 0, other, own)
    return low, high


def on_device(
    point_feats,
    send_slots,
    send_counts,
    neighbors,
    tile_fill,
    offsets,
    weight,
    conv_bias,
    cotangent,
):
    spaces = lax.axis_size("space")
    chans = lax.axis_size("chan")
    planes, rows_x, width_y, channels = cotangent.shape
    row_count = weight.shape[0]
    space = lax.axis_index("space")
    core = space % 2
    swap = [(i, i ^ 1) for i in range(spaces)]
    far = [(i, i ^ 2) for i in range(spaces)]
    cross = [(i, i ^ 3) for i in range(spaces)]
    up_space = [(i, i + 1) for i in range(spaces - 1)]
    down_space = [(i + 1, i) for i in range(spaces - 1)]
    up_chan = [(i, i + 1) for i in range(chans - 1)]
    down_chan = [(i + 1, i) for i in range(chans - 1)]

    by_tap = weight.transpose(1, 0, 2)
    half_taps = lax.dynamic_slice_in_dim(by_tap, core * 13, 14, 0)
    spread = jnp.broadcast_to(half_taps[None], (chans,) + half_taps.shape)
    gathered = lax.all_to_all(spread, "chan", split_axis=0, concat_axis=0, tiled=True)
    gathered_other = lax.ppermute(gathered, "space", swap)
    low, high = in_order(core, gathered, gathered_other)
    full_weight = jnp.concatenate([low, high[:, 1:]], axis=1)
    full_weight = full_weight.reshape(chans, 9, 3, row_count, channels)
    full_weight = full_weight.transpose(1, 0, 3, 2, 4).reshape(9 * channels, 3 * channels)

    outgoing = gather_listed(point_feats, send_slots[0, 0], send_counts[0, 0])
    incoming = lax.all_to_all(outgoing, "space", split_axis=0, concat_axis=0, tiled=True)
    table = incoming.reshape(-1, channels)
    latent = latent_block(
        table, neighbors[:, 0], tile_fill[:, 0], offsets[:, 0].transpose(0, 2, 1, 3)
    )

    below = lax.ppermute(latent[planes - 1 :], "space", up_space)
    above = lax.ppermute(latent[:1], "space", down_space)
    left = lax.ppermute(latent[:, rows_x - 1 :], "chan", up_chan)
    right = lax.ppermute(latent[:, :1], "chan", down_chan)
    rims = jnp.concatenate([below, above], axis=0)
    left_rim = lax.ppermute(rims[:, rows_x - 1 :], "chan", up_chan)
    right_rim = lax.ppermute(rims[:, :1], "chan", down_chan)
    activated, terms = conv_block(
        latent, below, above, left, right, left_rim, right_rim,
        full_weight, conv_bias.astype(F32)[None], cotangent,
    )

    mine = lax.dynamic_slice_in_dim(terms, core * 13, 14, 1)
    theirs = lax.dynamic_slice_in_dim(terms, (1 - core) * 13, 14, 1)
    paired = (mine.astype(F32) + lax.ppermute(theirs, "space", swap).astype(F32)).astype(BF)
    collected = lax.all_to_all(paired, "chan", split_axis=0, concat_axis=0, tiled=True)
    summed = jnp.sum(collected.astype(F32), axis=0)
    own_sum = summed + lax.ppermute(summed, "space", far)
    other_sum = lax.ppermute(summed, "space", swap) + lax.ppermute(summed, "space", cross)
    low_sum, high_sum = in_order(core, own_sum, other_sum)
    total = jnp.concatenate([low_sum, high_sum[1:]], axis=0)
    total = total.reshape(27, 2, row_count, channels // 2).transpose(2, 0, 1, 3)
    scaling = 1.0 / math.sqrt(planes * spaces * rows_x * chans * width_y)
    return (activated, total.reshape(row_count, 27, channels) * scaling)


def solution(mesh):
    return jax.shard_map(
        on_device,
        mesh=mesh,
        in_specs=(
            P(("space", "chan"), None),
            P("space", "chan", None, None),
            P("space", "chan", None),
            P("space", "chan", None, None),
            P("space", "chan", None),
            P("space", "chan", None, None, None),
            P("chan", None, None),
            P(),
            P("space", "chan", None, None),
        ),
        out_specs=(P("space", "chan", None, None), P("chan", None, None)),
        check_vma=False,
    )
```

time: 455 us -> 189 us (0.42)
  waiting for transfers between devices: 215 us -> 54.6 us
  matrix products: 107 us -> 0 us
  local copies, waits for them, and re-layouts: 91.7 us -> 8.33 us
  Pallas kernels: 0 us -> 47.9 us
  blocking collectives: 0 us -> 35.2 us
  starting transfers between devices: 16.1 us -> 36.6 us
  between operations: 14.4 us -> 0.94 us
    psum x1 -> x0, waiting for transfers between devices: 178 us -> none  [on_device(): summed_all = lax.psum(grad_part(padded, grad_pre), ('space', 'chan'))]
    dot_general x55 -> x0, matrix products: 107 us -> none  [the longest x27 68.5 us: conv_part(): jnp.einsum('zxyi,io->zxyo', window, weights[:, position, :], preferred_el...]
    gather x2 -> x0, local copies, waits for them, and re-layouts: 79.8 us -> none  [the longest x1 65.2 us: on_device(): picked = point_table[neighbors]]
    pallas_call x0 -> x3, Pallas kernels: none -> 47.9 us  [the longest x1 24.2 us: conv_block(): pl.pallas_call(conv_kernel, in_specs=[whole] * 10, out_specs=[whole] * 2,...]
    all_to_all x0 -> x1, blocking collectives: none -> 35.2 us  [on_device(): lax.all_to_all(paired, 'chan', split_axis=0, concat_axis=0, tiled=True)]
    all_to_all x0 -> x1, waiting for transfers between devices: none -> 17.1 us  [on_device(): lax.all_to_all(spread, 'chan', split_axis=0, concat_axis=0, tiled=True)]
    ppermute x4 -> x11, starting transfers between devices: 9.95 us -> 20.2 us  [the longest x1 4.56 us: on_device(): lax.ppermute(summed, 'space', cross)]
    all_to_all x0 -> x1, starting transfers between devices: none -> 9.86 us  [on_device(): lax.all_to_all(spread, 'chan', split_axis=0, concat_axis=0, tiled=True)]
  transfers between devices with their start and end apart: 7 -> 13, of which waited for: 6 -> 6; matrix products, arithmetic and copies ran while one was open for 23% -> 3% of each run, Pallas kernels for 0% -> 13%
where the time goes in v1:
time: 189 us
  waiting for transfers between devices  54.6 us (29%)
  Pallas kernels  47.9 us (25%)
  starting transfers between devices  36.6 us (19%)
  blocking collectives  35.2 us (19%)
  local copies, waits for them, and re-layouts  8.33 us (4%)
  other arithmetic  5.12 us (3%)
    all_to_all x1, blocking collectives, on_device(): lax.all_to_all(paired, 'chan', split_axis=0, concat_axis=0, tiled=True)  35.2 us
    all_to_all x1, waiting for transfers between devices, on_device(): lax.all_to_all(outgoing, 'space', split_axis=0, concat_axis=0, tiled=True)  26.3 us
    pallas_call x1, Pallas kernels, conv_block(): pl.pallas_call(conv_kernel, in_specs=[whole] * 10, out_specs=[whole] * 2,...  24.2 us
    all_to_all x1, waiting for transfers between devices, on_device(): lax.all_to_all(spread, 'chan', split_axis=0, concat_axis=0, tiled=True)  17.1 us
    pallas_call x1, Pallas kernels, latent_block(): pl.pallas_call(latent_kernel, grid=(planes,), in_specs=[pl.BlockSpec(memo...  16.6 us
    all_to_all x1, starting transfers between devices, on_device(): lax.all_to_all(spread, 'chan', split_axis=0, concat_axis=0, tiled=True)  9.86 us
    pallas_call x1, Pallas kernels, gather_listed(): pl.pallas_call(send_kernel, grid=(owners,), in_specs=[pl.BlockSpec((1, ca...  7.16 us
    all_to_all x1, starting transfers between devices, on_device(): lax.all_to_all(outgoing, 'space', split_axis=0, concat_axis=0, tiled=True)  6.49 us
  transfers between devices with their start and end apart: 13, of which 6 were waited for; matrix products, arithmetic and copies ran while one was open for 3% of the time, Pallas kernels for 13%

profile of v1, /device:TPU:1, one launch (start us, length us, event | category | flops | bytes accessed | tf_op | source)
XLA Modules:
  0.0 188.6 jit_solution(5619330199919642076)
XLA Ops:
  0.6 0.0 copy-start
  0.7 0.9 copy-done
  1.5 1.3 broadcast_in_dim.11
  2.9 9.9 %all-to-all-start.1 = ((bf16[32,14,8,256]{3,2,1,0:T(8,128)(2,1)}), bf16[32,14,8,256]{3,2,1,0:T(8,128)(2,1)S(1)}, u32[]{:S(2)}, u32[]{:S(2)}) async-start(bf16[32,14,8,256]{3,2,1,0:T(8,128)(2,1)} %broadcast_in_dim.11), calls=%async_computation.1 | async-start | bytes 3670016 | tf_op jit(solution)/shard_map/all_to_all | solution.py:267
  12.8 0.0 copy-done.10
  12.8 0.0 copy-done.2
  12.8 0.0 copy-done.6
  12.8 7.2 %shard_map.104 = bf16[4,1024,256]{2,1,0:T(8,128)(2,1)} custom-call(s32[4,8,128]{2,1,0:T(8,128)S(1)} %bitcast.27, s32[4]{0:T(128)S(1)} %bitcast.31, bf16[2048,256]{1,0:T(8,128)(2,1)S(1)} %copy-done.2), custom_call_target="tpu_custom_call" | custom-call | tf_op jit(solution)/shard_map/pallas_call | solution.py:38
  20.0 17.1 %all-to-all-done.1 = bf16[32,14,8,256]{3,2,1,0:T(8,128)(2,1)S(1)} async-done(((bf16[32,14,8,256]{3,2,1,0:T(8,128)(2,1)}), bf16[32,14,8,256]{3,2,1,0:T(8,128)(2,1)S(1)}, u32[]{:S(2)}, u32[]{:S(2)}) %all-to-all-start.1) | async-done | bytes 1835040 | tf_op jit(solution)/shard_map/all_to_all | solution.py:267
  37.1 1.2 copy-done.7
  38.3 6.5 %all-to-all-start = ((bf16[4,1024,256]{2,1,0:T(8,128)(2,1)}), bf16[4,1024,256]{2,1,0:T(8,128)(2,1)S(1)}, u32[]{:S(2)}, u32[]{:S(2)}) async-start(bf16[4,1024,256]{2,1,0:T(8,128)(2,1)} %shard_map.104), calls=%async_computation | async-start | bytes 4194304 | tf_op jit(solution)/shard_map/all_to_all | solution.py:275
  44.8 0.0 collective-permute-start.6
  44.8 26.3 %all-to-all-done = bf16[4,1024,256]{2,1,0:T(8,128)(2,1)S(1)} async-done(((bf16[4,1024,256]{2,1,0:T(8,128)(2,1)}), bf16[4,1024,256]{2,1,0:T(8,128)(2,1)S(1)}, u32[]{:S(2)}, u32[]{:S(2)}) %all-to-all-start) | async-done | bytes 2097184 | tf_op jit(solution)/shard_map/all_to_all | solution.py:275
  71.1 0.0 copy-done.4
  71.1 0.0 copy-start.11
  71.1 16.6 %shard_map.105.latent_ref = bf16[4,4,128,256]{3,2,1,0:T(8,128)(2,1)S(1)} custom-call(s32[4,32]{1,0:T(4,128)S(1)} %bitcast.29, s32[4,32,128]{2,1,0:T(8,128)S(1)} %bitcast.28, f32[4,3,32,128]{3,2,1,0:T(8,128)S(1)} %bitcast.26, bf16[4096,256]{1,0:T(8,128)(2,1)S(1)} %bitcast.25), custom_call_target="tpu_custom_call" | custom-call | tf_op jit(solution)/shard_map/pallas_call | solution.py:104
  87.7 0.7 fusion.2
  88.5 2.9 %collective-permute-start = (bf16[1,4,128,256]{3,2,1,0:T(8,128)(2,1)}, bf16[1,4,128,256]{3,2,1,0:T(8,128)(2,1)S(1)}, u32[]{:S(2)}, u32[]{:S(2)}) collective-permute-start(bf16[1,4,128,256]{3,2,1,0:T(8,128)(2,1)} %get-tuple-element.12), channel_id=1, source_target_pairs={{0,32},{32,64},{64,96},{1,33},{33,65},{65,97},{2,34},{34,66},{66,9... | collective-permute-start | bytes 786440 | tf_op jit(solution)/shard_map/ppermute | solution.py:281
  91.4 1.9 %collective-permute-start.1 = (bf16[1,4,128,256]{3,2,1,0:T(8,128)(2,1)S(1)}, bf16[1,4,128,256]{3,2,1,0:T(8,128)(2,1)S(1)}, u32[]{:S(2)}, u32[]{:S(2)}) collective-permute-start(bf16[1,4,128,256]{3,2,1,0:T(8,128)(2,1)S(1)} %get-tuple-element.11), channel_id=1, source_target_pairs={{32,0},{64,32},{96,64},{33,1},{65,33},{97,65},{34,2},{66,34},{98,6... | collective-permute-start | bytes 786440 | tf_op jit(solution)/shard_map/ppermute | solution.py:282
  93.3 1.3 collective-permute-start.3
  94.6 4.0 %collective-permute-start.2 = (bf16[4,1,128,256]{3,2,1,0:T(8,128)(2,1)S(1)}, bf16[4,1,128,256]{3,2,1,0:T(8,128)(2,1)S(1)}, u32[]{:S(2)}, u32[]{:S(2)}) collective-permute-start(bf16[4,1,128,256]{3,2,1,0:T(8,128)(2,1)S(1)} %get-tuple-element.10), channel_id=1, source_target_pairs={{0,1},{1,2},{2,3},{3,4},{4,5},{5,6},{6,7},{7,8},{8,9},{9,10},{10,1... | collective-permute-start | bytes 786440 | tf_op jit(solution)/shard_map/ppermute | solution.py:283
  98.6 0.0 collective-permute-done.below_ref
  98.7 1.9 collective-permute-done.1.above_ref
  100.6 1.3 collective-permute-start.5
  101.9 4.0 %collective-permute-start.4 = (bf16[2,1,128,256]{3,2,1,0:T(8,128)(2,1)S(1)}, bf16[2,1,128,256]{3,2,1,0:T(8,128)(2,1)S(1)}, u32[]{:S(2)}, u32[]{:S(2)}) collective-permute-start(bf16[2,1,128,256]{3,2,1,0:T(8,128)(2,1)S(1)} %get-tuple-element.14), channel_id=1, source_target_pairs={{0,1},{1,2},{2,3},{3,4},{4,5},{5,6},{6,7},{7,8},{8,9},{9,10},{10,1... | collective-permute-start | bytes 393224 | tf_op jit(solution)/shard_map/ppermute | solution.py:286
  105.9 0.0 collective-permute-done.6
  105.9 1.7 broadcast_select_fusion
  107.6 1.6 slice_select_fusion
  109.3 0.3 pad_maximum_fusion
  109.6 2.0 %copy.11 = bf16[9,32,8,3,256]{4,2,3,1,0:T(8,128)(2,1)} copy(bf16[9,32,8,3,256]{4,2,3,0,1:T(8,128)(2,1)S(1)} %bitcast.32) | data formatting | bytes 7077888 | tf_op jit(solution)/shard_map/transpose | solution.py:272
  111.6 0.0 collective-permute-done.3.right_ref
  111.6 0.0 collective-permute-done.2.left_ref
  111.6 0.0 collective-permute-done.5.right_rim_ref
  111.6 0.0 collective-permute-done.4.left_rim_ref
  111.6 24.2 %shard_map.106 = (bf16[4,4,128,256]{3,2,1,0:T(8,128)(2,1)}, bf16[32,27,16,128]{3,2,1,0:T(8,128)(2,1)}) custom-call(bf16[4,4,128,256]{3,2,1,0:T(8,128)(2,1)} %copy-done.1, bf16[1,4,128,256]{3,2,1,0:T(8,128)(2,1)S(1)} %collective-permute-done.below_ref, bf16[1,4,128,256]{3,2,1,0:T(8,128)(2,1)S(1)} %collective-permute-done.1.above_ref, ...), custom_call_target="tpu_custom_call" | custom-call | tf_op jit(solution)/shard_map/pallas_call | solution.py:215
  135.8 2.0 %constant_dynamic-slice_fusion = bf16[32,14,16,128]{3,2,1,0:T(8,128)(2,1)S(1)} fusion(bf16[32,27,16,128]{3,2,1,0:T(8,128)(2,1)} %get-tuple-element.5, s32[]{:T(128)S(6)} %select_n.44), kind=kLoop, calls=%fused_computation.13 | loop fusion | bytes 3670020 | tf_op jit(solution)/shard_map/dynamic_slice | solution.py:294
  137.8 0.1 collective-permute-start.7
  137.9 3.8 %collective-permute-done.7 = bf16[32,14,16,128]{3,2,1,0:T(8,128)(2,1)S(1)} collective-permute-done((bf16[32,14,16,128]{3,2,1,0:T(8,128)(2,1)S(1)}, bf16[32,14,16,128]{3,2,1,0:T(8,128)(2,1)S(1)}, u32[]{:S(2)}, u32[]{:S(2)}) %collective-permute-start.7) | collective-permute-done | bytes 1835040 | tf_op jit(solution)/shard_map/ppermute | solution.py:295
  141.6 0.5 add_convert_fusion
  142.1 35.2 %all_to_all.15 = bf16[32,14,16,128]{3,2,1,0:T(8,128)(2,1)S(1)} all-to-all(bf16[32,14,16,128]{3,2,1,0:T(8,128)(2,1)S(1)} %add_convert_fusion), channel_id=1, replica_groups=mesh['space'=4,'chan'=32] {'chan'}, dimensions={0} | all-to-all | bytes 3670016 | tf_op jit(solution)/shard_map/all_to_all | solution.py:296
  177.4 0.3 convert_reduce_fusion
  177.6 4.6 %collective-permute-start.10 = (f32[14,16,128]{2,1,0:T(8,128)S(1)}, f32[14,16,128]{2,1,0:T(8,128)S(1)}, u32[]{:S(2)}, u32[]{:S(2)}) collective-permute-start(f32[14,16,128]{2,1,0:T(8,128)S(1)} %convert_reduce_fusion), channel_id=1, source_target_pairs={{0,96},{32,64},{64,32},{96,0},{1,97},{33,65},{65,33},{97,1},{2,98}... | collective-permute-start | bytes 344072 | tf_op jit(solution)/shard_map/ppermute | solution.py:299
  182.2 0.0 collective-permute-start.9
  182.2 0.2 collective-permute-start.8
  182.4 3.5 %collective-permute-done.10 = f32[14,16,128]{2,1,0:T(8,128)S(1)} collective-permute-done((f32[14,16,128]{2,1,0:T(8,128)S(1)}, f32[14,16,128]{2,1,0:T(8,128)S(1)}, u32[]{:S(2)}, u32[]{:S(2)}) %collective-permute-start.10) | collective-permute-done | bytes 114720 | tf_op jit(solution)/shard_map/ppermute | solution.py:299
  185.9 0.0 collective-permute-done.9
  185.9 2.0 %collective-permute-done.8 = f32[14,16,128]{2,1,0:T(8,128)S(1)} collective-permute-done((f32[14,16,128]{2,1,0:T(8,128)S(1)}, f32[14,16,128]{2,1,0:T(8,128)S(1)}, u32[]{:S(2)}, u32[]{:S(2)}) %collective-permute-start.8) | collective-permute-done | bytes 114720 | tf_op jit(solution)/shard_map/ppermute | solution.py:298
  187.9 0.7 fusion
  (25 shorter events, 0.2 us)
Async XLA Ops:
  0.6 0.9 copy-start
  2.9 9.9 %copy-start.10 = (s32[1,1,4,1024]{3,2,1,0:T(4,128)S(1)}, s32[1,1,4,1024]{3,2,1,0:T(4,128)}, u32[]{:S(2)}) copy-start(s32[1,1,4,1024]{3,2,1,0:T(4,128)} %param.10) | copy-start | bytes 49156
  2.9 9.9 %copy-start.2 = (bf16[2048,256]{1,0:T(8,128)(2,1)S(1)}, bf16[2048,256]{1,0:T(8,128)(2,1)}, u32[]{:S(2)}) copy-start(bf16[2048,256]{1,0:T(8,128)(2,1)} %feats_ref.1) | copy-start | bytes 3145732
  2.9 9.9 %copy-start.6 = (s32[1,1,4]{2,1,0:T(1,128)S(1)}, s32[1,1,4]{2,1,0:T(1,128)}, u32[]{:S(2)}) copy-start(s32[1,1,4]{2,1,0:T(1,128)} %param.11) | copy-start | bytes 52
  2.9 34.2 %all-to-all-start.1 = ((bf16[32,14,8,256]{3,2,1,0:T(8,128)(2,1)}), bf16[32,14,8,256]{3,2,1,0:T(8,128)(2,1)S(1)}, u32[]{:S(2)}, u32[]{:S(2)}) async-start(bf16[32,14,8,256]{3,2,1,0:T(8,128)(2,1)} %broadcast_in_dim.11), calls=%async_computation.1 | async-start | bytes 3670016 | tf_op jit(solution)/shard_map/all_to_all | solution.py:267
  20.0 51.2 %copy-start.3 = (f32[4,1,32,3,128]{4,2,3,1,0:T(8,128)S(1)}, f32[4,1,32,3,128]{4,2,3,1,0:T(8,128)}, u32[]{:S(2)}) copy-start(f32[4,1,32,3,128]{4,2,3,1,0:T(8,128)} %param.14) | copy-start | bytes 589828
  20.0 51.2 %copy-start.4 = (s32[4,1,32,128]{3,2,1,0:T(8,128)S(1)}, s32[4,1,32,128]{3,2,1,0:T(8,128)}, u32[]{:S(2)}) copy-start(s32[4,1,32,128]{3,2,1,0:T(8,128)} %param.12) | copy-start | bytes 196612
  20.0 51.2 %copy-start.5 = (s32[4,1,32]{2,1,0:T(1,128)S(1)}, s32[4,1,32]{2,1,0:T(1,128)}, u32[]{:S(2)}) copy-start(s32[4,1,32]{2,1,0:T(1,128)} %param.13) | copy-start | bytes 1540
  37.0 1.2 copy-start.7
  38.3 32.8 %all-to-all-start = ((bf16[4,1024,256]{2,1,0:T(8,128)(2,1)}), bf16[4,1024,256]{2,1,0:T(8,128)(2,1)S(1)}, u32[]{:S(2)}, u32[]{:S(2)}) async-start(bf16[4,1024,256]{2,1,0:T(8,128)(2,1)} %shard_map.104), calls=%async_computation | async-start | bytes 4194304 | tf_op jit(solution)/shard_map/all_to_all | solution.py:275
  44.8 61.1 %collective-permute-start.6 = (bf16[32,14,8,256]{3,2,1,0:T(8,128)(2,1)}, bf16[32,14,8,256]{3,2,1,0:T(8,128)(2,1)}, u32[]{:S(2)}, u32[]{:S(2)}) collective-permute-start(bf16[32,14,8,256]{3,2,1,0:T(8,128)(2,1)} %copy-done.7), channel_id=1, source_target_pairs={{0,32},{32,0},{64,96},{96,64},{1,33},{33,1},{65,97},{97,65},{2,34}... | collective-permute-start | bytes 5505032 | tf_op jit(solution)/shard_map/ppermute | solution.py:268
  71.1 20.2 %copy-start.11 = (bf16[256]{0:T(256)(128)(2,1)S(1)}, bf16[256]{0:T(256)(128)(2,1)}, u32[]{:S(2)}) copy-start(bf16[256]{0:T(256)(128)(2,1)} %param.16) | copy-start | bytes 1540
  87.7 12.9 %copy-start.1 = (bf16[4,4,128,256]{3,2,1,0:T(8,128)(2,1)}, bf16[4,4,128,256]{3,2,1,0:T(8,128)(2,1)S(1)}, u32[]{:S(2)}) copy-start(bf16[4,4,128,256]{3,2,1,0:T(8,128)(2,1)S(1)} %shard_map.105.latent_ref) | copy-start | bytes 3145732
  87.7 18.2 %copy-start.8 = (bf16[32,14,8,256]{3,2,1,0:T(8,128)(2,1)S(1)}, bf16[32,14,8,256]{3,2,1,0:T(8,128)(2,1)}, u32[]{:S(2)}) copy-start(bf16[32,14,8,256]{3,2,1,0:T(8,128)(2,1)} %copy-done.7) | copy-start | bytes 5505028
  88.5 10.2 %collective-permute-start = (bf16[1,4,128,256]{3,2,1,0:T(8,128)(2,1)}, bf16[1,4,128,256]{3,2,1,0:T(8,128)(2,1)S(1)}, u32[]{:S(2)}, u32[]{:S(2)}) collective-permute-start(bf16[1,4,128,256]{3,2,1,0:T(8,128)(2,1)} %get-tuple-element.12), channel_id=1, source_target_pairs={{0,32},{32,64},{64,96},{1,33},{33,65},{65,97},{2,34},{34,66},{66,9... | collective-permute-start | bytes 786440 | tf_op jit(solution)/shard_map/ppermute | solution.py:281
  91.4 9.2 %collective-permute-start.1 = (bf16[1,4,128,256]{3,2,1,0:T(8,128)(2,1)S(1)}, bf16[1,4,128,256]{3,2,1,0:T(8,128)(2,1)S(1)}, u32[]{:S(2)}, u32[]{:S(2)}) collective-permute-start(bf16[1,4,128,256]{3,2,1,0:T(8,128)(2,1)S(1)} %get-tuple-element.11), channel_id=1, source_target_pairs={{32,0},{64,32},{96,64},{33,1},{65,33},{97,65},{34,2},{66,34},{98,6... | collective-permute-start | bytes 786440 | tf_op jit(solution)/shard_map/ppermute | solution.py:282
  93.3 18.3 %collective-permute-start.3 = (bf16[4,1,128,256]{3,2,1,0:T(8,128)(2,1)S(1)}, bf16[4,1,128,256]{3,2,1,0:T(8,128)(2,1)S(1)}, u32[]{:S(2)}, u32[]{:S(2)}) collective-permute-start(bf16[4,1,128,256]{3,2,1,0:T(8,128)(2,1)S(1)} %get-tuple-element.9), channel_id=1, source_target_pairs={{1,0},{2,1},{3,2},{4,3},{5,4},{6,5},{7,6},{8,7},{9,8},{10,9},{11,1... | collective-permute-start | bytes 786440 | tf_op jit(solution)/shard_map/ppermute | solution.py:284
  94.6 17.0 %collective-permute-start.2 = (bf16[4,1,128,256]{3,2,1,0:T(8,128)(2,1)S(1)}, bf16[4,1,128,256]{3,2,1,0:T(8,128)(2,1)S(1)}, u32[]{:S(2)}, u32[]{:S(2)}) collective-permute-start(bf16[4,1,128,256]{3,2,1,0:T(8,128)(2,1)S(1)} %get-tuple-element.10), channel_id=1, source_target_pairs={{0,1},{1,2},{2,3},{3,4},{4,5},{5,6},{6,7},{7,8},{8,9},{9,10},{10,1... | collective-permute-start | bytes 786440 | tf_op jit(solution)/shard_map/ppermute | solution.py:283
  100.6 11.0 %collective-permute-start.5 = (bf16[2,1,128,256]{3,2,1,0:T(8,128)(2,1)S(1)}, bf16[2,1,128,256]{3,2,1,0:T(8,128)(2,1)S(1)}, u32[]{:S(2)}, u32[]{:S(2)}) collective-permute-start(bf16[2,1,128,256]{3,2,1,0:T(8,128)(2,1)S(1)} %get-tuple-element.13), channel_id=1, source_target_pairs={{1,0},{2,1},{3,2},{4,3},{5,4},{6,5},{7,6},{8,7},{9,8},{10,9},{11,1... | collective-permute-start | bytes 393224 | tf_op jit(solution)/shard_map/ppermute | solution.py:287
  101.9 9.7 %collective-permute-start.4 = (bf16[2,1,128,256]{3,2,1,0:T(8,128)(2,1)S(1)}, bf16[2,1,128,256]{3,2,1,0:T(8,128)(2,1)S(1)}, u32[]{:S(2)}, u32[]{:S(2)}) collective-permute-start(bf16[2,1,128,256]{3,2,1,0:T(8,128)(2,1)S(1)} %get-tuple-element.14), channel_id=1, source_target_pairs={{0,1},{1,2},{2,3},{3,4},{4,5},{5,6},{6,7},{7,8},{8,9},{9,10},{10,1... | collective-permute-start | bytes 393224 | tf_op jit(solution)/shard_map/ppermute | solution.py:286
  135.8 5.8 %copy-start.9 = (bf16[32,27,16,128]{3,2,1,0:T(8,128)(2,1)S(1)}, bf16[32,27,16,128]{3,2,1,0:T(8,128)(2,1)}, u32[]{:S(2)}) copy-start(bf16[32,27,16,128]{3,2,1,0:T(8,128)(2,1)} %get-tuple-element.5) | copy-start | bytes 10616836
  137.8 3.9 %collective-permute-start.7 = (bf16[32,14,16,128]{3,2,1,0:T(8,128)(2,1)S(1)}, bf16[32,14,16,128]{3,2,1,0:T(8,128)(2,1)S(1)}, u32[]{:S(2)}, u32[]{:S(2)}) collective-permute-start(bf16[32,14,16,128]{3,2,1,0:T(8,128)(2,1)S(1)} %constant_dynamic-slice_fusion), channel_id=1, source_target_pairs={{0,32},{32,0},{64,96},{96,64},{1,33},{33,1},{65,97},{97,65},{2,34}... | collective-permute-start | bytes 5505032 | tf_op jit(solution)/shard_map/ppermute | solution.py:295
  177.6 8.3 %collective-permute-start.10 = (f32[14,16,128]{2,1,0:T(8,128)S(1)}, f32[14,16,128]{2,1,0:T(8,128)S(1)}, u32[]{:S(2)}, u32[]{:S(2)}) collective-permute-start(f32[14,16,128]{2,1,0:T(8,128)S(1)} %convert_reduce_fusion), channel_id=1, source_target_pairs={{0,96},{32,64},{64,32},{96,0},{1,97},{33,65},{65,33},{97,1},{2,98}... | collective-permute-start | bytes 344072 | tf_op jit(solution)/shard_map/ppermute | solution.py:299
  182.2 3.7 %collective-permute-start.9 = (f32[14,16,128]{2,1,0:T(8,128)S(1)}, f32[14,16,128]{2,1,0:T(8,128)S(1)}, u32[]{:S(2)}, u32[]{:S(2)}) collective-permute-start(f32[14,16,128]{2,1,0:T(8,128)S(1)} %convert_reduce_fusion), channel_id=1, source_target_pairs={{0,32},{32,0},{64,96},{96,64},{1,33},{33,1},{65,97},{97,65},{2,34}... | collective-permute-start | bytes 344072 | tf_op jit(solution)/shard_map/ppermute | solution.py:299
  182.2 5.7 %collective-permute-start.8 = (f32[14,16,128]{2,1,0:T(8,128)S(1)}, f32[14,16,128]{2,1,0:T(8,128)S(1)}, u32[]{:S(2)}, u32[]{:S(2)}) collective-permute-start(f32[14,16,128]{2,1,0:T(8,128)S(1)} %convert_reduce_fusion), channel_id=1, source_target_pairs={{0,64},{32,96},{64,0},{96,32},{1,65},{33,97},{65,1},{97,33},{2,66}... | collective-permute-start | bytes 344072 | tf_op jit(solution)/shard_map/ppermute | solution.py:298

commit v2 on v1

v2 whole, which is shorter than its diff:
```python
import math

import jax
import jax.numpy as jnp
from jax import lax
from jax.experimental import pallas as pl
from jax.experimental.pallas import tpu as pltpu
from jax.sharding import PartitionSpec as P

BF = jnp.bfloat16
F32 = jnp.float32


def send_kernel(owner_ref, slots_ref, counts_ref, feats_ref, *out_refs):
    points = feats_ref.shape[0]
    point_ids = lax.broadcasted_iota(jnp.int32, (128, points), 1)
    for place, out_ref in enumerate(out_refs):
        owner = owner_ref[place]
        slots = slots_ref[owner]
        position = lax.broadcasted_iota(
            jnp.int32, slots.shape, 0
        ) * 128 + lax.broadcasted_iota(jnp.int32, slots.shape, 1)
        columns = jnp.where(position < counts_ref[owner], slots, -1).T
        for half in range(2):
            hot = [
                jnp.where(point_ids == columns[:, r : r + 1], 1.0, 0.0).astype(BF)
                for r in range(half * 4, half * 4 + 4)
            ]
            rows = jnp.dot(
                jnp.concatenate(hot, axis=0), feats_ref[...], preferred_element_type=F32
            )
            out_ref[half * 512 : half * 512 + 512, :] = rows.astype(BF)


def gather_listed(feats, slots, counts, owners):
    spaces, capacity = slots.shape
    channels = feats.shape[1]
    whole = pl.BlockSpec(memory_space=pltpu.VMEM)
    scalars = pl.BlockSpec(memory_space=pltpu.SMEM)
    count = owners.shape[0]
    return pl.pallas_call(
        send_kernel,
        in_specs=[scalars, whole, scalars, whole],
        out_specs=[whole] * count,
        out_shape=[jax.ShapeDtypeStruct((capacity, channels), BF)] * count,
        compiler_params=pltpu.CompilerParams(vmem_limit_bytes=40 << 20),
    )(owners, slots.reshape(spaces, capacity // 128, 128), counts, feats)


def spread_kernel(fill_ref, near_ref, place_ref, out_ref, denom_ref):
    plane = pl.program_id(0)
    tiles = near_ref.shape[1]
    slots = near_ref.shape[2]
    groups = out_ref.shape[1] // 256
    cell = lax.broadcasted_iota(jnp.int32, (16, slots), 0)
    centre_x = (cell // 4).astype(F32) - 1.5
    centre_y = (cell % 4).astype(F32) - 1.5
    lane = lax.broadcasted_iota(jnp.int32, (16, slots), 1)
    low_ids = lax.broadcasted_iota(jnp.int32, (256, slots), 0)

    def one_tile(tile, carry):
        near = near_ref[0, pl.ds(tile, 1), :]
        along_x = place_ref[0, 0, pl.ds(tile, 1), :] - centre_x
        along_y = place_ref[0, 1, pl.ds(tile, 1), :] - centre_y
        along_z = place_ref[0, 2, pl.ds(tile, 1), :]
        values = jnp.exp(-0.5 * (along_x * along_x + along_y * along_y + along_z * along_z))
        values = jnp.where(lane < fill_ref[plane, tile], values, 0.0)
        start = pl.multiple_of(tile * 16, 16)
        denom_ref[pl.ds(start, 16), :] = jnp.broadcast_to(
            1.0 + jnp.sum(values, axis=1, keepdims=True), (16, 128)
        )
        half = values.astype(BF).astype(F32)
        high = jnp.broadcast_to(near >> 8, (16, slots))
        low = near & 255
        stacked = jnp.concatenate(
            [jnp.where(high == g, half, 0.0).astype(BF) for g in range(groups)], axis=0
        )
        hot = jnp.where(low_ids == low, 1.0, 0.0).astype(BF)
        block = lax.dot_general(
            stacked, hot, (((1,), (1,)), ((), ())), preferred_element_type=F32
        ).astype(BF)
        for g in range(groups):
            out_ref[pl.ds(start, 16), g * 256 : g * 256 + 256] = block[g * 16 : g * 16 + 16, :]
        return carry

    lax.fori_loop(0, tiles, one_tile, 0, unroll=4)


def spread_weights(near, fill, place, rows):
    planes, tiles, slots = near.shape
    return pl.pallas_call(
        spread_kernel,
        grid=(planes,),
        in_specs=[
            pl.BlockSpec(memory_space=pltpu.SMEM),
            pl.BlockSpec((1, tiles, slots), lambda z: (z, 0, 0)),
            pl.BlockSpec((1, 3, tiles, slots), lambda z: (z, 0, 0, 0)),
        ],
        out_specs=[
            pl.BlockSpec((tiles * 16, rows), lambda z: (z, 0)),
            pl.BlockSpec((tiles * 16, 128), lambda z: (z, 0)),
        ],
        out_shape=[
            jax.ShapeDtypeStruct((planes * tiles * 16, rows), BF),
            jax.ShapeDtypeStruct((planes * tiles * 16, 128), F32),
        ],
        compiler_params=pltpu.CompilerParams(vmem_limit_bytes=40 << 20),
        cost_estimate=pl.CostEstimate(
            flops=4 << 30, bytes_accessed=18 << 20, transcendentals=1 << 20
        ),
    )(fill, near, place)


def latent_kernel(
    flags_ref, spread_ref, denom_ref, t0, t1, t2, t3,
    out_ref, near_ref, far_ref, low_ref, high_ref, total, order,
):
    plane = pl.program_id(0)
    last = pl.num_programs(0) - 1
    core = flags_ref[0]
    capacity, channels = t0.shape
    cells = spread_ref.shape[0]
    tiles = cells // 16
    summed = jnp.dot(
        spread_ref[:, 0:capacity], t0[...], preferred_element_type=F32
    )
    for place, table in ((1, t1), (2, t2), (3, t3)):
        summed = summed + jnp.dot(
            spread_ref[:, place * capacity : (place + 1) * capacity],
            table[...],
            preferred_element_type=F32,
        )
    for lanes in range(0, channels, 128):
        part = slice(lanes, lanes + 128)
        total[...] = summed[:, part] / denom_ref[...]
        for u in range(4):
            for v in range(4):
                order[pl.ds(v, tiles, stride=4), :] = total[
                    pl.ds(u * 4 + v, tiles, stride=16), :
                ]
            out_ref[0, u, :, part] = order[...].astype(BF)
    low_ref[0, 0] = out_ref[0, 0]
    high_ref[0, 0] = out_ref[0, 3]

    @pl.when(plane == (1 - core) * last)
    def _():
        near_ref[...] = out_ref[...]

    @pl.when(plane == core * last)
    def _():
        far_ref[...] = out_ref[...]


def latent_block(flags, spread, denom, tables):
    cells = spread.shape[0]
    planes = 4
    per_plane = cells // planes
    capacity, channels = tables[0].shape
    width = per_plane // 4
    whole = pl.BlockSpec((capacity, channels), lambda z: (0, 0))
    plane_spec = pl.BlockSpec((1, 4, width, channels), lambda z: (0, 0, 0, 0))
    row_spec = pl.BlockSpec((1, 1, width, channels), lambda z: (z, 0, 0, 0))
    return pl.pallas_call(
        latent_kernel,
        grid=(planes,),
        in_specs=[
            pl.BlockSpec(memory_space=pltpu.SMEM),
            pl.BlockSpec((per_plane, spread.shape[1]), lambda z: (z, 0)),
            pl.BlockSpec((per_plane, 128), lambda z: (z, 0)),
        ]
        + [whole] * 4,
        out_specs=[
            pl.BlockSpec((1, 4, width, channels), lambda z: (z, 0, 0, 0)),
            plane_spec,
            plane_spec,
            row_spec,
            row_spec,
        ],
        out_shape=[
            jax.ShapeDtypeStruct((planes, 4, width, channels), BF),
            jax.ShapeDtypeStruct((1, 4, width, channels), BF),
            jax.ShapeDtypeStruct((1, 4, width, channels), BF),
            jax.ShapeDtypeStruct((planes, 1, width, channels), BF),
            jax.ShapeDtypeStruct((planes, 1, width, channels), BF),
        ],
        scratch_shapes=[
            pltpu.VMEM((per_plane, 128), F32),
            pltpu.VMEM((width, 128), F32),
        ],
        compiler_params=pltpu.CompilerParams(vmem_limit_bytes=40 << 20),
    )(flags, spread, denom, *tables)


def conv_kernel(
    flags_ref, latent_ref, near_ref, far_ref, left_ref, right_ref, left_rim_ref, right_rim_ref,
    weight_ref, bias_ref, cotangent_ref, act_ref, keep_ref, give_ref,
    padded, turned, taps, shifted,
):
    planes, rows_x, width, channels = latent_ref.shape
    flat = rows_x * width
    padded[1 : planes + 1, 1 : rows_x + 1] = latent_ref[...]
    core = flags_ref[0]
    has_far = flags_ref[1] > 0
    has_left = flags_ref[2] > 0
    has_right = flags_ref[3] > 0
    near_z = (1 - core) * (planes + 1)
    far_z = core * (planes + 1)
    none = jnp.zeros((), BF)
    padded[pl.ds(near_z, 1), 1 : rows_x + 1] = near_ref[...]
    padded[pl.ds(far_z, 1), 1 : rows_x + 1] = jnp.where(has_far, far_ref[...], none)
    for has, column, face_ref, rim_ref in (
        (has_left, 0, left_ref, left_rim_ref),
        (has_right, rows_x + 1, right_ref, right_rim_ref),
    ):
        padded[1 : planes + 1, column] = jnp.where(has, face_ref[:, 0], none)
        padded[pl.ds(near_z, 1), column] = jnp.where(has, rim_ref[0:1], none)
        padded[pl.ds(far_z, 1), column] = jnp.where(
            jnp.logical_and(has, has_far), rim_ref[1:2], none
        )
    y_ids = lax.broadcasted_iota(jnp.int32, (width, channels), 0)
    root = math.sqrt(2.0 / math.pi)

    def turn(z, carry):
        block = padded[z].reshape((rows_x + 2) * width, channels)
        turned[z] = block.T
        return carry

    lax.fori_loop(0, planes + 2, turn, 0)

    def conv_plane(z, carry):
        pieces = [
            padded[z + dz, dx : dx + rows_x].reshape(flat, channels)
            for dz in range(3)
            for dx in range(3)
        ]
        patch = jnp.concatenate(pieces, axis=1)
        for dy in range(3):
            matrix = jnp.concatenate([weight_ref[3 * tap + dy] for tap in range(9)], axis=0)
            taps[:, dy * channels : (dy + 1) * channels] = jnp.dot(
                patch, matrix, preferred_element_type=F32
            )
        for x in range(rows_x):
            rows = slice(x * width, (x + 1) * width)
            low = jnp.where(y_ids == 0, 0.0, pltpu.roll(taps[rows, 0:channels], 1, 0))
            high = jnp.where(
                y_ids == width - 1, 0.0, pltpu.roll(taps[rows, 2 * channels :], width - 1, 0)
            )
            pre = low + taps[rows, channels : 2 * channels] + high + bias_ref[...]
            square = pre * pre
            inner = root * (pre + 0.044715 * (square * pre))
            bent = jnp.tanh(inner)
            gate = 0.5 * (1.0 + bent)
            act_ref[z, x] = (pre * gate).astype(BF)
            slope = gate + 0.5 * pre * (1.0 - bent * bent) * (
                root * (1.0 + 3.0 * 0.044715 * square)
            )
            grad = (cotangent_ref[z, x].astype(F32) * slope).astype(BF).astype(F32)
            start = pl.multiple_of(z * flat + x * width, width)
            shifted[pl.ds(start, width), 0:channels] = jnp.where(
                y_ids == width - 1, 0.0, pltpu.roll(grad, width - 1, 0)
            ).astype(BF)
            shifted[pl.ds(start, width), channels : 2 * channels] = grad.astype(BF)
            shifted[pl.ds(start, width), 2 * channels :] = jnp.where(
                y_ids == 0, 0.0, pltpu.roll(grad, 1, 0)
            ).astype(BF)
        return carry

    lax.fori_loop(0, planes, conv_plane, 0)

    def grad_taps(tap, carry):
        dz = tap // 3
        start = pl.multiple_of((tap % 3) * width, width)
        pieces = [turned[z + dz, :, pl.ds(start, flat)] for z in range(planes)]
        sums = jnp.dot(
            jnp.concatenate(pieces, axis=1), shifted[...], preferred_element_type=F32
        )
        for dy in range(3):
            part = sums[:, dy * channels : (dy + 1) * channels]
            both = jnp.concatenate(
                [
                    part[:, :128].reshape(channels // 8, 8, 128),
                    part[:, 128:].reshape(channels // 8, 8, 128),
                ],
                axis=1,
            )
            position = tap * 3 + dy
            half = position // 14
            slot = position - half * 14
            rounded = both.astype(BF)

            @pl.when(half == core)
            def _():
                keep_ref[:, slot] = rounded

            @pl.when(half != core)
            def _():
                give_ref[:, slot] = rounded
        return carry

    lax.fori_loop(0, 9, grad_taps, 0)
    unused = jnp.zeros((channels // 8, 16, 128), BF)

    @pl.when(core == 1)
    def _():
        keep_ref[:, 13] = unused

    @pl.when(core == 0)
    def _():
        give_ref[:, 13] = unused


def conv_block(
    flags, latent, near, far, left, right, left_rim, right_rim, weight, bias, cotangent
):
    planes, rows_x, width, channels = latent.shape
    flat = rows_x * width
    whole = pl.BlockSpec(memory_space=pltpu.VMEM)
    half_terms = jax.ShapeDtypeStruct((channels // 8, 14, 16, 128), BF)
    return pl.pallas_call(
        conv_kernel,
        in_specs=[pl.BlockSpec(memory_space=pltpu.SMEM)] + [whole] * 10,
        out_specs=[whole] * 3,
        out_shape=[jax.ShapeDtypeStruct(latent.shape, BF), half_terms, half_terms],
        scratch_shapes=[
            pltpu.VMEM((planes + 2, rows_x + 2, width, channels), BF),
            pltpu.VMEM((planes + 2, channels, (rows_x + 2) * width), BF),
            pltpu.VMEM((flat, 3 * channels), F32),
            pltpu.VMEM((planes * flat, 3 * channels), BF),
        ],
        compiler_params=pltpu.CompilerParams(vmem_limit_bytes=52 << 20),
    )(flags, latent, near, far, left, right, left_rim, right_rim, weight, bias, cotangent)


def in_order(core, own, other):
    low = jnp.where(core == 0, own, other)
    high = jnp.where(core == 0, other, own)
    return low, high


def on_device(
    point_feats,
    send_slots,
    send_counts,
    neighbors,
    tile_fill,
    offsets,
    weight,
    conv_bias,
    cotangent,
):
    spaces = lax.axis_size("space")
    chans = lax.axis_size("chan")
    planes, rows_x, width_y, channels = cotangent.shape
    row_count = weight.shape[0]
    space = lax.axis_index("space")
    chan = lax.axis_index("chan")
    core = lax.rem(space, 2)
    swap = [(i, i ^ 1) for i in range(spaces)]
    far = [(i, i ^ 2) for i in range(spaces)]
    cross = [(i, i ^ 3) for i in range(spaces)]
    up_chan = [(i, (i + 1) % chans) for i in range(chans)]
    down_chan = [((i + 1) % chans, i) for i in range(chans)]
    flags = jnp.stack(
        [
            core,
            jnp.logical_or(space == 1, space == 2).astype(jnp.int32),
            (chan > 0).astype(jnp.int32),
            (chan < chans - 1).astype(jnp.int32),
        ]
    )

    slots, counts = send_slots[0, 0], send_counts[0, 0]
    owners = space ^ jnp.arange(spaces, dtype=jnp.int32)
    to_far, to_cross = gather_listed(point_feats, slots, counts, owners[2:])
    from_far = lax.ppermute(to_far, "space", far)
    from_cross = lax.ppermute(to_cross, "space", cross)
    held_feats, _ = lax.optimization_barrier((point_feats, to_far))
    to_self, to_other = gather_listed(held_feats, slots, counts, owners[:2])
    from_other = lax.ppermute(to_other, "space", swap)

    taps = jnp.pad(weight.transpose(1, 0, 2), ((0, 1), (0, 0), (0, 0)))
    gathered = lax.dynamic_slice_in_dim(taps, core * 14, 14, 0)
    for step, count in ((16, 2), (1, 4), (4, 4)):
        index = lax.rem(chan // step, count)
        pieces = [gathered] + [
            lax.ppermute(gathered, "chan", [(i, i ^ (offset * step)) for i in range(chans)])
            for offset in range(1, count)
        ]
        if step == 4:
            break
        gathered = jnp.zeros((count,) + gathered.shape, BF)
        for offset, piece in enumerate(pieces):
            gathered = lax.dynamic_update_index_in_dim(gathered, piece, index ^ offset, 0)
    gathered = jnp.zeros((2, count) + pieces[0].shape, BF)
    for offset, piece in enumerate(pieces):
        for half, part in ((core, piece), (1 - core, lax.ppermute(piece, "space", swap))):
            gathered = lax.dynamic_update_slice(
                gathered, part[None, None], (half, index ^ offset) + (0,) * part.ndim
            )
    full_weight = gathered.transpose(0, 4, 3, 1, 2, 5, 6).reshape(28, channels, channels)

    capacity = slots.shape[1]
    spread, denom = spread_weights(
        neighbors[:, 0] ^ (space * capacity),
        tile_fill[:, 0],
        offsets[:, 0].transpose(0, 2, 1, 3),
        spaces * capacity,
    )
    latent, near_plane, far_plane, low_row, high_row = latent_block(
        flags, spread, denom, (to_self, from_other, from_far, from_cross)
    )

    far_rim = lax.ppermute(far_plane, "space", cross)
    near_rim = lax.ppermute(near_plane, "space", swap)
    left = lax.ppermute(high_row, "chan", up_chan)
    right = lax.ppermute(low_row, "chan", down_chan)
    rims = jnp.concatenate([near_rim, far_rim], axis=0)
    left_rim = lax.ppermute(rims[:, rows_x - 1], "chan", up_chan)
    right_rim = lax.ppermute(rims[:, 0], "chan", down_chan)

    activated, keep, give = conv_block(
        flags, latent, near_rim, far_rim, left, right, left_rim, right_rim,
        full_weight, conv_bias.astype(F32)[None], cotangent,
    )

    paired = (keep.astype(F32) + lax.ppermute(give, "space", swap).astype(F32)).astype(BF)
    collected = lax.all_to_all(paired, "chan", split_axis=0, concat_axis=0, tiled=True)
    summed = jnp.sum(collected.astype(F32), axis=0)
    own_sum = summed + lax.ppermute(summed, "space", far)
    low_sum, high_sum = in_order(core, own_sum, lax.ppermute(own_sum, "space", swap))
    total = jnp.concatenate([low_sum, high_sum[:13]], axis=0)
    total = total.reshape(27, 2, row_count, channels // 2).transpose(2, 0, 1, 3)
    scaling = 1.0 / math.sqrt(planes * spaces * rows_x * chans * width_y)
    return (activated, total.reshape(row_count, 27, channels) * scaling)


def solution(mesh):
    return jax.shard_map(
        on_device,
        mesh=mesh,
        in_specs=(
            P(("space", "chan"), None),
            P("space", "chan", None, None),
            P("space", "chan", None),
            P("space", "chan", None, None),
            P("space", "chan", None),
            P("space", "chan", None, None, None),
            P("chan", None, None),
            P(),
            P("space", "chan", None, None),
        ),
        out_specs=(P("space", "chan", None, None), P("chan", None, None)),
        check_vma=False,
    )
```

time: 189 us -> 177 us (0.937)
  waiting for transfers between devices: 54.6 us -> 37.4 us
  Pallas kernels: 47.9 us -> 55 us
  blocking collectives: 35.2 us -> 31.1 us
  local copies, waits for them, and re-layouts: 8.33 us -> 11.8 us
    all_to_all x2 -> x0, waiting for transfers between devices: 43.4 us -> none  [the longest x1 26.3 us: on_device(): lax.all_to_all(outgoing, 'space', split_axis=0, concat_axis=0, tiled=True)]
    ppermute x10 -> x22, waiting for transfers between devices: 9.15 us -> 33.8 us  [the longest x7 24.5 us: on_device(): lax.ppermute(gathered, 'chan', [(i, i ^ offset * step) for i in range(cha...]
    all_to_all x2 -> x0, starting transfers between devices: 16.4 us -> none  [the longest x1 9.86 us: on_device(): lax.all_to_all(spread, 'chan', split_axis=0, concat_axis=0, tiled=True)]
    pallas_call x2 -> x4, Pallas kernels: 31.3 us -> 45.9 us  [the longest x1 25.4 us: conv_block(): pl.pallas_call(conv_kernel, in_specs=[pl.BlockSpec(memory_space=pltpu.SME...]
    ppermute x10 -> x22, starting transfers between devices: 20 us -> 34.6 us  [the longest x7 11.2 us: on_device(): lax.ppermute(gathered, 'chan', [(i, i ^ offset * step) for i in range(cha...]
    pallas_call x1, Pallas kernels: 16.6 us -> 9.04 us  [latent_block(): pl.pallas_call(latent_kernel, grid=(planes,), in_specs=[pl.BlockSpec(memo...]
    dynamic_update_slice x0 -> x14, local copies, waits for them, and re-layouts: none -> 5.88 us  [the longest x6 3.49 us: on_device(): lax.dynamic_update_index_in_dim(gathered, piece, index ^ offset, 0)]
    all_to_all x1, blocking collectives: 35.2 us -> 31.1 us  [on_device(): lax.all_to_all(paired, 'chan', split_axis=0, concat_axis=0, tiled=True)]
  transfers between devices with their start and end apart: 13 -> 23, of which waited for: 6 -> 11; matrix products, arithmetic and copies ran while one was open for 3% -> 5% of each run, Pallas kernels for 13% -> 15%
where the time goes in v2:
time: 177 us; the launch traced here: 176 us
  Pallas kernels  55 us (31%)
  waiting for transfers between devices  37.4 us (21%)
  starting transfers between devices  36.2 us (20%)
  blocking collectives  31.1 us (18%)
  local copies, waits for them, and re-layouts  11.8 us (7%)
  other arithmetic  3.91 us (2%)
    all_to_all x1, blocking collectives, on_device(): lax.all_to_all(paired, 'chan', split_axis=0, concat_axis=0, tiled=True)  31.1 us
    pallas_call x1, Pallas kernels, conv_block(): pl.pallas_call(conv_kernel, in_specs=[pl.BlockSpec(memory_space=pltpu.SME...  25.4 us
    ppermute x7, waiting for transfers between devices, on_device(): lax.ppermute(gathered, 'chan', [(i, i ^ offset * step) for i in range(cha...  24.5 us
    pallas_call x1, Pallas kernels, spread_weights(): pl.pallas_call(spread_kernel, grid=(planes,), in_specs=[pl.BlockSpec(memo...  12.7 us
    ppermute x7, starting transfers between devices, on_device(): lax.ppermute(gathered, 'chan', [(i, i ^ offset * step) for i in range(cha...  11.2 us
    pallas_call x1, Pallas kernels, latent_block(): pl.pallas_call(latent_kernel, grid=(planes,), in_specs=[pl.BlockSpec(memo...  9.04 us
    pallas_call x2, Pallas kernels, gather_listed(): pl.pallas_call(send_kernel, in_specs=[scalars, whole, scalars, whole], ou...  7.83 us
    ppermute x4, starting transfers between devices, on_device(): lax.ppermute(piece, 'space', swap)  4.75 us
  transfers between devices with their start and end apart: 23, of which 11 were waited for; matrix products, arithmetic and copies ran while one was open for 5% of the time, Pallas kernels for 15%

profile of v2, /device:TPU:1, one launch (start us, length us, event | category | flops | bytes accessed | tf_op | source)
XLA Modules:
  0.0 176.3 jit_solution(11572482887384785760)
XLA Ops:
  0.7 0.7 copy.29
  1.5 1.2 copy-done
  2.7 0.7 copy-done.3
  3.3 3.9 %shard_map.105 = (bf16[1024,256]{1,0:T(8,128)(2,1)}, bf16[1024,256]{1,0:T(8,128)(2,1)}) custom-call(s32[2]{0:T(128)S(1)} %get-tuple-element.36.owner_ref, s32[4,8,128]{2,1,0:T(8,128)S(1)} %bitcast.91, s32[4]{0:T(128)S(1)} %bitcast.93, bf16[2048,256]{1,0:T(8,128)(2,1)S(1)} %copy-done), custom_call_target="tpu_custom_call" | custom-call | tf_op jit(solution)/shard_map/pallas_call | solution.py:41
  7.2 3.8 %collective-permute-start.1 = (bf16[1024,256]{1,0:T(8,128)(2,1)}, bf16[1024,256]{1,0:T(8,128)(2,1)S(1)}, u32[]{:S(2)}, u32[]{:S(2)}) collective-permute-start(bf16[1024,256]{1,0:T(8,128)(2,1)} %get-tuple-element.19), channel_id=1, source_target_pairs={{0,64},{32,96},{64,0},{96,32},{1,65},{33,97},{65,1},{97,33},{2,66}... | collective-permute-start | bytes 1572872 | tf_op jit(solution)/shard_map/ppermute | solution.py:375
  11.0 1.2 copy-done.1
  12.2 0.7 copy-done.4
  12.9 3.9 %shard_map.106 = (bf16[1024,256]{1,0:T(8,128)(2,1)S(1)}, bf16[1024,256]{1,0:T(8,128)(2,1)}) custom-call(s32[2]{0:T(128)S(1)} %get-tuple-element.37.owner_ref, s32[4,8,128]{2,1,0:T(8,128)S(1)} %bitcast.92, s32[4]{0:T(128)S(1)} %bitcast.94, bf16[2048,256]{1,0:T(8,128)(2,1)S(1)} %copy-done.1), custom_call_target="tpu_custom_call" | custom-call | tf_op jit(solution)/shard_map/pallas_call | solution.py:41
  16.8 1.0 collective-permute-start
  17.8 0.8 bitcast_dynamic-update-slice_fusion.13
  18.6 1.3 collective-permute-start.9
  19.9 0.8 fusion.1.near_ref
  20.7 14.3 %collective-permute-done.9 = bf16[14,8,256]{2,1,0:T(8,128)(2,1)S(1)} collective-permute-done((bf16[14,8,256]{2,1,0:T(8,128)(2,1)S(1)}, bf16[14,8,256]{2,1,0:T(8,128)(2,1)S(1)}, u32[]{:S(2)}, u32[]{:S(2)}) %collective-permute-start.9) | collective-permute-done | bytes 57376 | tf_op jit(solution)/shard_map/ppermute | solution.py:386
  35.1 1.7 collective-permute-start.10
  36.8 3.3 %collective-permute-start.11 = (bf16[2,14,8,256]{3,2,0,1:T(8,128)(2,1)S(1)}, bf16[2,14,8,256]{3,2,0,1:T(8,128)(2,1)S(1)}, u32[]{:S(2)}, u32[]{:S(2)}) collective-permute-start(bf16[2,14,8,256]{3,2,0,1:T(8,128)(2,1)S(1)} %bitcast_dynamic-update-slice_fusion.12), channel_id=1, source_target_pairs={{0,2},{1,3},{2,0},{3,1},{4,6},{5,7},{6,4},{7,5},{8,10},{9,11},{10,... | collective-permute-start | bytes 344072 | tf_op jit(solution)/shard_map/ppermute | solution.py:386
  40.1 0.8 broadcast_in_dim.59
  40.9 0.7 bitcast_dynamic-update-slice_fusion.10
  41.6 1.0 collective-permute-start.12
  42.6 0.7 bitcast_dynamic-update-slice_fusion.9
  43.6 0.7 bitcast_dynamic-update-slice_fusion.8
  44.3 2.9 %collective-permute-done.12 = bf16[2,14,8,256]{3,2,0,1:T(8,128)(2,1)S(1)} collective-permute-done((bf16[2,14,8,256]{3,2,0,1:T(8,128)(2,1)S(1)}, bf16[2,14,8,256]{3,2,0,1:T(8,128)(2,1)S(1)}, u32[]{:S(2)}, u32[]{:S(2)}) %collective-permute-start.12) | collective-permute-done | bytes 114720 | tf_op jit(solution)/shard_map/ppermute | solution.py:386
  47.2 0.7 bitcast_dynamic-update-slice_fusion.11
  47.9 2.8 %collective-permute-start.13 = (bf16[4,2,14,8,256]{4,3,0,1,2:T(8,128)(2,1)}, bf16[4,2,14,8,256]{4,3,0,1,2:T(8,128)(2,1)}, u32[]{:S(2)}, u32[]{:S(2)}) collective-permute-start(bf16[4,2,14,8,256]{4,3,0,1,2:T(8,128)(2,1)} %bitcast_dynamic-update-slice_fusion.11), channel_id=1, source_target_pairs={{0,32},{32,0},{64,96},{96,64},{1,33},{33,1},{65,97},{97,65},{2,34}... | collective-permute-start | bytes 1376264 | tf_op jit(solution)/shard_map/ppermute | solution.py:396
  50.7 12.7 %shard_map.104 = (bf16[2048,4096]{1,0:T(8,128)(2,1)}, f32[2048,128]{1,0:T(8,128)S(1)}) custom-call(s32[4,32]{1,0:T(4,128)S(1)} %bitcast.99, s32[4,32,128]{2,1,0:T(8,128)S(1)} %fusion.1.near_ref, f32[4,3,32,128]{3,2,1,0:T(8,128)S(1)} %bitcast.98), custom_call_target="tpu_custom_call" | custom-call | flops 4294967296 | bytes 18874368 | tf_op jit(solution)/shard_map/pallas_call | solution.py:91
  63.5 1.2 collective-permute-start.14
  65.2 1.1 bitcast_dynamic-update-slice_fusion.6
  66.3 2.5 %collective-permute-start.16 = (bf16[4,2,14,8,256]{4,3,0,1,2:T(8,128)(2,1)}, bf16[4,2,14,8,256]{4,3,0,1,2:T(8,128)(2,1)S(1)}, u32[]{:S(2)}, u32[]{:S(2)}) collective-permute-start(bf16[4,2,14,8,256]{4,3,0,1,2:T(8,128)(2,1)} %bitcast_dynamic-update-slice_fusion.11), channel_id=1, source_target_pairs={{0,8},{1,9},{2,10},{3,11},{4,12},{5,13},{6,14},{7,15},{8,0},{9,1},... | collective-permute-start | bytes 1376264 | tf_op jit(solution)/shard_map/ppermute | solution.py:386
  69.0 9.0 %shard_map.107 = (bf16[4,4,128,256]{3,2,1,0:T(8,128)(2,1)S(1)}, bf16[1,4,128,256]{3,2,1,0:T(8,128)(2,1)S(1)}, bf16[1,4,128,256]{3,2,1,0:T(8,128)(2,1)S(1)}, bf16...) custom-call(s32[4]{0:T(128)S(1)} %pad_add_fusion.flags_ref, bf16[2048,4096]{1,0:T(8,128)(2,1)} %get-tuple-element.17.spread_ref, ...), custom_call_target="tpu_custom_call" | custom-call | tf_op jit(solution)/shard_map/pallas_call | solution.py:163
  78.1 0.9 collective-permute-start.3
  79.0 1.5 collective-permute-start.4
  80.5 1.1 bitcast_dynamic-update-slice_fusion.5
  82.3 5.6 %collective-permute-done.16 = bf16[4,2,14,8,256]{4,3,0,1,2:T(8,128)(2,1)S(1)} collective-permute-done((bf16[4,2,14,8,256]{4,3,0,1,2:T(8,128)(2,1)}, bf16[4,2,14,8,256]{4,3,0,1,2:T(8,128)(2,1)S(1)}, u32[]{:S(2)}, u32[]{:S(2)}) %collective-permute-start.16) | collective-permute-done | bytes 458784 | tf_op jit(solution)/shard_map/ppermute | solution.py:386
  87.9 2.4 %collective-permute-start.6 = (bf16[4,1,128,256]{3,2,1,0:T(8,128)(2,1)S(1)}, bf16[4,1,128,256]{3,2,1,0:T(8,128)(2,1)S(1)}, u32[]{:S(2)}, u32[]{:S(2)}) collective-permute-start(bf16[4,1,128,256]{3,2,1,0:T(8,128)(2,1)S(1)} %get-tuple-element.28), channel_id=1, source_target_pairs={{1,0},{2,1},{3,2},{4,3},{5,4},{6,5},{7,6},{8,7},{9,8},{10,9},{11,1... | collective-permute-start | bytes 786440 | tf_op jit(solution)/shard_map/ppermute | solution.py:416
  90.3 1.2 collective-permute-done.18
  91.5 1.4 collective-permute-start.17
  93.3 1.2 collective-permute-done.17
  94.4 4.6 %collective-permute-start.8 = (bf16[2,128,256]{2,1,0:T(8,128)(2,1)S(1)}, bf16[2,128,256]{2,1,0:T(8,128)(2,1)S(1)}, u32[]{:S(2)}, u32[]{:S(2)}) collective-permute-start(bf16[2,128,256]{2,1,0:T(8,128)(2,1)S(1)} %get-tuple-element.34), channel_id=1, source_target_pairs={{1,0},{2,1},{3,2},{4,3},{5,4},{6,5},{7,6},{8,7},{9,8},{10,9},{11,1... | collective-permute-start | bytes 393224 | tf_op jit(solution)/shard_map/ppermute | solution.py:419
  99.4 3.3 %collective-permute-done.7.left_rim_ref = bf16[2,128,256]{2,1,0:T(8,128)(2,1)S(1)} collective-permute-done((bf16[2,128,256]{2,1,0:T(8,128)(2,1)S(1)}, bf16[2,128,256]{2,1,0:T(8,128)(2,1)S(1)}, u32[]{:S(2)}, u32[]{:S(2)}) %collective-permute-start.7) | collective-permute-done | bytes 131104 | tf_op jit(solution)/shard_map/ppermute | solution.py:418
  102.7 25.4 %shard_map.108 = (bf16[4,4,128,256]{3,2,1,0:T(8,128)(2,1)}, bf16[32,14,16,128]{3,2,1,0:T(8,128)(2,1)}, bf16[32,14,16,128]{3,2,1,0:T(8,128)(2,1)}) custom-call(s32[4]{0:T(128)S(1)} %pad_add_fusion.flags_ref, bf16[4,4,128,256]{3,2,1,0:T(8,128)(2,1)} %copy-done.2, bf16[1,4,128,256]{3,2,1,0:T(8,128)(2,1)S(1)} %bitcast.89, bf16[1,4,128,256]{3,2,1,0:T(8,128)(2,1)S(1)} %bitcast.90, ...), custom_call_target="tpu_custom_call" | custom-call | tf_op jit(solution)/shard_map/pallas_call | solution.py:319
  128.0 1.0 collective-permute-start.20
  129.0 3.6 %collective-permute-done.20 = bf16[32,14,16,128]{3,2,1,0:T(8,128)(2,1)S(1)} collective-permute-done((bf16[32,14,16,128]{3,2,1,0:T(8,128)(2,1)}, bf16[32,14,16,128]{3,2,1,0:T(8,128)(2,1)S(1)}, u32[]{:S(2)}, u32[]{:S(2)}) %collective-permute-start.20) | collective-permute-done | bytes 1835040 | tf_op jit(solution)/shard_map/ppermute | solution.py:426
  132.6 2.0 %add_convert_fusion = bf16[32,14,16,128]{3,2,1,0:T(8,128)(2,1)S(1)} fusion(bf16[32,14,16,128]{3,2,1,0:T(8,128)(2,1)S(1)} %collective-permute-done.20, bf16[32,14,16,128]{3,2,1,0:T(8,128)(2,1)} %get-tuple-element.30), kind=kLoop, calls=%fused_computation.1 | loop fusion | flops 3670016 | bytes 5505024 | tf_op jit(solution)/shard_map/convert_element_type | solution.py:426
  134.6 31.1 %all_to_all.5 = bf16[32,14,16,128]{3,2,1,0:T(8,128)(2,1)S(1)} all-to-all(bf16[32,14,16,128]{3,2,1,0:T(8,128)(2,1)S(1)} %add_convert_fusion), channel_id=1, replica_groups=mesh['space'=4,'chan'=32] {'chan'}, dimensions={0} | all-to-all | bytes 3670016 | tf_op jit(solution)/shard_map/all_to_all | solution.py:427
  166.0 1.6 collective-permute-start.21
  167.7 3.6 %collective-permute-done.21 = f32[14,16,128]{2,1,0:T(8,128)S(1)} collective-permute-done((f32[14,16,128]{2,1,0:T(8,128)S(1)}, f32[14,16,128]{2,1,0:T(8,128)S(1)}, u32[]{:S(2)}, u32[]{:S(2)}) %collective-permute-start.21) | collective-permute-done | bytes 114720 | tf_op jit(solution)/shard_map/ppermute | solution.py:429
  171.3 3.3 %collective-permute-start.22 = (f32[14,16,128]{2,1,0:T(8,128)S(1)}, f32[14,16,128]{2,1,0:T(8,128)S(1)}, u32[]{:S(2)}, u32[]{:S(2)}) collective-permute-start(f32[14,16,128]{2,1,0:T(8,128)S(1)} %add.77), channel_id=1, source_target_pairs={{0,32},{32,0},{64,96},{96,64},{1,33},{33,1},{65,97},{97,65},{2,34}... | collective-permute-start | bytes 344072 | tf_op jit(solution)/shard_map/ppermute | solution.py:430
  174.6 1.0 collective-permute-done.22
  175.6 0.7 fusion
  (54 shorter events, 2.8 us)
Async XLA Ops:
  0.6 50.1 %copy-start.6 = (s32[4,1,32]{2,1,0:T(1,128)S(1)}, s32[4,1,32]{2,1,0:T(1,128)}, u32[]{:S(2)}) copy-start(s32[4,1,32]{2,1,0:T(1,128)} %param.13) | copy-start | bytes 1540
  1.4 1.2 copy-start
  2.7 0.7 copy-start.3
  3.3 47.4 %copy-start.5 = (f32[4,1,32,3,128]{4,2,3,1,0:T(8,128)S(1)}, f32[4,1,32,3,128]{4,2,3,1,0:T(8,128)}, u32[]{:S(2)}) copy-start(f32[4,1,32,3,128]{4,2,3,1,0:T(8,128)} %param.14) | copy-start | bytes 589828
  7.2 61.6 %collective-permute-start.1 = (bf16[1024,256]{1,0:T(8,128)(2,1)}, bf16[1024,256]{1,0:T(8,128)(2,1)S(1)}, u32[]{:S(2)}, u32[]{:S(2)}) collective-permute-start(bf16[1024,256]{1,0:T(8,128)(2,1)} %get-tuple-element.19), channel_id=1, source_target_pairs={{0,64},{32,96},{64,0},{96,32},{1,65},{33,97},{65,1},{97,33},{2,66}... | collective-permute-start | bytes 1572872 | tf_op jit(solution)/shard_map/ppermute | solution.py:375
  11.0 1.2 copy-start.1
  12.2 0.7 copy-start.4
  16.8 49.5 %collective-permute-start = (bf16[1024,256]{1,0:T(8,128)(2,1)}, bf16[1024,256]{1,0:T(8,128)(2,1)S(1)}, u32[]{:S(2)}, u32[]{:S(2)}) collective-permute-start(bf16[1024,256]{1,0:T(8,128)(2,1)} %get-tuple-element.22), channel_id=1, source_target_pairs={{0,32},{32,0},{64,96},{96,64},{1,33},{33,1},{65,97},{97,65},{2,34}... | collective-permute-start | bytes 1572872 | tf_op jit(solution)/shard_map/ppermute | solution.py:379
  17.8 51.2 %collective-permute-start.2 = (bf16[1024,256]{1,0:T(8,128)(2,1)}, bf16[1024,256]{1,0:T(8,128)(2,1)S(1)}, u32[]{:S(2)}, u32[]{:S(2)}) collective-permute-start(bf16[1024,256]{1,0:T(8,128)(2,1)} %get-tuple-element.23), channel_id=1, source_target_pairs={{0,96},{32,64},{64,32},{96,0},{1,97},{33,65},{65,33},{97,1},{2,98}... | collective-permute-start | bytes 1572872 | tf_op jit(solution)/shard_map/ppermute | solution.py:376
  18.6 16.5 %collective-permute-start.9 = (bf16[14,8,256]{2,1,0:T(8,128)(2,1)S(1)}, bf16[14,8,256]{2,1,0:T(8,128)(2,1)S(1)}, u32[]{:S(2)}, u32[]{:S(2)}) collective-permute-start(bf16[14,8,256]{2,1,0:T(8,128)(2,1)S(1)} %get-tuple-element.33), channel_id=1, source_target_pairs={{0,16},{1,17},{2,18},{3,19},{4,20},{5,21},{6,22},{7,23},{8,24},{9,... | collective-permute-start | bytes 172040 | tf_op jit(solution)/shard_map/ppermute | solution.py:386
  35.1 6.5 %collective-permute-start.10 = (bf16[2,14,8,256]{3,2,0,1:T(8,128)(2,1)S(1)}, bf16[2,14,8,256]{3,2,0,1:T(8,128)(2,1)S(1)}, u32[]{:S(2)}, u32[]{:S(2)}) collective-permute-start(bf16[2,14,8,256]{3,2,0,1:T(8,128)(2,1)S(1)} %bitcast_dynamic-update-slice_fusion.12), channel_id=1, source_target_pairs={{0,1},{1,0},{2,3},{3,2},{4,5},{5,4},{6,7},{7,6},{8,9},{9,8},{10,11... | collective-permute-start | bytes 344072 | tf_op jit(solution)/shard_map/ppermute | solution.py:386
  36.8 6.8 %collective-permute-start.11 = (bf16[2,14,8,256]{3,2,0,1:T(8,128)(2,1)S(1)}, bf16[2,14,8,256]{3,2,0,1:T(8,128)(2,1)S(1)}, u32[]{:S(2)}, u32[]{:S(2)}) collective-permute-start(bf16[2,14,8,256]{3,2,0,1:T(8,128)(2,1)S(1)} %bitcast_dynamic-update-slice_fusion.12), channel_id=1, source_target_pairs={{0,2},{1,3},{2,0},{3,1},{4,6},{5,7},{6,4},{7,5},{8,10},{9,11},{10,... | collective-permute-start | bytes 344072 | tf_op jit(solution)/shard_map/ppermute | solution.py:386
  41.6 5.6 %collective-permute-start.12 = (bf16[2,14,8,256]{3,2,0,1:T(8,128)(2,1)S(1)}, bf16[2,14,8,256]{3,2,0,1:T(8,128)(2,1)S(1)}, u32[]{:S(2)}, u32[]{:S(2)}) collective-permute-start(bf16[2,14,8,256]{3,2,0,1:T(8,128)(2,1)S(1)} %bitcast_dynamic-update-slice_fusion.12), channel_id=1, source_target_pairs={{0,3},{1,2},{2,1},{3,0},{4,7},{5,6},{6,5},{7,4},{8,11},{9,10},{10,... | collective-permute-start | bytes 344072 | tf_op jit(solution)/shard_map/ppermute | solution.py:386
  47.9 31.1 %collective-permute-start.13 = (bf16[4,2,14,8,256]{4,3,0,1,2:T(8,128)(2,1)}, bf16[4,2,14,8,256]{4,3,0,1,2:T(8,128)(2,1)}, u32[]{:S(2)}, u32[]{:S(2)}) collective-permute-start(bf16[4,2,14,8,256]{4,3,0,1,2:T(8,128)(2,1)} %bitcast_dynamic-update-slice_fusion.11), channel_id=1, source_target_pairs={{0,32},{32,0},{64,96},{96,64},{1,33},{33,1},{65,97},{97,65},{2,34}... | collective-permute-start | bytes 1376264 | tf_op jit(solution)/shard_map/ppermute | solution.py:396
  50.7 12.7 %copy-start.8 = (bf16[256]{0:T(256)(128)(2,1)S(1)}, bf16[256]{0:T(256)(128)(2,1)}, u32[]{:S(2)}) copy-start(bf16[256]{0:T(256)(128)(2,1)} %param.16) | copy-start | bytes 1540
  63.5 18.1 %collective-permute-start.14 = (bf16[4,2,14,8,256]{4,3,0,1,2:T(8,128)(2,1)}, bf16[4,2,14,8,256]{4,3,0,1,2:T(8,128)(2,1)S(1)}, u32[]{:S(2)}, u32[]{:S(2)}) collective-permute-start(bf16[4,2,14,8,256]{4,3,0,1,2:T(8,128)(2,1)} %bitcast_dynamic-update-slice_fusion.11), channel_id=1, source_target_pairs={{0,4},{1,5},{2,6},{3,7},{4,0},{5,1},{6,2},{7,3},{8,12},{9,13},{10,... | collective-permute-start | bytes 1376264 | tf_op jit(solution)/shard_map/ppermute | solution.py:386
  66.3 21.7 %collective-permute-start.16 = (bf16[4,2,14,8,256]{4,3,0,1,2:T(8,128)(2,1)}, bf16[4,2,14,8,256]{4,3,0,1,2:T(8,128)(2,1)S(1)}, u32[]{:S(2)}, u32[]{:S(2)}) collective-permute-start(bf16[4,2,14,8,256]{4,3,0,1,2:T(8,128)(2,1)} %bitcast_dynamic-update-slice_fusion.11), channel_id=1, source_target_pairs={{0,8},{1,9},{2,10},{3,11},{4,12},{5,13},{6,14},{7,15},{8,0},{9,1},... | collective-permute-start | bytes 1376264 | tf_op jit(solution)/shard_map/ppermute | solution.py:386
  68.8 22.7 %collective-permute-start.18 = (bf16[4,2,14,8,256]{4,3,0,1,2:T(8,128)(2,1)}, bf16[4,2,14,8,256]{4,3,0,1,2:T(8,128)(2,1)S(1)}, u32[]{:S(2)}, u32[]{:S(2)}) collective-permute-start(bf16[4,2,14,8,256]{4,3,0,1,2:T(8,128)(2,1)} %bitcast_dynamic-update-slice_fusion.11), channel_id=1, source_target_pairs={{0,12},{1,13},{2,14},{3,15},{4,8},{5,9},{6,10},{7,11},{8,4},{9,5},... | collective-permute-start | bytes 1376264 | tf_op jit(solution)/shard_map/ppermute | solution.py:386
  78.0 21.1 %copy-start.2 = (bf16[4,4,128,256]{3,2,1,0:T(8,128)(2,1)}, bf16[4,4,128,256]{3,2,1,0:T(8,128)(2,1)S(1)}, u32[]{:S(2)}) copy-start(bf16[4,4,128,256]{3,2,1,0:T(8,128)(2,1)S(1)} %get-tuple-element.24.latent_ref) | copy-start | bytes 3145732
  78.1 3.7 %collective-permute-start.3 = (bf16[1,4,128,256]{3,2,0,1:T(8,128)(2,1)S(1)}, bf16[1,4,128,256]{3,2,0,1:T(8,128)(2,1)S(1)}, u32[]{:S(2)}, u32[]{:S(2)}) collective-permute-start(bf16[1,4,128,256]{3,2,0,1:T(8,128)(2,1)S(1)} %bitcast.97), channel_id=1, source_target_pairs={{0,32},{32,0},{64,96},{96,64},{1,33},{33,1},{65,97},{97,65},{2,34}... | collective-permute-start | bytes 786440 | tf_op jit(solution)/shard_map/ppermute | solution.py:414
  79.0 14.0 %collective-permute-start.4 = (bf16[1,4,128,256]{3,2,0,1:T(8,128)(2,1)S(1)}, bf16[1,4,128,256]{3,2,0,1:T(8,128)(2,1)S(1)}, u32[]{:S(2)}, u32[]{:S(2)}) collective-permute-start(bf16[1,4,128,256]{3,2,0,1:T(8,128)(2,1)S(1)} %bitcast.96), channel_id=1, source_target_pairs={{0,96},{32,64},{64,32},{96,0},{1,97},{33,65},{65,33},{97,1},{2,98}... | collective-permute-start | bytes 786440 | tf_op jit(solution)/shard_map/ppermute | solution.py:413
  81.6 17.8 %collective-permute-start.5 = (bf16[4,1,128,256]{3,2,1,0:T(8,128)(2,1)S(1)}, bf16[4,1,128,256]{3,2,1,0:T(8,128)(2,1)S(1)}, u32[]{:S(2)}, u32[]{:S(2)}) collective-permute-start(bf16[4,1,128,256]{3,2,1,0:T(8,128)(2,1)S(1)} %get-tuple-element.27), channel_id=1, source_target_pairs={{0,1},{1,2},{2,3},{3,4},{4,5},{5,6},{6,7},{7,8},{8,9},{9,10},{10,1... | collective-permute-start | bytes 786440 | tf_op jit(solution)/shard_map/ppermute | solution.py:415
  81.8 11.3 %collective-permute-start.15 = (bf16[4,2,14,8,256]{4,3,0,1,2:T(8,128)(2,1)S(1)}, bf16[4,2,14,8,256]{4,3,0,1,2:T(8,128)(2,1)S(1)}, u32[]{:S(2)}, u32[]{:S(2)}) collective-permute-start(bf16[4,2,14,8,256]{4,3,0,1,2:T(8,128)(2,1)S(1)} %collective-permute-done.14), channel_id=1, source_target_pairs={{0,32},{32,0},{64,96},{96,64},{1,33},{33,1},{65,97},{97,65},{2,34}... | collective-permute-start | bytes 1376264 | tf_op jit(solution)/shard_map/ppermute | solution.py:396
  87.9 11.5 %collective-permute-start.6 = (bf16[4,1,128,256]{3,2,1,0:T(8,128)(2,1)S(1)}, bf16[4,1,128,256]{3,2,1,0:T(8,128)(2,1)S(1)}, u32[]{:S(2)}, u32[]{:S(2)}) collective-permute-start(bf16[4,1,128,256]{3,2,1,0:T(8,128)(2,1)S(1)} %get-tuple-element.28), channel_id=1, source_target_pairs={{1,0},{2,1},{3,2},{4,3},{5,4},{6,5},{7,6},{8,7},{9,8},{10,9},{11,1... | collective-permute-start | bytes 786440 | tf_op jit(solution)/shard_map/ppermute | solution.py:416
  91.5 2.9 %collective-permute-start.17 = (bf16[4,2,14,8,256]{4,3,0,1,2:T(8,128)(2,1)S(1)}, bf16[4,2,14,8,256]{4,3,0,1,2:T(8,128)(2,1)S(1)}, u32[]{:S(2)}, u32[]{:S(2)}) collective-permute-start(bf16[4,2,14,8,256]{4,3,0,1,2:T(8,128)(2,1)S(1)} %collective-permute-done.16), channel_id=1, source_target_pairs={{0,32},{32,0},{64,96},{96,64},{1,33},{33,1},{65,97},{97,65},{2,34}... | collective-permute-start | bytes 1376264 | tf_op jit(solution)/shard_map/ppermute | solution.py:396
  93.0 6.1 %collective-permute-start.19 = (bf16[4,2,14,8,256]{4,3,0,1,2:T(8,128)(2,1)S(1)}, bf16[4,2,14,8,256]{4,3,0,1,2:T(8,128)(2,1)S(1)}, u32[]{:S(2)}, u32[]{:S(2)}) collective-permute-start(bf16[4,2,14,8,256]{4,3,0,1,2:T(8,128)(2,1)S(1)} %collective-permute-done.18), channel_id=1, source_target_pairs={{0,32},{32,0},{64,96},{96,64},{1,33},{33,1},{65,97},{97,65},{2,34}... | collective-permute-start | bytes 1376264 | tf_op jit(solution)/shard_map/ppermute | solution.py:396
  93.1 9.6 %collective-permute-start.7 = (bf16[2,128,256]{2,1,0:T(8,128)(2,1)S(1)}, bf16[2,128,256]{2,1,0:T(8,128)(2,1)S(1)}, u32[]{:S(2)}, u32[]{:S(2)}) collective-permute-start(bf16[2,128,256]{2,1,0:T(8,128)(2,1)S(1)} %get-tuple-element.35), channel_id=1, source_target_pairs={{0,1},{1,2},{2,3},{3,4},{4,5},{5,6},{6,7},{7,8},{8,9},{9,10},{10,1... | collective-permute-start | bytes 393224 | tf_op jit(solution)/shard_map/ppermute | solution.py:418
  94.4 8.2 %collective-permute-start.8 = (bf16[2,128,256]{2,1,0:T(8,128)(2,1)S(1)}, bf16[2,128,256]{2,1,0:T(8,128)(2,1)S(1)}, u32[]{:S(2)}, u32[]{:S(2)}) collective-permute-start(bf16[2,128,256]{2,1,0:T(8,128)(2,1)S(1)} %get-tuple-element.34), channel_id=1, source_target_pairs={{1,0},{2,1},{3,2},{4,3},{5,4},{6,5},{7,6},{8,7},{9,8},{10,9},{11,1... | collective-permute-start | bytes 393224 | tf_op jit(solution)/shard_map/ppermute | solution.py:419
  99.2 3.5 %copy-start.7 = (bf16[2,4,4,2,14,8,256]{6,5,2,1,3,4,0:T(8,128)(2,1)}, bf16[2,4,4,2,14,8,256]{6,5,2,1,3,4,0:T(8,128)(2,1)S(1)}, u32[]{:S(2)}) copy-start(bf16[2,4,4,2,14,8,256]{6,5,2,1,3,4,0:T(8,128)(2,1)S(1)} %bitcast_dynamic-update-slice_fusion.7) | copy-start | bytes 11010052
  128.0 4.6 %collective-permute-start.20 = (bf16[32,14,16,128]{3,2,1,0:T(8,128)(2,1)}, bf16[32,14,16,128]{3,2,1,0:T(8,128)(2,1)S(1)}, u32[]{:S(2)}, u32[]{:S(2)}) collective-permute-start(bf16[32,14,16,128]{3,2,1,0:T(8,128)(2,1)} %get-tuple-element.31), channel_id=1, source_target_pairs={{0,32},{32,0},{64,96},{96,64},{1,33},{33,1},{65,97},{97,65},{2,34}... | collective-permute-start | bytes 5505032 | tf_op jit(solution)/shard_map/ppermute | solution.py:426
  166.0 5.2 %collective-permute-start.21 = (f32[14,16,128]{2,1,0:T(8,128)S(1)}, f32[14,16,128]{2,1,0:T(8,128)S(1)}, u32[]{:S(2)}, u32[]{:S(2)}) collective-permute-start(f32[14,16,128]{2,1,0:T(8,128)S(1)} %convert_reduce_fusion), channel_id=1, source_target_pairs={{0,64},{32,96},{64,0},{96,32},{1,65},{33,97},{65,1},{97,33},{2,66}... | collective-permute-start | bytes 344072 | tf_op jit(solution)/shard_map/ppermute | solution.py:429
  171.3 4.3 %collective-permute-start.22 = (f32[14,16,128]{2,1,0:T(8,128)S(1)}, f32[14,16,128]{2,1,0:T(8,128)S(1)}, u32[]{:S(2)}, u32[]{:S(2)}) collective-permute-start(f32[14,16,128]{2,1,0:T(8,128)S(1)} %add.77), channel_id=1, source_target_pairs={{0,32},{32,0},{64,96},{96,64},{1,33},{33,1},{65,97},{97,65},{2,34}... | collective-permute-start | bytes 344072 | tf_op jit(solution)/shard_map/ppermute | solution.py:430

commit v3 on v2

v3 whole, which is shorter than its diff:
```python
import functools
import math

import jax
import jax.numpy as jnp
from jax import lax
from jax.experimental import pallas as pl
from jax.experimental.pallas import tpu as pltpu
from jax.sharding import PartitionSpec as P

BF = jnp.bfloat16
F32 = jnp.float32
BRIEF = pl.CostEstimate(flops=1, bytes_accessed=1, transcendentals=0)


def send_kernel(scalars_ref, slots_ref, feats_ref, *out_refs):
    points = feats_ref.shape[0]
    point_ids = lax.broadcasted_iota(jnp.int32, (128, points), 1)
    for place, out_ref in enumerate(out_refs):
        owner = scalars_ref[place]
        slots = slots_ref[owner]
        position = lax.broadcasted_iota(
            jnp.int32, slots.shape, 0
        ) * 128 + lax.broadcasted_iota(jnp.int32, slots.shape, 1)
        columns = jnp.where(position < scalars_ref[2 + place], slots, -1).T
        for half in range(2):
            hot = [
                jnp.where(point_ids == columns[:, r : r + 1], 1.0, 0.0).astype(BF)
                for r in range(half * 4, half * 4 + 4)
            ]
            rows = jnp.dot(
                jnp.concatenate(hot, axis=0), feats_ref[...], preferred_element_type=F32
            )
            out_ref[half * 512 : half * 512 + 512, :] = rows.astype(BF)


def gather_listed(feats, slots, scalars):
    capacity = slots.shape[1] * slots.shape[2]
    channels = feats.shape[1]
    whole = pl.BlockSpec(memory_space=pltpu.VMEM)
    return pl.pallas_call(
        send_kernel,
        in_specs=[pl.BlockSpec(memory_space=pltpu.SMEM), whole, whole],
        out_specs=[whole] * 2,
        out_shape=[jax.ShapeDtypeStruct((capacity, channels), BF)] * 2,
        compiler_params=pltpu.CompilerParams(vmem_limit_bytes=16 << 20),
        cost_estimate=BRIEF,
    )(scalars, slots, feats)


def spread_kernel(fill_ref, near_ref, place_ref, t0, t1, out_ref, part_ref, denom_ref, close):
    plane = pl.program_id(0)
    tiles = near_ref.shape[1]
    slots = near_ref.shape[2]
    groups = (out_ref.shape[1] + close.shape[1]) // 256
    split = close.shape[1]
    capacity = t0.shape[0]
    cell = lax.broadcasted_iota(jnp.int32, (16, slots), 0)
    centre_x = (cell // 4).astype(F32) - 1.5
    centre_y = (cell % 4).astype(F32) - 1.5
    lane = lax.broadcasted_iota(jnp.int32, (16, slots), 1)
    low_ids = lax.broadcasted_iota(jnp.int32, (256, slots), 0)

    def one_tile(tile, carry):
        near = near_ref[0, pl.ds(tile, 1), :]
        along_x = place_ref[0, 0, pl.ds(tile, 1), :] - centre_x
        along_y = place_ref[0, 1, pl.ds(tile, 1), :] - centre_y
        along_z = place_ref[0, 2, pl.ds(tile, 1), :]
        values = jnp.exp(-0.5 * (along_x * along_x + along_y * along_y + along_z * along_z))
        values = jnp.where(lane < fill_ref[plane, tile], values, 0.0)
        start = pl.multiple_of(tile * 16, 16)
        denom_ref[pl.ds(start, 16), :] = jnp.broadcast_to(
            1.0 + jnp.sum(values, axis=1, keepdims=True), (16, 128)
        )
        half = values.astype(BF).astype(F32)
        high = jnp.broadcast_to(near >> 8, (16, slots))
        low = near & 255
        stacked = jnp.concatenate(
            [jnp.where(high == g, half, 0.0).astype(BF) for g in range(groups)], axis=0
        )
        hot = jnp.where(low_ids == low, 1.0, 0.0).astype(BF)
        block = lax.dot_general(
            stacked, hot, (((1,), (1,)), ((), ())), preferred_element_type=F32
        ).astype(BF)
        for g in range(groups):
            rows = block[g * 16 : g * 16 + 16, :]
            if g * 256 < split:
                close[pl.ds(start, 16), g * 256 : g * 256 + 256] = rows
            else:
                out_ref[pl.ds(start, 16), g * 256 - split : g * 256 - split + 256] = rows
        return carry

    lax.fori_loop(0, tiles, one_tile, 0, unroll=4)
    part_ref[...] = jnp.dot(
        close[:, :capacity], t0[...], preferred_element_type=F32
    ) + jnp.dot(close[:, capacity:], t1[...], preferred_element_type=F32)


def spread_weights(near, fill, place, tables):
    planes, tiles, slots = near.shape
    capacity, channels = tables[0].shape
    rows = 2 * capacity
    return pl.pallas_call(
        spread_kernel,
        grid=(planes,),
        in_specs=[
            pl.BlockSpec(memory_space=pltpu.SMEM),
            pl.BlockSpec((1, tiles, slots), lambda z: (z, 0, 0)),
            pl.BlockSpec((1, 3, tiles, slots), lambda z: (z, 0, 0, 0)),
        ]
        + [pl.BlockSpec((capacity, channels), lambda z: (0, 0))] * 2,
        out_specs=[
            pl.BlockSpec((tiles * 16, rows), lambda z: (z, 0)),
            pl.BlockSpec((tiles * 16, channels), lambda z: (z, 0)),
            pl.BlockSpec((tiles * 16, 128), lambda z: (z, 0)),
        ],
        out_shape=[
            jax.ShapeDtypeStruct((planes * tiles * 16, rows), BF),
            jax.ShapeDtypeStruct((planes * tiles * 16, channels), F32),
            jax.ShapeDtypeStruct((planes * tiles * 16, 128), F32),
        ],
        scratch_shapes=[pltpu.VMEM((tiles * 16, rows), BF)],
        compiler_params=pltpu.CompilerParams(vmem_limit_bytes=16 << 20),
    )(fill, near, place, *tables)


def latent_kernel(
    flags_ref, spread_ref, part_ref, denom_ref, t0, t1,
    out_ref, near_ref, far_ref, first_ref, second_ref, total, order,
):
    plane = pl.program_id(0)
    last = pl.num_programs(0) - 1
    core = flags_ref[0]
    odd = flags_ref[2]
    capacity, channels = t0.shape
    cells = spread_ref.shape[0]
    tiles = cells // 16
    summed = part_ref[...]
    for place, table in ((0, t0), (1, t1)):
        summed = summed + jnp.dot(
            spread_ref[:, place * capacity : (place + 1) * capacity],
            table[...],
            preferred_element_type=F32,
        )
    for lanes in range(0, channels, 128):
        part = slice(lanes, lanes + 128)
        total[...] = summed[:, part] / denom_ref[...]
        for u in range(4):
            for v in range(4):
                order[pl.ds(v, tiles, stride=4), :] = total[
                    pl.ds(u * 4 + v, tiles, stride=16), :
                ]
            out_ref[0, u, :, part] = order[...].astype(BF)
    first_ref[0, 0] = out_ref[0, 3 * (1 - odd)]
    second_ref[0, 0] = out_ref[0, 3 * odd]

    @pl.when(plane == (1 - core) * last)
    def _():
        near_ref[...] = out_ref[...]

    @pl.when(plane == core * last)
    def _():
        far_ref[...] = out_ref[...]


def latent_block(flags, spread, part, denom, tables):
    cells = spread.shape[0]
    planes = 4
    per_plane = cells // planes
    capacity, channels = tables[0].shape
    width = per_plane // 4
    whole = pl.BlockSpec((capacity, channels), lambda z: (0, 0))
    plane_spec = pl.BlockSpec((1, 4, width, channels), lambda z: (0, 0, 0, 0))
    row_spec = pl.BlockSpec((1, 1, width, channels), lambda z: (z, 0, 0, 0))
    return pl.pallas_call(
        latent_kernel,
        grid=(planes,),
        in_specs=[
            pl.BlockSpec(memory_space=pltpu.SMEM),
            pl.BlockSpec((per_plane, spread.shape[1]), lambda z: (z, 0)),
            pl.BlockSpec((per_plane, channels), lambda z: (z, 0)),
            pl.BlockSpec((per_plane, 128), lambda z: (z, 0)),
        ]
        + [whole] * 2,
        out_specs=[
            pl.BlockSpec((1, 4, width, channels), lambda z: (z, 0, 0, 0)),
            plane_spec,
            plane_spec,
            row_spec,
            row_spec,
        ],
        out_shape=[
            jax.ShapeDtypeStruct((planes, 4, width, channels), BF),
            jax.ShapeDtypeStruct((1, 4, width, channels), BF),
            jax.ShapeDtypeStruct((1, 4, width, channels), BF),
            jax.ShapeDtypeStruct((planes, 1, width, channels), BF),
            jax.ShapeDtypeStruct((planes, 1, width, channels), BF),
        ],
        scratch_shapes=[
            pltpu.VMEM((per_plane, 128), F32),
            pltpu.VMEM((width, 128), F32),
        ],
        compiler_params=pltpu.CompilerParams(vmem_limit_bytes=20 << 20),
    )(flags, spread, part, denom, *tables)


def with_shifts(taps_ref, start, width, channels, y_ids):
    rows = pl.ds(start, width)
    low = pltpu.roll(taps_ref[rows, 0:channels], 1, 0)
    high = pltpu.roll(taps_ref[rows, 2 * channels :], width - 1, 0)
    return (
        jnp.where(y_ids == 0, 0.0, low)
        + taps_ref[rows, channels : 2 * channels]
        + jnp.where(y_ids == width - 1, 0.0, high)
    )


def times_weight(taps_ref, pieces, weight_ref, positions, channels):
    patch = jnp.concatenate(pieces, axis=1)
    for dy in range(3):
        matrix = jnp.concatenate([weight_ref[p + dy] for p in positions], axis=0)
        taps_ref[:, dy * channels : (dy + 1) * channels] = jnp.dot(
            patch, matrix, preferred_element_type=F32
        )


def inner_kernel(chosen, latent_ref, weight_ref, part_ref, padded, taps):
    planes, rows_x, width, channels = latent_ref.shape
    flat = rows_x * width
    none = jnp.zeros((planes, width, channels), BF)
    padded[:, 0] = none
    padded[:, 1 : rows_x + 1] = latent_ref[...]
    padded[:, rows_x + 1] = none
    y_ids = lax.broadcasted_iota(jnp.int32, (width, channels), 0)
    for place, z in enumerate(chosen):
        reach = [(dz, dx) for dz in range(3) if 0 <= z + dz - 1 < planes for dx in range(3)]
        pieces = [
            padded[z + dz - 1, dx : dx + rows_x].reshape(flat, channels) for dz, dx in reach
        ]
        times_weight(
            taps, pieces, weight_ref, [9 * dz + 3 * dx for dz, dx in reach], channels
        )
        for x in range(rows_x):
            part_ref[place, x] = with_shifts(taps, x * width, width, channels, y_ids)


def inner_conv(chosen, latent, weight):
    planes, rows_x, width, channels = latent.shape
    whole = pl.BlockSpec(memory_space=pltpu.VMEM)
    return pl.pallas_call(
        functools.partial(inner_kernel, chosen),
        in_specs=[whole] * 2,
        out_specs=whole,
        out_shape=jax.ShapeDtypeStruct((len(chosen), rows_x, width, channels), F32),
        scratch_shapes=[
            pltpu.VMEM((planes, rows_x + 2, width, channels), BF),
            pltpu.VMEM((rows_x * width, 3 * channels), F32),
        ],
        compiler_params=pltpu.CompilerParams(vmem_limit_bytes=20 << 20),
        cost_estimate=BRIEF,
    )(latent, weight)


def grad_taps(first, count, core, turned, shifted, keep_ref, give_ref, width):
    planes = turned.shape[0] - 2
    channels = turned.shape[1]
    flat = shifted.shape[0] // planes
    half_size = keep_ref.shape[1]

    def one_tap(index, carry):
        tap = first + index
        dz = tap // 3
        start = pl.multiple_of((tap % 3) * width, width)
        pieces = [turned[z + dz, :, pl.ds(start, flat)] for z in range(planes)]
        sums = jnp.dot(
            jnp.concatenate(pieces, axis=1), shifted[...], preferred_element_type=F32
        )
        for dy in range(3):
            part = sums[:, dy * channels : (dy + 1) * channels]
            both = jnp.concatenate(
                [
                    part[:, :128].reshape(channels // 8, 8, 128),
                    part[:, 128:].reshape(channels // 8, 8, 128),
                ],
                axis=1,
            )
            position = index * 3 + dy
            half = position // half_size
            slot = position - half * half_size
            rounded = both.astype(BF)

            @pl.when(half == core)
            def _():
                keep_ref[:, slot] = rounded

            @pl.when(half != core)
            def _():
                give_ref[:, slot] = rounded

        return carry

    lax.fori_loop(0, count, one_tap, 0)
    if 3 * count < 2 * half_size:
        unused = jnp.zeros((channels // 8, 16, 128), BF)

        @pl.when(core == 1)
        def _():
            keep_ref[:, half_size - 1] = unused

        @pl.when(core == 0)
        def _():
            give_ref[:, half_size - 1] = unused


def outer_kernel(
    flags_ref, middle_ref, edge_ref, latent_ref, near_ref, far_ref, first_ref, second_ref,
    first_end_ref, second_end_ref, weight_ref, bias_ref, cotangent_ref,
    act_ref, turned, shifted, keep_ref, give_ref,
    padded, rims, side_x, side_z,
):
    planes, rows_x, width, channels = latent_ref.shape
    flat = rows_x * width
    core = flags_ref[0]
    has_far = flags_ref[1] > 0
    odd = flags_ref[2]
    has_second = flags_ref[3] > 0
    near_z = (1 - core) * (planes + 1)
    far_z = core * (planes + 1)
    first_x = (1 - odd) * (rows_x + 1)
    second_x = odd * (rows_x + 1)
    none = jnp.zeros((), BF)
    padded[1 : planes + 1, 1 : rows_x + 1] = latent_ref[...]
    padded[near_z, 1 : rows_x + 1] = near_ref[0]
    padded[far_z, 1 : rows_x + 1] = jnp.where(has_far, far_ref[0], none)
    for x, face_ref, end_ref, present in (
        (first_x, first_ref, first_end_ref, True),
        (second_x, second_ref, second_end_ref, has_second),
    ):
        padded[1 : planes + 1, x] = jnp.where(present, face_ref[:, 0], none)
        padded[near_z, x] = jnp.where(present, end_ref[0], none)
        padded[far_z, x] = jnp.where(jnp.logical_and(present, has_far), end_ref[1], none)
    blank = jnp.zeros((width, channels), BF)
    for side in range(2):
        rims[side, 0] = blank
        rims[side, 1 : rows_x + 1] = padded[side * (planes + 1), 1 : rows_x + 1]
        rims[side, rows_x + 1] = blank
    y_ids = lax.broadcasted_iota(jnp.int32, (width, channels), 0)
    root = math.sqrt(2.0 / math.pi)

    def turn(z, carry):
        turned[z] = padded[z].reshape((rows_x + 2) * width, channels).T
        return carry

    lax.fori_loop(0, planes + 2, turn, 0)

    for side in range(2):
        column = side * (rows_x + 1)
        times_weight(
            side_x.at[side],
            [padded[dz : dz + planes, column].reshape(planes * width, channels) for dz in range(3)],
            weight_ref,
            [9 * dz + 6 * side for dz in range(3)],
            channels,
        )
        times_weight(
            side_z.at[side],
            [rims[side, dx : dx + rows_x].reshape(flat, channels) for dx in range(3)],
            weight_ref,
            [18 * side + 3 * dx for dx in range(3)],
            channels,
        )
    for z in range(planes):
        for x in range(rows_x):
            inner_part = edge_ref[int(z > 0), x] if z in (0, planes - 1) else middle_ref[z - 1, x]
            pre = inner_part + bias_ref[...]
            if x in (0, rows_x - 1):
                pre = pre + with_shifts(
                    side_x.at[int(x > 0)], z * width, width, channels, y_ids
                )
            if z in (0, planes - 1):
                pre = pre + with_shifts(
                    side_z.at[int(z > 0)], x * width, width, channels, y_ids
                )
            square = pre * pre
            inner = root * (pre + 0.044715 * (square * pre))
            bent = jnp.tanh(inner)
            gate = 0.5 * (1.0 + bent)
            act_ref[z, x] = (pre * gate).astype(BF)
            slope = gate + 0.5 * pre * (1.0 - bent * bent) * (
                root * (1.0 + 3.0 * 0.044715 * square)
            )
            grad = (cotangent_ref[z, x].astype(F32) * slope).astype(BF).astype(F32)
            rows = pl.ds(z * flat + x * width, width)
            shifted[rows, 0:channels] = jnp.where(
                y_ids == width - 1, 0.0, pltpu.roll(grad, width - 1, 0)
            ).astype(BF)
            shifted[rows, channels : 2 * channels] = grad.astype(BF)
            shifted[rows, 2 * channels :] = jnp.where(
                y_ids == 0, 0.0, pltpu.roll(grad, 1, 0)
            ).astype(BF)
    grad_taps(0, 5, core, turned, shifted, keep_ref, give_ref, width)


def outer_conv(flags, parts, latent, near, far, faces, weight, bias, cotangent):
    planes, rows_x, width, channels = latent.shape
    flat = rows_x * width
    whole = pl.BlockSpec(memory_space=pltpu.VMEM)
    half_terms = jax.ShapeDtypeStruct((channels // 8, 8, 16, 128), BF)
    return pl.pallas_call(
        outer_kernel,
        in_specs=[pl.BlockSpec(memory_space=pltpu.SMEM)] + [whole] * 12,
        out_specs=[whole] * 5,
        out_shape=[
            jax.ShapeDtypeStruct(latent.shape, BF),
            jax.ShapeDtypeStruct((planes + 2, channels, (rows_x + 2) * width), BF),
            jax.ShapeDtypeStruct((planes * flat, 3 * channels), BF),
            half_terms,
            half_terms,
        ],
        scratch_shapes=[
            pltpu.VMEM((planes + 2, rows_x + 2, width, channels), BF),
            pltpu.VMEM((2, rows_x + 2, width, channels), BF),
            pltpu.VMEM((2, planes * width, 3 * channels), F32),
            pltpu.VMEM((2, flat, 3 * channels), F32),
        ],
        compiler_params=pltpu.CompilerParams(vmem_limit_bytes=32 << 20),
    )(flags, *parts, latent, near, far, *faces, weight, bias, cotangent)


def rest_kernel(flags_ref, turned, shifted, keep_ref, give_ref):
    width = turned.shape[2] // 6
    grad_taps(5, 4, flags_ref[0], turned, shifted, keep_ref, give_ref, width)


def rest_terms(flags, turned, shifted):
    channels = turned.shape[1]
    whole = pl.BlockSpec(memory_space=pltpu.VMEM)
    half_terms = jax.ShapeDtypeStruct((channels // 8, 6, 16, 128), BF)
    return pl.pallas_call(
        rest_kernel,
        in_specs=[pl.BlockSpec(memory_space=pltpu.SMEM)] + [whole] * 2,
        out_specs=[whole] * 2,
        out_shape=[half_terms] * 2,
        compiler_params=pltpu.CompilerParams(vmem_limit_bytes=20 << 20),
    )(flags, turned, shifted)


def pair_sum(keep, give, swap):
    paired = keep.astype(F32) + lax.ppermute(give, "space", swap).astype(F32)
    return paired.astype(BF).reshape((2, 4, 4) + keep.shape[1:])


def sum_over(block, step, count, dim):
    chans = lax.axis_size("chan")
    index = lax.rem(lax.axis_index("chan") // step, count)
    total = lax.dynamic_index_in_dim(block, index, dim, keepdims=False).astype(F32)
    for offset in range(1, count):
        part = lax.dynamic_index_in_dim(block, index ^ offset, dim, keepdims=False)
        total = total + lax.ppermute(
            part, "chan", [(i, i ^ (offset * step)) for i in range(chans)]
        ).astype(F32)
    return total


def chan_pieces(array, step, count):
    chans = lax.axis_size("chan")
    return [array] + [
        lax.ppermute(array, "chan", [(i, i ^ (offset * step)) for i in range(chans)])
        for offset in range(1, count)
    ]


def in_place(index, pieces):
    result = jnp.zeros((len(pieces),) + pieces[0].shape, BF)
    for offset, piece in enumerate(pieces):
        result = lax.dynamic_update_index_in_dim(result, piece, index ^ offset, 0)
    return result


def in_order(core, own, other):
    low = jnp.where(core == 0, own, other)
    high = jnp.where(core == 0, other, own)
    return low, high


def on_device(
    point_feats,
    send_slots,
    send_counts,
    neighbors,
    tile_fill,
    offsets,
    weight,
    conv_bias,
    cotangent,
):
    spaces = lax.axis_size("space")
    chans = lax.axis_size("chan")
    planes, rows_x, width_y, channels = cotangent.shape
    row_count = weight.shape[0]
    space = lax.axis_index("space")
    chan = lax.axis_index("chan")
    core = lax.rem(space, 2)
    swap = [(i, i ^ 1) for i in range(spaces)]
    far = [(i, i ^ 2) for i in range(spaces)]
    cross = [(i, i ^ 3) for i in range(spaces)]
    first_pairs = [(i, i ^ 1) for i in range(chans)]
    second_pairs = [(i, (i - 1 + 2 * (i % 2)) % chans) for i in range(chans)]
    flags = jnp.stack(
        [
            core,
            jnp.logical_or(space == 1, space == 2).astype(jnp.int32),
            lax.rem(chan, 2),
            jnp.logical_and(chan > 0, chan < chans - 1).astype(jnp.int32),
        ]
    )

    taps = jnp.pad(weight.transpose(1, 0, 2), ((0, 1), (0, 0), (0, 0)))
    gathered = lax.dynamic_slice_in_dim(taps, core * 14, 14, 0)
    gathered = in_place(chan // 16, chan_pieces(gathered, 16, 2))

    slots, counts = send_slots[0, 0], send_counts[0, 0]
    capacity = slots.shape[1]
    slots = slots.reshape(spaces, capacity // 128, 128)
    owners = space ^ jnp.arange(spaces, dtype=jnp.int32)
    scalars = jnp.concatenate([owners.reshape(2, 2), counts[owners].reshape(2, 2)], axis=1)
    to_far, to_cross = gather_listed(point_feats, slots, scalars[1])
    to_far, to_cross, gathered = lax.optimization_barrier((to_far, to_cross, gathered))
    from_far = lax.ppermute(to_far, "space", far)
    from_cross = lax.ppermute(to_cross, "space", cross)
    gathered = jnp.broadcast_to(gathered[None], (16,) + gathered.shape)
    gathered = lax.all_to_all(
        gathered,
        "chan",
        split_axis=0,
        concat_axis=0,
        axis_index_groups=[[16 * y + i for i in range(16)] for y in range(chans // 16)],
        tiled=True,
    )
    held_scalars, _ = lax.optimization_barrier((scalars[0], to_far))
    to_self, to_other = gather_listed(point_feats, slots, held_scalars)
    from_other = lax.ppermute(to_other, "space", swap)

    near, _ = lax.optimization_barrier((neighbors[:, 0], to_self))
    spread, close_part, denom = spread_weights(
        near ^ (space * capacity),
        tile_fill[:, 0],
        offsets[:, 0].transpose(0, 2, 1, 3),
        (to_self, from_other),
    )

    latent, near_plane, far_plane, first_row, second_row = latent_block(
        flags, spread, close_part, denom, (from_far, from_cross)
    )

    far_rim = lax.ppermute(far_plane, "space", cross)
    near_rim = lax.ppermute(near_plane, "space", swap)
    gathered, _ = lax.optimization_barrier((gathered, near_plane))
    gathered = jnp.stack(in_order(core, gathered, lax.ppermute(gathered, "space", swap)))
    full_weight = gathered.transpose(0, 3, 2, 1, 4, 5).reshape(28, channels, channels)
    faces = [
        lax.ppermute(first_row, "chan", first_pairs),
        lax.ppermute(second_row, "chan", second_pairs),
    ]
    middle = inner_conv((1, 2), latent, full_weight)
    far_rim, near_rim, middle = lax.optimization_barrier((far_rim, near_rim, middle))
    odd = lax.rem(chan, 2)
    corners = []
    for side, pairs in ((1 - odd, first_pairs), (odd, second_pairs)):
        ends = [
            lax.dynamic_index_in_dim(rim, (rows_x - 1) * side, 1, keepdims=False)
            for rim in (near_rim, far_rim)
        ]
        ends = jnp.concatenate(ends, axis=0)
        corners.append(lax.ppermute(ends, "chan", pairs))
        held_latent = lax.optimization_barrier((latent, ends))[0]
    edge = inner_conv((0, 3), held_latent, full_weight)

    activated, turned, shifted, keep, give = outer_conv(
        flags, (middle, edge), latent, near_rim, far_rim, (*faces, *corners),
        full_weight, conv_bias.astype(F32)[None], cotangent,
    )
    early = pair_sum(keep, give, swap)
    held_flags, early = lax.optimization_barrier((flags, early))
    late = pair_sum(*rest_terms(held_flags, turned, shifted), swap)
    early = sum_over(early, 1, 4, 2).astype(BF)
    late = sum_over(late, 4, 4, 1).astype(BF)
    early = sum_over(early, 4, 4, 1)
    late = sum_over(late, 1, 4, 1)
    summed = sum_over(jnp.concatenate([early, late], axis=1), 16, 2, 0)
    own_sum = summed + lax.ppermute(summed, "space", far)
    low_sum, high_sum = in_order(core, own_sum, lax.ppermute(own_sum, "space", swap))
    total = jnp.concatenate([low_sum[:8], high_sum[:7], low_sum[8:], high_sum[8:]], axis=0)
    total = total.reshape(27, 2, row_count, channels // 2).transpose(2, 0, 1, 3)
    scaling = 1.0 / math.sqrt(planes * spaces * rows_x * chans * width_y)
    return (activated, total.reshape(row_count, 27, channels) * scaling)


def solution(mesh):
    return jax.shard_map(
        on_device,
        mesh=mesh,
        in_specs=(
            P(("space", "chan"), None),
            P("space", "chan", None, None),
            P("space", "chan", None),
            P("space", "chan", None, None),
            P("space", "chan", None),
            P("space", "chan", None, None, None),
            P("chan", None, None),
            P(),
            P("space", "chan", None, None),
        ),
        out_specs=(P("space", "chan", None, None), P("chan", None, None)),
        check_vma=False,
    )
```

time: 177 us -> 147 us (0.83)
  blocking collectives: 31.1 us -> 0 us
  starting transfers between devices: 36.2 us -> 49.4 us
  Pallas kernels: 55 us -> 48.7 us
  local copies, waits for them, and re-layouts: 11.8 us -> 5.73 us
    all_to_all x1 -> x0, blocking collectives: 31.1 us -> none  [on_device(): lax.all_to_all(paired, 'chan', split_axis=0, concat_axis=0, tiled=True)]
    ppermute x16 -> x21, waiting for transfers between devices: 32.8 us -> 21.7 us  [the longest x13 15.8 us: sum_over(): lax.ppermute(part, 'chan', [(i, i ^ offset * step) for i in range(chans)])]
    ppermute x1, waiting for transfers between devices: 0.01 us -> 9.8 us  [on_device(): from_cross = lax.ppermute(to_cross, 'space', cross)]
    all_to_all x0 -> x1, starting transfers between devices: none -> 7.79 us  [on_device(): lax.all_to_all(gathered, 'chan', split_axis=0, concat_axis=0, axis_index_...]
    dynamic_update_slice x14 -> x2, local copies, waits for them, and re-layouts: 5.88 us -> 0.84 us  [in_place(): result = lax.dynamic_update_index_in_dim(result, piece, index ^ offset, 0)]
    pallas_call x1, Pallas kernels: 9.04 us -> 4.45 us  [latent_block(): pl.pallas_call(latent_kernel, grid=(planes,), in_specs=[pl.BlockSpec(memo...]
    ppermute x16 -> x21, starting transfers between devices: 24.1 us -> 27.1 us  [the longest x13 15 us: sum_over(): lax.ppermute(part, 'chan', [(i, i ^ offset * step) for i in range(chans)])]
    ppermute x1, starting transfers between devices: 3.32 us -> 5.97 us  [on_device(): lax.ppermute(own_sum, 'space', swap)]
  transfers between devices with their start and end apart: 23 -> 29, of which waited for: 11 -> 11; matrix products, arithmetic and copies ran while one was open for 5% -> 4% of each run, Pallas kernels for 15% -> 21%
where the time goes in v3:
time: 147 us
  starting transfers between devices  49.4 us (34%)
  Pallas kernels  48.7 us (33%)
  waiting for transfers between devices  37.5 us (26%)
  local copies, waits for them, and re-layouts  5.73 us (4%)
  other arithmetic  4.51 us (3%)
    ppermute x13, waiting for transfers between devices, sum_over(): lax.ppermute(part, 'chan', [(i, i ^ offset * step) for i in range(chans)])  15.8 us
    ppermute x13, starting transfers between devices, sum_over(): lax.ppermute(part, 'chan', [(i, i ^ offset * step) for i in range(chans)])  15 us
    pallas_call x1, Pallas kernels, spread_weights(): pl.pallas_call(spread_kernel, grid=(planes,), in_specs=[pl.BlockSpec(memo...  13.5 us
    pallas_call x1, Pallas kernels, outer_conv(): pl.pallas_call(outer_kernel, in_specs=[pl.BlockSpec(memory_space=pltpu.SM...  12.4 us
    ppermute x1, waiting for transfers between devices, on_device(): from_cross = lax.ppermute(to_cross, 'space', cross)  9.8 us
    all_to_all x1, starting transfers between devices, on_device(): lax.all_to_all(gathered, 'chan', split_axis=0, concat_axis=0, axis_index_...  7.79 us
    pallas_call x2, Pallas kernels, gather_listed(): pl.pallas_call(send_kernel, in_specs=[pl.BlockSpec(memory_space=pltpu.SME...  7.01 us
    pallas_call x2, Pallas kernels, inner_conv(): pl.pallas_call(functools.partial(inner_kernel, chosen), in_specs=[whole]...  6.47 us
  transfers between devices with their start and end apart: 29, of which 11 were waited for; matrix products, arithmetic and copies ran while one was open for 4% of the time, Pallas kernels for 21%

profile of v3, /device:TPU:1, one launch (start us, length us, event | category | flops | bytes accessed | tf_op | source)
XLA Modules:
  0.0 147.0 jit_solution(16117633950888968077)
XLA Ops:
  0.7 0.8 bitcast_dynamic-update-slice_fusion.1
  1.5 2.2 %collective-permute-start = (bf16[14,8,256]{2,1,0:T(8,128)(2,1)S(1)}, bf16[14,8,256]{2,1,0:T(8,128)(2,1)S(1)}, u32[]{:S(2)}, u32[]{:S(2)}) collective-permute-start(bf16[14,8,256]{2,1,0:T(8,128)(2,1)S(1)} %get-tuple-element.65), channel_id=1, source_target_pairs={{0,16},{1,17},{2,18},{3,19},{4,20},{5,21},{6,22},{7,23},{8,24},{9,... | collective-permute-start | bytes 172040 | tf_op jit(solution)/shard_map/ppermute | solution.py:468
  3.8 0.6 gather_fusion
  4.6 0.7 copy.19
  5.3 1.2 copy-done.1
  6.5 3.1 %shard_map.104 = (bf16[1024,256]{1,0:T(8,128)(2,1)}, bf16[1024,256]{1,0:T(8,128)(2,1)S(1)}) custom-call(s32[4]{0:T(128)S(1)} %get-tuple-element.86.scalars_ref, s32[4,8,128]{2,1,0:T(8,128)S(1)} %bitcast.99, bf16[2048,256]{1,0:T(8,128)(2,1)S(1)} %copy-done.1), custom_call_target="tpu_custom_call" | custom-call | flops 1 | bytes 1 | tf_op jit(solution)/shard_map/pallas_call | solution.py:41
  9.7 1.4 broadcast_in_dim.25
  11.1 7.8 %all-to-all-start = ((bf16[16,2,14,8,256]{4,3,1,2,0:T(8,128)(2,1)}), bf16[16,2,14,8,256]{4,3,1,2,0:T(8,128)(2,1)}, u32[]{:S(2)}, u32[]{:S(2)}) async-start(bf16[16,2,14,8,256]{4,3,1,2,0:T(8,128)(2,1)} %broadcast_in_dim.25), calls=%async_computation | async-start | bytes 3670016 | tf_op jit(solution)/shard_map/all_to_all | solution.py:532
  18.9 3.9 %shard_map.105 = (bf16[1024,256]{1,0:T(8,128)(2,1)S(1)}, bf16[1024,256]{1,0:T(8,128)(2,1)}) custom-call(s32[4]{0:T(128)S(1)} %get-tuple-element.36.scalars_ref, s32[4,8,128]{2,1,0:T(8,128)S(1)} %bitcast.100, bf16[2048,256]{1,0:T(8,128)(2,1)S(1)} %copy-done.2), custom_call_target="tpu_custom_call" | custom-call | flops 1 | bytes 1 | tf_op jit(solution)/shard_map/pallas_call | solution.py:41
  22.8 1.2 collective-permute-start.1
  24.0 2.6 %collective-permute-start.2 = (bf16[1024,256]{1,0:T(8,128)(2,1)}, bf16[1024,256]{1,0:T(8,128)(2,1)S(1)}, u32[]{:S(2)}, u32[]{:S(2)}) collective-permute-start(bf16[1024,256]{1,0:T(8,128)(2,1)} %get-tuple-element.35), channel_id=1, source_target_pairs={{0,64},{32,96},{64,0},{96,32},{1,65},{33,97},{65,1},{97,33},{2,66}... | collective-permute-start | bytes 1572872 | tf_op jit(solution)/shard_map/ppermute | solution.py:529
  26.7 0.5 collective-permute-start.3
  27.3 13.5 %shard_map.106 = (bf16[2048,2048]{1,0:T(8,128)(2,1)S(1)}, f32[2048,256]{1,0:T(8,128)S(1)}, f32[2048,128]{1,0:T(8,128)S(1)}) custom-call(s32[4,32]{1,0:T(4,128)S(1)} %bitcast.101, s32[4,32,128]{2,1,0:T(8,128)S(1)} %broadcast_xor_fusion.near_ref, f32[4,3,32,128]{3,2,1,0:T(8,128)S(1)} %bitcast.98, bf16[1024,256]{1,0:T(8,128)(2,1)S(1)} %get-tuple-element.37.t0, ...), custom_call_target="tpu_custom_call" | custom-call | tf_op jit(solution)/shard_map/pallas_call | solution.py:103
  40.8 9.8 %collective-permute-done.3.t1 = bf16[1024,256]{1,0:T(8,128)(2,1)S(1)} collective-permute-done((bf16[1024,256]{1,0:T(8,128)(2,1)S(1)}, bf16[1024,256]{1,0:T(8,128)(2,1)S(1)}, u32[]{:S(2)}, u32[]{:S(2)}) %collective-permute-start.3) | collective-permute-done | bytes 524320 | tf_op jit(solution)/shard_map/ppermute | solution.py:530
  50.6 4.5 %shard_map.107 = (bf16[4,4,128,256]{3,2,1,0:T(8,128)(2,1)S(1)}, bf16[1,4,128,256]{3,2,1,0:T(8,128)(2,1)S(1)}, bf16[1,4,128,256]{3,2,1,0:T(8,128)(2,1)S(1)}, bf16...) custom-call(s32[4]{0:T(128)S(1)} %pad_add_fusion.1.flags_ref, ...), custom_call_target="tpu_custom_call" | custom-call | tf_op jit(solution)/shard_map/pallas_call | solution.py:175
  55.7 2.8 %collective-permute-start.4 = (bf16[1,4,128,256]{3,2,1,0:T(8,128)(2,1)S(1)}, bf16[1,4,128,256]{3,2,1,0:T(8,128)(2,1)S(1)}, u32[]{:S(2)}, u32[]{:S(2)}) collective-permute-start(bf16[1,4,128,256]{3,2,1,0:T(8,128)(2,1)S(1)} %get-tuple-element.44), channel_id=1, source_target_pairs={{0,96},{32,64},{64,32},{96,0},{1,97},{33,65},{65,33},{97,1},{2,98}... | collective-permute-start | bytes 786440 | tf_op jit(solution)/shard_map/ppermute | solution.py:556
  58.5 1.6 %collective-permute-start.7 = (bf16[4,1,128,256]{3,2,1,0:T(8,128)(2,1)S(1)}, bf16[4,1,128,256]{3,2,1,0:T(8,128)(2,1)S(1)}, u32[]{:S(2)}, u32[]{:S(2)}) collective-permute-start(bf16[4,1,128,256]{3,2,1,0:T(8,128)(2,1)S(1)} %get-tuple-element.53), channel_id=1, source_target_pairs={{0,1},{1,0},{2,3},{3,2},{4,5},{5,4},{6,7},{7,6},{8,9},{9,8},{10,11... | collective-permute-start | bytes 786440 | tf_op jit(solution)/shard_map/ppermute | solution.py:562
  60.1 3.5 %collective-permute-start.8 = (bf16[4,1,128,256]{3,2,1,0:T(8,128)(2,1)S(1)}, bf16[4,1,128,256]{3,2,1,0:T(8,128)(2,1)S(1)}, u32[]{:S(2)}, u32[]{:S(2)}) collective-permute-start(bf16[4,1,128,256]{3,2,1,0:T(8,128)(2,1)S(1)} %get-tuple-element.54), channel_id=1, source_target_pairs={{0,31},{1,2},{2,1},{3,4},{4,3},{5,6},{6,5},{7,8},{8,7},{9,10},{10,... | collective-permute-start | bytes 786440 | tf_op jit(solution)/shard_map/ppermute | solution.py:563
  63.6 2.3 %select_bitcast_fusion.1 = (bf16[1,16,2,14,8,256]{5,4,2,3,1,0:T(8,128)(2,1)S(1)}, bf16[1,16,2,14,8,256]{5,4,2,3,1,0:T(8,128)(2,1)S(1)}) fusion(bf16[16,2,14,8,256]{4,3,1,2,0:T(8,128)(2,1)} %all-to-all-done, bf16[16,2,14,8,256]{4,3,1,2,0:T(8,128)(2,1)} %collective-permute-done.6, pred[]{:T(512)S(6)} %eq.14), kind=kLoop, calls=%fused_computation.4 | loop fusion | flops 1835008 | bytes 7340033 | tf_op jit(solution)/shard_map/stack | solution.py:559
  66.2 0.5 copy.16
  66.7 3.8 %shard_map.108.middle_ref = f32[2,4,128,256]{3,2,1,0:T(8,128)S(1)} custom-call(bf16[4,4,128,256]{3,2,1,0:T(8,128)(2,1)S(1)} %get-tuple-element.52.latent_ref, bf16[28,256,256]{2,1,0:T(8,128)(2,1)S(1)} %bitcast.95), custom_call_target="tpu_custom_call" | custom-call | flops 1 | bytes 1 | tf_op jit(solution)/shard_map/pallas_call | solution.py:250
  70.8 2.3 %collective-permute-start.10 = (bf16[2,128,256]{2,1,0:T(8,128)(2,1)S(1)}, bf16[2,128,256]{2,1,0:T(8,128)(2,1)S(1)}, u32[]{:S(2)}, u32[]{:S(2)}) collective-permute-start(bf16[2,128,256]{2,1,0:T(8,128)(2,1)S(1)} %pad_maximum_fusion), channel_id=1, source_target_pairs={{0,31},{1,2},{2,1},{3,4},{4,3},{5,6},{6,5},{7,8},{8,7},{9,10},{10,... | collective-permute-start | bytes 393224 | tf_op jit(solution)/shard_map/ppermute | solution.py:575
  73.1 2.6 %shard_map.109.edge_ref = f32[2,4,128,256]{3,2,1,0:T(8,128)S(1)} custom-call(bf16[4,4,128,256]{3,2,1,0:T(8,128)(2,1)S(1)} %get-tuple-element.52.latent_ref, bf16[28,256,256]{2,1,0:T(8,128)(2,1)S(1)} %bitcast.96), custom_call_target="tpu_custom_call" | custom-call | flops 1 | bytes 1 | tf_op jit(solution)/shard_map/pallas_call | solution.py:250
  75.7 3.6 %collective-permute-done.10.second_end_ref = bf16[2,128,256]{2,1,0:T(8,128)(2,1)S(1)} collective-permute-done((bf16[2,128,256]{2,1,0:T(8,128)(2,1)S(1)}, bf16[2,128,256]{2,1,0:T(8,128)(2,1)S(1)}, u32[]{:S(2)}, u32[]{:S(2)}) %collective-permute-start.10) | collective-permute-done | bytes 131104 | tf_op jit(solution)/shard_map/ppermute | solution.py:575
  79.3 12.4 %shard_map.110 = (bf16[4,4,128,256]{3,2,1,0:T(8,128)(2,1)}, bf16[6,256,768]{2,1,0:T(8,128)(2,1)S(1)}, bf16[2048,768]{1,0:T(8,128)(2,1)S(1)}, bf16[32,8,16,128]{3...) custom-call(s32[4]{0:T(128)S(1)} %pad_add_fusion.1.flags_ref, f32[2,4,128,256]{3,2,1,0:T(8,128)S(1)} %shard_map.108.middle_ref, ...), custom_call_target="tpu_custom_call" | custom-call | tf_op jit(solution)/shard_map/pallas_call | solution.py:409
  91.8 1.7 %collective-permute-start.11 = (bf16[32,8,16,128]{3,2,1,0:T(8,128)(2,1)S(1)}, bf16[32,8,16,128]{3,2,1,0:T(8,128)(2,1)S(1)}, u32[]{:S(2)}, u32[]{:S(2)}) collective-permute-start(bf16[32,8,16,128]{3,2,1,0:T(8,128)(2,1)S(1)} %get-tuple-element.57), channel_id=1, source_target_pairs={{0,32},{32,0},{64,96},{96,64},{1,33},{33,1},{65,97},{97,65},{2,34}... | collective-permute-start | bytes 3145736 | tf_op jit(solution)/shard_map/ppermute | solution.py:449
  93.4 2.3 %collective-permute-done.11 = bf16[32,8,16,128]{3,2,1,0:T(8,128)(2,1)S(1)} collective-permute-done((bf16[32,8,16,128]{3,2,1,0:T(8,128)(2,1)S(1)}, bf16[32,8,16,128]{3,2,1,0:T(8,128)(2,1)S(1)}, u32[]{:S(2)}, u32[]{:S(2)}) %collective-permute-start.11) | collective-permute-done | bytes 1048608 | tf_op jit(solution)/shard_map/ppermute | solution.py:449
  96.1 4.8 %shard_map.111 = (bf16[32,6,16,128]{3,2,1,0:T(8,128)(2,1)S(1)}, bf16[32,6,16,128]{3,2,1,0:T(8,128)(2,1)S(1)}) custom-call(s32[4]{0:T(128)S(1)} %pad_add_fusion.1.flags_ref, bf16[6,256,768]{2,1,0:T(8,128)(2,1)S(1)} %get-tuple-element.60.turned, bf16[2048,768]{1,0:T(8,128)(2,1)S(1)} %get-tuple-element.61.shifted), custom_call_target="tpu_custom_call" | custom-call | tf_op jit(solution)/shard_map/pallas_call | solution.py:439
  100.9 0.5 collective-permute-start.18
  101.6 2.3 %collective-permute-start.13 = (bf16[2,4,8,16,128]{4,3,2,1,0:T(8,128)(2,1)S(1)}, bf16[2,4,8,16,128]{4,3,2,1,0:T(8,128)(2,1)S(1)}, u32[]{:S(2)}, u32[]{:S(2)}) collective-permute-start(bf16[2,4,8,16,128]{4,3,2,1,0:T(8,128)(2,1)S(1)} %get-tuple-element.70), channel_id=1, source_target_pairs={{0,2},{1,3},{2,0},{3,1},{4,6},{5,7},{6,4},{7,5},{8,10},{9,11},{10,... | collective-permute-start | bytes 786440 | tf_op jit(solution)/shard_map/ppermute | solution.py:459
  103.9 1.5 %collective-permute-start.14 = (bf16[2,4,8,16,128]{4,3,2,1,0:T(8,128)(2,1)S(1)}, bf16[2,4,8,16,128]{4,3,2,1,0:T(8,128)(2,1)S(1)}, u32[]{:S(2)}, u32[]{:S(2)}) collective-permute-start(bf16[2,4,8,16,128]{4,3,2,1,0:T(8,128)(2,1)S(1)} %get-tuple-element.69), channel_id=1, source_target_pairs={{0,3},{1,2},{2,1},{3,0},{4,7},{5,6},{6,5},{7,4},{8,11},{9,10},{10,... | collective-permute-start | bytes 786440 | tf_op jit(solution)/shard_map/ppermute | solution.py:459
  105.8 1.1 collective-permute-start.20
  106.9 2.5 %collective-permute-done.12 = bf16[2,4,8,16,128]{4,3,2,1,0:T(8,128)(2,1)S(1)} collective-permute-done((bf16[2,4,8,16,128]{4,3,2,1,0:T(8,128)(2,1)S(1)}, bf16[2,4,8,16,128]{4,3,2,1,0:T(8,128)(2,1)S(1)}, u32[]{:S(2)}, u32[]{:S(2)}) %collective-permute-start.12) | collective-permute-done | bytes 262176 | tf_op jit(solution)/shard_map/ppermute | solution.py:459
  109.7 6.2 %collective-permute-done.13 = bf16[2,4,8,16,128]{4,3,2,1,0:T(8,128)(2,1)S(1)} collective-permute-done((bf16[2,4,8,16,128]{4,3,2,1,0:T(8,128)(2,1)S(1)}, bf16[2,4,8,16,128]{4,3,2,1,0:T(8,128)(2,1)S(1)}, u32[]{:S(2)}, u32[]{:S(2)}) %collective-permute-start.13) | collective-permute-done | bytes 262176 | tf_op jit(solution)/shard_map/ppermute | solution.py:459
  115.9 2.0 %collective-permute-done.14 = bf16[2,4,8,16,128]{4,3,2,1,0:T(8,128)(2,1)S(1)} collective-permute-done((bf16[2,4,8,16,128]{4,3,2,1,0:T(8,128)(2,1)S(1)}, bf16[2,4,8,16,128]{4,3,2,1,0:T(8,128)(2,1)S(1)}, u32[]{:S(2)}, u32[]{:S(2)}) %collective-permute-start.14) | collective-permute-done | bytes 262176 | tf_op jit(solution)/shard_map/ppermute | solution.py:459
  118.2 1.8 %collective-permute-start.16 = (bf16[2,8,16,128]{3,2,1,0:T(8,128)(2,1)S(1)}, bf16[2,8,16,128]{3,2,1,0:T(8,128)(2,1)S(1)}, u32[]{:S(2)}, u32[]{:S(2)}) collective-permute-start(bf16[2,8,16,128]{3,2,1,0:T(8,128)(2,1)S(1)} %get-tuple-element.76), channel_id=1, source_target_pairs={{0,8},{1,9},{2,10},{3,11},{4,12},{5,13},{6,14},{7,15},{8,0},{9,1},... | collective-permute-start | bytes 196616 | tf_op jit(solution)/shard_map/ppermute | solution.py:459
  120.0 2.0 %collective-permute-start.17 = (bf16[2,8,16,128]{3,2,1,0:T(8,128)(2,1)S(1)}, bf16[2,8,16,128]{3,2,1,0:T(8,128)(2,1)S(1)}, u32[]{:S(2)}, u32[]{:S(2)}) collective-permute-start(bf16[2,8,16,128]{3,2,1,0:T(8,128)(2,1)S(1)} %get-tuple-element.75), channel_id=1, source_target_pairs={{0,12},{1,13},{2,14},{3,15},{4,8},{5,9},{6,10},{7,11},{8,4},{9,5},... | collective-permute-start | bytes 196616 | tf_op jit(solution)/shard_map/ppermute | solution.py:459
  122.3 2.7 %collective-permute-start.23 = (bf16[2,6,16,128]{3,2,1,0:T(8,128)(2,1)S(1)}, bf16[2,6,16,128]{3,2,1,0:T(8,128)(2,1)S(1)}, u32[]{:S(2)}, u32[]{:S(2)}) collective-permute-start(bf16[2,6,16,128]{3,2,1,0:T(8,128)(2,1)S(1)} %get-tuple-element.85), channel_id=1, source_target_pairs={{0,2},{1,3},{2,0},{3,1},{4,6},{5,7},{6,4},{7,5},{8,10},{9,11},{10,... | collective-permute-start | bytes 147464 | tf_op jit(solution)/shard_map/ppermute | solution.py:459
  125.0 1.1 collective-permute-start.24
  126.2 0.8 collective-permute-done.23
  127.0 2.2 %collective-permute-done.24 = bf16[2,6,16,128]{3,2,1,0:T(8,128)(2,1)S(1)} collective-permute-done((bf16[2,6,16,128]{3,2,1,0:T(8,128)(2,1)S(1)}, bf16[2,6,16,128]{3,2,1,0:T(8,128)(2,1)S(1)}, u32[]{:S(2)}, u32[]{:S(2)}) %collective-permute-start.24) | collective-permute-done | bytes 49184 | tf_op jit(solution)/shard_map/ppermute | solution.py:459
  129.2 1.7 %collective-permute-start.25 = (f32[14,16,128]{2,1,0:T(8,128)S(1)}, f32[14,16,128]{2,1,0:T(8,128)S(1)}, u32[]{:S(2)}, u32[]{:S(2)}) collective-permute-start(f32[14,16,128]{2,1,0:T(8,128)S(1)} %fusion.10), channel_id=1, source_target_pairs={{0,16},{1,17},{2,18},{3,19},{4,20},{5,21},{6,22},{7,23},{8,24},{9,... | collective-permute-start | bytes 344072 | tf_op jit(solution)/shard_map/ppermute | solution.py:459
  130.9 2.2 %collective-permute-done.25 = f32[14,16,128]{2,1,0:T(8,128)S(1)} collective-permute-done((f32[14,16,128]{2,1,0:T(8,128)S(1)}, f32[14,16,128]{2,1,0:T(8,128)S(1)}, u32[]{:S(2)}, u32[]{:S(2)}) %collective-permute-start.25) | collective-permute-done | bytes 114720 | tf_op jit(solution)/shard_map/ppermute | solution.py:459
  133.1 1.2 collective-permute-start.26
  134.3 5.0 %collective-permute-done.26 = f32[14,16,128]{2,1,0:T(8,128)S(1)} collective-permute-done((f32[14,16,128]{2,1,0:T(8,128)S(1)}, f32[14,16,128]{2,1,0:T(8,128)S(1)}, u32[]{:S(2)}, u32[]{:S(2)}) %collective-permute-start.26) | collective-permute-done | bytes 114720 | tf_op jit(solution)/shard_map/ppermute | solution.py:591
  139.2 6.0 %collective-permute-start.27 = (f32[14,16,128]{2,1,0:T(8,128)S(1)}, f32[14,16,128]{2,1,0:T(8,128)S(1)}, u32[]{:S(2)}, u32[]{:S(2)}) collective-permute-start(f32[14,16,128]{2,1,0:T(8,128)S(1)} %add.157), channel_id=1, source_target_pairs={{0,32},{32,0},{64,96},{96,64},{1,33},{33,1},{65,97},{97,65},{2,34}... | collective-permute-start | bytes 344072 | tf_op jit(solution)/shard_map/ppermute | solution.py:592
  145.2 1.0 collective-permute-done.27
  146.3 0.7 fusion.6
  (74 shorter events, 3.3 us)
Async XLA Ops:
  0.6 3.1 %copy-start = (s32[1,1,4]{2,1,0:T(1,128)S(1)}, s32[1,1,4]{2,1,0:T(1,128)}, u32[]{:S(2)}) copy-start(s32[1,1,4]{2,1,0:T(1,128)} %param.11) | copy-start | bytes 52
  1.5 8.1 %collective-permute-start = (bf16[14,8,256]{2,1,0:T(8,128)(2,1)S(1)}, bf16[14,8,256]{2,1,0:T(8,128)(2,1)S(1)}, u32[]{:S(2)}, u32[]{:S(2)}) collective-permute-start(bf16[14,8,256]{2,1,0:T(8,128)(2,1)S(1)} %get-tuple-element.65), channel_id=1, source_target_pairs={{0,16},{1,17},{2,18},{3,19},{4,20},{5,21},{6,22},{7,23},{8,24},{9,... | collective-permute-start | bytes 172040 | tf_op jit(solution)/shard_map/ppermute | solution.py:468
  5.3 1.2 copy-start.1
  11.1 7.8 %copy-start.2 = (bf16[2048,256]{1,0:T(8,128)(2,1)S(1)}, bf16[2048,256]{1,0:T(8,128)(2,1)}, u32[]{:S(2)}) copy-start(bf16[2048,256]{1,0:T(8,128)(2,1)} %feats_ref.3) | copy-start | bytes 3145732
  11.1 16.2 %copy-start.6 = (s32[4,1,32,128]{3,2,1,0:T(8,128)S(1)}, s32[4,1,32,128]{3,2,1,0:T(8,128)}, u32[]{:S(2)}) copy-start(s32[4,1,32,128]{3,2,1,0:T(8,128)} %param.12) | copy-start | bytes 196612
  11.1 16.2 %copy-start.4 = (f32[4,1,32,3,128]{4,2,3,1,0:T(8,128)S(1)}, f32[4,1,32,3,128]{4,2,3,1,0:T(8,128)}, u32[]{:S(2)}) copy-start(f32[4,1,32,3,128]{4,2,3,1,0:T(8,128)} %param.14) | copy-start | bytes 589828
  11.1 16.2 %copy-start.5 = (s32[4,1,32]{2,1,0:T(1,128)S(1)}, s32[4,1,32]{2,1,0:T(1,128)}, u32[]{:S(2)}) copy-start(s32[4,1,32]{2,1,0:T(1,128)} %param.13) | copy-start | bytes 1540
  11.1 44.0 %all-to-all-start = ((bf16[16,2,14,8,256]{4,3,1,2,0:T(8,128)(2,1)}), bf16[16,2,14,8,256]{4,3,1,2,0:T(8,128)(2,1)}, u32[]{:S(2)}, u32[]{:S(2)}) async-start(bf16[16,2,14,8,256]{4,3,1,2,0:T(8,128)(2,1)} %broadcast_in_dim.25), calls=%async_computation | async-start | bytes 3670016 | tf_op jit(solution)/shard_map/all_to_all | solution.py:532
  22.8 4.5 %collective-permute-start.1 = (bf16[1024,256]{1,0:T(8,128)(2,1)}, bf16[1024,256]{1,0:T(8,128)(2,1)S(1)}, u32[]{:S(2)}, u32[]{:S(2)}) collective-permute-start(bf16[1024,256]{1,0:T(8,128)(2,1)} %get-tuple-element.39), channel_id=1, source_target_pairs={{0,32},{32,0},{64,96},{96,64},{1,33},{33,1},{65,97},{97,65},{2,34}... | collective-permute-start | bytes 1572872 | tf_op jit(solution)/shard_map/ppermute | solution.py:542
  24.0 16.8 %collective-permute-start.2 = (bf16[1024,256]{1,0:T(8,128)(2,1)}, bf16[1024,256]{1,0:T(8,128)(2,1)S(1)}, u32[]{:S(2)}, u32[]{:S(2)}) collective-permute-start(bf16[1024,256]{1,0:T(8,128)(2,1)} %get-tuple-element.35), channel_id=1, source_target_pairs={{0,64},{32,96},{64,0},{96,32},{1,65},{33,97},{65,1},{97,33},{2,66}... | collective-permute-start | bytes 1572872 | tf_op jit(solution)/shard_map/ppermute | solution.py:529
  26.7 24.0 %collective-permute-start.3 = (bf16[1024,256]{1,0:T(8,128)(2,1)S(1)}, bf16[1024,256]{1,0:T(8,128)(2,1)S(1)}, u32[]{:S(2)}, u32[]{:S(2)}) collective-permute-start(bf16[1024,256]{1,0:T(8,128)(2,1)S(1)} %get-tuple-element.43), channel_id=1, source_target_pairs={{0,96},{32,64},{64,32},{96,0},{1,97},{33,65},{65,33},{97,1},{2,98}... | collective-permute-start | bytes 1572872 | tf_op jit(solution)/shard_map/ppermute | solution.py:530
  55.1 8.5 %collective-permute-start.6 = (bf16[16,2,14,8,256]{4,3,1,2,0:T(8,128)(2,1)}, bf16[16,2,14,8,256]{4,3,1,2,0:T(8,128)(2,1)}, u32[]{:S(2)}, u32[]{:S(2)}) collective-permute-start(bf16[16,2,14,8,256]{4,3,1,2,0:T(8,128)(2,1)} %all-to-all-done), channel_id=1, source_target_pairs={{0,32},{32,0},{64,96},{96,64},{1,33},{33,1},{65,97},{97,65},{2,34}... | collective-permute-start | bytes 5505032 | tf_op jit(solution)/shard_map/ppermute | solution.py:559
  55.5 15.1 %collective-permute-start.5 = (bf16[1,4,128,256]{3,2,1,0:T(8,128)(2,1)S(1)}, bf16[1,4,128,256]{3,2,1,0:T(8,128)(2,1)S(1)}, u32[]{:S(2)}, u32[]{:S(2)}) collective-permute-start(bf16[1,4,128,256]{3,2,1,0:T(8,128)(2,1)S(1)} %get-tuple-element.45), channel_id=1, source_target_pairs={{0,32},{32,0},{64,96},{96,64},{1,33},{33,1},{65,97},{97,65},{2,34}... | collective-permute-start | bytes 786440 | tf_op jit(solution)/shard_map/ppermute | solution.py:557
  55.7 14.9 %collective-permute-start.4 = (bf16[1,4,128,256]{3,2,1,0:T(8,128)(2,1)S(1)}, bf16[1,4,128,256]{3,2,1,0:T(8,128)(2,1)S(1)}, u32[]{:S(2)}, u32[]{:S(2)}) collective-permute-start(bf16[1,4,128,256]{3,2,1,0:T(8,128)(2,1)S(1)} %get-tuple-element.44), channel_id=1, source_target_pairs={{0,96},{32,64},{64,32},{96,0},{1,97},{33,65},{65,33},{97,1},{2,98}... | collective-permute-start | bytes 786440 | tf_op jit(solution)/shard_map/ppermute | solution.py:556
  58.5 17.2 %collective-permute-start.7 = (bf16[4,1,128,256]{3,2,1,0:T(8,128)(2,1)S(1)}, bf16[4,1,128,256]{3,2,1,0:T(8,128)(2,1)S(1)}, u32[]{:S(2)}, u32[]{:S(2)}) collective-permute-start(bf16[4,1,128,256]{3,2,1,0:T(8,128)(2,1)S(1)} %get-tuple-element.53), channel_id=1, source_target_pairs={{0,1},{1,0},{2,3},{3,2},{4,5},{5,4},{6,7},{7,6},{8,9},{9,8},{10,11... | collective-permute-start | bytes 786440 | tf_op jit(solution)/shard_map/ppermute | solution.py:562
  60.1 15.6 %collective-permute-start.8 = (bf16[4,1,128,256]{3,2,1,0:T(8,128)(2,1)S(1)}, bf16[4,1,128,256]{3,2,1,0:T(8,128)(2,1)S(1)}, u32[]{:S(2)}, u32[]{:S(2)}) collective-permute-start(bf16[4,1,128,256]{3,2,1,0:T(8,128)(2,1)S(1)} %get-tuple-element.54), channel_id=1, source_target_pairs={{0,31},{1,2},{2,1},{3,4},{4,3},{5,6},{6,5},{7,8},{8,7},{9,10},{10,... | collective-permute-start | bytes 786440 | tf_op jit(solution)/shard_map/ppermute | solution.py:563
  66.7 6.3 %copy-start.7 = (bf16[256]{0:T(256)(128)(2,1)S(1)}, bf16[256]{0:T(256)(128)(2,1)}, u32[]{:S(2)}) copy-start(bf16[256]{0:T(256)(128)(2,1)} %param.16) | copy-start | bytes 1540
  70.7 5.1 %collective-permute-start.9 = (bf16[2,128,256]{2,1,0:T(8,128)(2,1)S(1)}, bf16[2,128,256]{2,1,0:T(8,128)(2,1)S(1)}, u32[]{:S(2)}, u32[]{:S(2)}) collective-permute-start(bf16[2,128,256]{2,1,0:T(8,128)(2,1)S(1)} %pad_maximum_fusion.1), channel_id=1, source_target_pairs={{0,1},{1,0},{2,3},{3,2},{4,5},{5,4},{6,7},{7,6},{8,9},{9,8},{10,11... | collective-permute-start | bytes 393224 | tf_op jit(solution)/shard_map/ppermute | solution.py:575
  70.8 8.6 %collective-permute-start.10 = (bf16[2,128,256]{2,1,0:T(8,128)(2,1)S(1)}, bf16[2,128,256]{2,1,0:T(8,128)(2,1)S(1)}, u32[]{:S(2)}, u32[]{:S(2)}) collective-permute-start(bf16[2,128,256]{2,1,0:T(8,128)(2,1)S(1)} %pad_maximum_fusion), channel_id=1, source_target_pairs={{0,31},{1,2},{2,1},{3,4},{4,3},{5,6},{6,5},{7,8},{8,7},{9,10},{10,... | collective-permute-start | bytes 393224 | tf_op jit(solution)/shard_map/ppermute | solution.py:575
  73.1 6.3 %copy-start.3 = (bf16[4,4,128,256]{3,2,1,0:T(8,128)(2,1)S(1)}, bf16[4,4,128,256]{3,2,1,0:T(8,128)(2,1)}, u32[]{:S(2)}) copy-start(bf16[4,4,128,256]{3,2,1,0:T(8,128)(2,1)} %cotangent_ref.1) | copy-start | bytes 3145732
  91.8 3.9 %collective-permute-start.11 = (bf16[32,8,16,128]{3,2,1,0:T(8,128)(2,1)S(1)}, bf16[32,8,16,128]{3,2,1,0:T(8,128)(2,1)S(1)}, u32[]{:S(2)}, u32[]{:S(2)}) collective-permute-start(bf16[32,8,16,128]{3,2,1,0:T(8,128)(2,1)S(1)} %get-tuple-element.57), channel_id=1, source_target_pairs={{0,32},{32,0},{64,96},{96,64},{1,33},{33,1},{65,97},{97,65},{2,34}... | collective-permute-start | bytes 3145736 | tf_op jit(solution)/shard_map/ppermute | solution.py:449
  100.9 4.5 %collective-permute-start.18 = (bf16[32,6,16,128]{3,2,1,0:T(8,128)(2,1)S(1)}, bf16[32,6,16,128]{3,2,1,0:T(8,128)(2,1)S(1)}, u32[]{:S(2)}, u32[]{:S(2)}) collective-permute-start(bf16[32,6,16,128]{3,2,1,0:T(8,128)(2,1)S(1)} %get-tuple-element.63), channel_id=1, source_target_pairs={{0,32},{32,0},{64,96},{96,64},{1,33},{33,1},{65,97},{97,65},{2,34}... | collective-permute-start | bytes 2359304 | tf_op jit(solution)/shard_map/ppermute | solution.py:449
  101.5 7.8 %collective-permute-start.12 = (bf16[2,4,8,16,128]{4,3,2,1,0:T(8,128)(2,1)S(1)}, bf16[2,4,8,16,128]{4,3,2,1,0:T(8,128)(2,1)S(1)}, u32[]{:S(2)}, u32[]{:S(2)}) collective-permute-start(bf16[2,4,8,16,128]{4,3,2,1,0:T(8,128)(2,1)S(1)} %get-tuple-element.68), channel_id=1, source_target_pairs={{0,1},{1,0},{2,3},{3,2},{4,5},{5,4},{6,7},{7,6},{8,9},{9,8},{10,11... | collective-permute-start | bytes 786440 | tf_op jit(solution)/shard_map/ppermute | solution.py:459
  101.6 14.3 %collective-permute-start.13 = (bf16[2,4,8,16,128]{4,3,2,1,0:T(8,128)(2,1)S(1)}, bf16[2,4,8,16,128]{4,3,2,1,0:T(8,128)(2,1)S(1)}, u32[]{:S(2)}, u32[]{:S(2)}) collective-permute-start(bf16[2,4,8,16,128]{4,3,2,1,0:T(8,128)(2,1)S(1)} %get-tuple-element.70), channel_id=1, source_target_pairs={{0,2},{1,3},{2,0},{3,1},{4,6},{5,7},{6,4},{7,5},{8,10},{9,11},{10,... | collective-permute-start | bytes 786440 | tf_op jit(solution)/shard_map/ppermute | solution.py:459
  103.9 14.0 %collective-permute-start.14 = (bf16[2,4,8,16,128]{4,3,2,1,0:T(8,128)(2,1)S(1)}, bf16[2,4,8,16,128]{4,3,2,1,0:T(8,128)(2,1)S(1)}, u32[]{:S(2)}, u32[]{:S(2)}) collective-permute-start(bf16[2,4,8,16,128]{4,3,2,1,0:T(8,128)(2,1)S(1)} %get-tuple-element.69), channel_id=1, source_target_pairs={{0,3},{1,2},{2,1},{3,0},{4,7},{5,6},{6,5},{7,4},{8,11},{9,10},{10,... | collective-permute-start | bytes 786440 | tf_op jit(solution)/shard_map/ppermute | solution.py:459
  105.8 14.2 %collective-permute-start.19 = (bf16[2,4,6,16,128]{4,3,2,1,0:T(8,128)(2,1)S(1)}, bf16[2,4,6,16,128]{4,3,2,1,0:T(8,128)(2,1)S(1)}, u32[]{:S(2)}, u32[]{:S(2)}) collective-permute-start(bf16[2,4,6,16,128]{4,3,2,1,0:T(8,128)(2,1)S(1)} %get-tuple-element.71), channel_id=1, source_target_pairs={{0,4},{1,5},{2,6},{3,7},{4,0},{5,1},{6,2},{7,3},{8,12},{9,13},{10,... | collective-permute-start | bytes 589832 | tf_op jit(solution)/shard_map/ppermute | solution.py:459
  105.8 16.2 %collective-permute-start.20 = (bf16[2,4,6,16,128]{4,3,2,1,0:T(8,128)(2,1)S(1)}, bf16[2,4,6,16,128]{4,3,2,1,0:T(8,128)(2,1)S(1)}, u32[]{:S(2)}, u32[]{:S(2)}) collective-permute-start(bf16[2,4,6,16,128]{4,3,2,1,0:T(8,128)(2,1)S(1)} %get-tuple-element.73), channel_id=1, source_target_pairs={{0,8},{1,9},{2,10},{3,11},{4,12},{5,13},{6,14},{7,15},{8,0},{9,1},... | collective-permute-start | bytes 589832 | tf_op jit(solution)/shard_map/ppermute | solution.py:459
  109.4 12.6 %collective-permute-start.21 = (bf16[2,4,6,16,128]{4,3,2,1,0:T(8,128)(2,1)S(1)}, bf16[2,4,6,16,128]{4,3,2,1,0:T(8,128)(2,1)S(1)}, u32[]{:S(2)}, u32[]{:S(2)}) collective-permute-start(bf16[2,4,6,16,128]{4,3,2,1,0:T(8,128)(2,1)S(1)} %get-tuple-element.72), channel_id=1, source_target_pairs={{0,12},{1,13},{2,14},{3,15},{4,8},{5,9},{6,10},{7,11},{8,4},{9,5},... | collective-permute-start | bytes 589832 | tf_op jit(solution)/shard_map/ppermute | solution.py:459
  118.1 6.9 %collective-permute-start.15 = (bf16[2,8,16,128]{3,2,1,0:T(8,128)(2,1)S(1)}, bf16[2,8,16,128]{3,2,1,0:T(8,128)(2,1)S(1)}, u32[]{:S(2)}, u32[]{:S(2)}) collective-permute-start(bf16[2,8,16,128]{3,2,1,0:T(8,128)(2,1)S(1)} %get-tuple-element.74), channel_id=1, source_target_pairs={{0,4},{1,5},{2,6},{3,7},{4,0},{5,1},{6,2},{7,3},{8,12},{9,13},{10,... | collective-permute-start | bytes 196616 | tf_op jit(solution)/shard_map/ppermute | solution.py:459
  118.2 7.9 %collective-permute-start.16 = (bf16[2,8,16,128]{3,2,1,0:T(8,128)(2,1)S(1)}, bf16[2,8,16,128]{3,2,1,0:T(8,128)(2,1)S(1)}, u32[]{:S(2)}, u32[]{:S(2)}) collective-permute-start(bf16[2,8,16,128]{3,2,1,0:T(8,128)(2,1)S(1)} %get-tuple-element.76), channel_id=1, source_target_pairs={{0,8},{1,9},{2,10},{3,11},{4,12},{5,13},{6,14},{7,15},{8,0},{9,1},... | collective-permute-start | bytes 196616 | tf_op jit(solution)/shard_map/ppermute | solution.py:459
  120.0 6.1 %collective-permute-start.17 = (bf16[2,8,16,128]{3,2,1,0:T(8,128)(2,1)S(1)}, bf16[2,8,16,128]{3,2,1,0:T(8,128)(2,1)S(1)}, u32[]{:S(2)}, u32[]{:S(2)}) collective-permute-start(bf16[2,8,16,128]{3,2,1,0:T(8,128)(2,1)S(1)} %get-tuple-element.75), channel_id=1, source_target_pairs={{0,12},{1,13},{2,14},{3,15},{4,8},{5,9},{6,10},{7,11},{8,4},{9,5},... | collective-permute-start | bytes 196616 | tf_op jit(solution)/shard_map/ppermute | solution.py:459
  122.2 4.0 %collective-permute-start.22 = (bf16[2,6,16,128]{3,2,1,0:T(8,128)(2,1)S(1)}, bf16[2,6,16,128]{3,2,1,0:T(8,128)(2,1)S(1)}, u32[]{:S(2)}, u32[]{:S(2)}) collective-permute-start(bf16[2,6,16,128]{3,2,1,0:T(8,128)(2,1)S(1)} %get-tuple-element.83), channel_id=1, source_target_pairs={{0,1},{1,0},{2,3},{3,2},{4,5},{5,4},{6,7},{7,6},{8,9},{9,8},{10,11... | collective-permute-start | bytes 147464 | tf_op jit(solution)/shard_map/ppermute | solution.py:459
  122.3 4.7 %collective-permute-start.23 = (bf16[2,6,16,128]{3,2,1,0:T(8,128)(2,1)S(1)}, bf16[2,6,16,128]{3,2,1,0:T(8,128)(2,1)S(1)}, u32[]{:S(2)}, u32[]{:S(2)}) collective-permute-start(bf16[2,6,16,128]{3,2,1,0:T(8,128)(2,1)S(1)} %get-tuple-element.85), channel_id=1, source_target_pairs={{0,2},{1,3},{2,0},{3,1},{4,6},{5,7},{6,4},{7,5},{8,10},{9,11},{10,... | collective-permute-start | bytes 147464 | tf_op jit(solution)/shard_map/ppermute | solution.py:459
  125.0 4.2 %collective-permute-start.24 = (bf16[2,6,16,128]{3,2,1,0:T(8,128)(2,1)S(1)}, bf16[2,6,16,128]{3,2,1,0:T(8,128)(2,1)S(1)}, u32[]{:S(2)}, u32[]{:S(2)}) collective-permute-start(bf16[2,6,16,128]{3,2,1,0:T(8,128)(2,1)S(1)} %get-tuple-element.84), channel_id=1, source_target_pairs={{0,3},{1,2},{2,1},{3,0},{4,7},{5,6},{6,5},{7,4},{8,11},{9,10},{10,... | collective-permute-start | bytes 147464 | tf_op jit(solution)/shard_map/ppermute | solution.py:459
  129.2 3.9 %collective-permute-start.25 = (f32[14,16,128]{2,1,0:T(8,128)S(1)}, f32[14,16,128]{2,1,0:T(8,128)S(1)}, u32[]{:S(2)}, u32[]{:S(2)}) collective-permute-start(f32[14,16,128]{2,1,0:T(8,128)S(1)} %fusion.10), channel_id=1, source_target_pairs={{0,16},{1,17},{2,18},{3,19},{4,20},{5,21},{6,22},{7,23},{8,24},{9,... | collective-permute-start | bytes 344072 | tf_op jit(solution)/shard_map/ppermute | solution.py:459
  133.1 6.1 %collective-permute-start.26 = (f32[14,16,128]{2,1,0:T(8,128)S(1)}, f32[14,16,128]{2,1,0:T(8,128)S(1)}, u32[]{:S(2)}, u32[]{:S(2)}) collective-permute-start(f32[14,16,128]{2,1,0:T(8,128)S(1)} %fusion.13), channel_id=1, source_target_pairs={{0,64},{32,96},{64,0},{96,32},{1,65},{33,97},{65,1},{97,33},{2,66}... | collective-permute-start | bytes 344072 | tf_op jit(solution)/shard_map/ppermute | solution.py:591
  139.2 6.9 %collective-permute-start.27 = (f32[14,16,128]{2,1,0:T(8,128)S(1)}, f32[14,16,128]{2,1,0:T(8,128)S(1)}, u32[]{:S(2)}, u32[]{:S(2)}) collective-permute-start(f32[14,16,128]{2,1,0:T(8,128)S(1)} %add.157), channel_id=1, source_target_pairs={{0,32},{32,0},{64,96},{96,64},{1,33},{33,1},{65,97},{97,65},{2,34}... | collective-permute-start | bytes 344072 | tf_op jit(solution)/shard_map/ppermute | solution.py:592

commit v4 on v3

--- a/solution.py
+++ b/solution.py
@@ -18,11 +18,7 @@
     point_ids = lax.broadcasted_iota(jnp.int32, (128, points), 1)
     for place, out_ref in enumerate(out_refs):
         owner = scalars_ref[place]
-        slots = slots_ref[owner]
-        position = lax.broadcasted_iota(
-            jnp.int32, slots.shape, 0
-        ) * 128 + lax.broadcasted_iota(jnp.int32, slots.shape, 1)
-        columns = jnp.where(position < scalars_ref[2 + place], slots, -1).T
+        columns = slots_ref[owner].T
         for half in range(2):
             hot = [
                 jnp.where(point_ids == columns[:, r : r + 1], 1.0, 0.0).astype(BF)
@@ -371,7 +367,7 @@
         )
     for z in range(planes):
         for x in range(rows_x):
-            inner_part = edge_ref[int(z > 0), x] if z in (0, planes - 1) else middle_ref[z - 1, x]
+            inner_part = middle_ref[0, x] if z == 1 else edge_ref[max(z - 1, 0), x]
             pre = inner_part + bias_ref[...]
             if x in (0, rows_x - 1):
                 pre = pre + with_shifts(
@@ -521,9 +517,9 @@
 
     slots, counts = send_slots[0, 0], send_counts[0, 0]
     capacity = slots.shape[1]
-    slots = slots.reshape(spaces, capacity // 128, 128)
-    owners = space ^ jnp.arange(spaces, dtype=jnp.int32)
-    scalars = jnp.concatenate([owners.reshape(2, 2), counts[owners].reshape(2, 2)], axis=1)
+    listed = jnp.arange(capacity, dtype=jnp.int32) < counts[:, None]
+    slots = jnp.where(listed, slots, -1).reshape(spaces, capacity // 128, 128)
+    scalars = (space ^ jnp.arange(spaces, dtype=jnp.int32)).reshape(2, 2)
     to_far, to_cross = gather_listed(point_feats, slots, scalars[1])
     to_far, to_cross, gathered = lax.optimization_barrier((to_far, to_cross, gathered))
     from_far = lax.ppermute(to_far, "space", far)
@@ -562,7 +558,7 @@
         lax.ppermute(first_row, "chan", first_pairs),
         lax.ppermute(second_row, "chan", second_pairs),
     ]
-    middle = inner_conv((1, 2), latent, full_weight)
+    middle = inner_conv((1,), latent, full_weight)
     far_rim, near_rim, middle = lax.optimization_barrier((far_rim, near_rim, middle))
     odd = lax.rem(chan, 2)
     corners = []
@@ -574,7 +570,7 @@
         ends = jnp.concatenate(ends, axis=0)
         corners.append(lax.ppermute(ends, "chan", pairs))
         held_latent = lax.optimization_barrier((latent, ends))[0]
-    edge = inner_conv((0, 3), held_latent, full_weight)
+    edge = inner_conv((0, 2, 3), held_latent, full_weight)
 
     activated, turned, shifted, keep, give = outer_conv(
         flags, (middle, edge), latent, near_rim, far_rim, (*faces, *corners),
@@ -587,8 +583,18 @@
     late = sum_over(late, 4, 4, 1).astype(BF)
     early = sum_over(early, 4, 4, 1)
     late = sum_over(late, 1, 4, 1)
-    summed = sum_over(jnp.concatenate([early, late], axis=1), 16, 2, 0)
-    own_sum = summed + lax.ppermute(summed, "space", far)
+    both = jnp.concatenate([early, late], axis=1)
+    y_low = chan // 16
+    kept = lax.dynamic_index_in_dim(both, y_low, 0, keepdims=False)
+    passed = lax.dynamic_index_in_dim(both, 1 - y_low, 0, keepdims=False).astype(BF)
+    over = [(i, i ^ 16) for i in range(chans)]
+    far_over = [(i, i ^ (2 * chans) ^ 16) for i in range(spaces * chans)]
+    own_sum = (
+        kept
+        + lax.ppermute(passed, "chan", over).astype(F32)
+        + lax.ppermute(passed, ("space", "chan"), far_over).astype(F32)
+        + lax.ppermute(kept.astype(BF), "space", far).astype(F32)
+    )
     low_sum, high_sum = in_order(core, own_sum, lax.ppermute(own_sum, "space", swap))
     total = jnp.concatenate([low_sum[:8], high_sum[:7], low_sum[8:], high_sum[8:]], axis=0)
     total = total.reshape(27, 2, row_count, channels // 2).transpose(2, 0, 1, 3)

time: 147 us -> 143 us (0.973)
  waiting for transfers between devices: 37.5 us -> 30 us
  starting transfers between devices: 49.4 us -> 53 us
    ppermute x13 -> x12, waiting for transfers between devices: 15.8 us -> 11 us  [sum_over(): lax.ppermute(part, 'chan', [(i, i ^ offset * step) for i in range(chans)])]
    ppermute x1 -> x3, starting transfers between devices: 1.19 us -> 3.33 us  [the longest x1 1.91 us: on_device(): lax.ppermute(passed, ('space', 'chan'), far_over).astype(F32)]
    ppermute x2, waiting for transfers between devices: 3.61 us -> 1.77 us  [on_device(): corners.append(lax.ppermute(ends, 'chan', pairs))]
    ppermute x13 -> x12, starting transfers between devices: 15 us -> 16.5 us  [sum_over(): lax.ppermute(part, 'chan', [(i, i ^ offset * step) for i in range(chans)])]
    ppermute x1 -> x3, waiting for transfers between devices: 4.96 us -> 4.18 us  [the longest x1 2.21 us: on_device(): lax.ppermute(kept.astype(BF), 'space', far).astype(F32)]
  transfers between devices with their start and end apart: 29 -> 30, of which waited for: 11 -> 11; matrix products, arithmetic and copies ran while one was open for 4% -> 3% of each run, Pallas kernels for 21% -> 22%
where the time goes in v4:
time: 143 us; the launch traced here: 142 us
  starting transfers between devices  53 us (37%)
  Pallas kernels  48.6 us (34%)
  waiting for transfers between devices  30 us (21%)
  other arithmetic  5.22 us (4%)
  local copies, waits for them, and re-layouts  4.34 us (3%)
    ppermute x12, starting transfers between devices, sum_over(): lax.ppermute(part, 'chan', [(i, i ^ offset * step) for i in range(chans)])  16.5 us
    pallas_call x1, Pallas kernels, spread_weights(): pl.pallas_call(spread_kernel, grid=(planes,), in_specs=[pl.BlockSpec(memo...  13.5 us
    pallas_call x1, Pallas kernels, outer_conv(): pl.pallas_call(outer_kernel, in_specs=[pl.BlockSpec(memory_space=pltpu.SM...  12.4 us
    ppermute x12, waiting for transfers between devices, sum_over(): lax.ppermute(part, 'chan', [(i, i ^ offset * step) for i in range(chans)])  11 us
    ppermute x1, waiting for transfers between devices, on_device(): from_cross = lax.ppermute(to_cross, 'space', cross)  9.81 us
    all_to_all x1, starting transfers between devices, on_device(): lax.all_to_all(gathered, 'chan', split_axis=0, concat_axis=0, axis_index_...  7.79 us
    pallas_call x2, Pallas kernels, gather_listed(): pl.pallas_call(send_kernel, in_specs=[pl.BlockSpec(memory_space=pltpu.SME...  6.99 us
    pallas_call x2, Pallas kernels, inner_conv(): pl.pallas_call(functools.partial(inner_kernel, chosen), in_specs=[whole]...  6.45 us
  transfers between devices with their start and end apart: 30, of which 11 were waited for; matrix products, arithmetic and copies ran while one was open for 3% of the time, Pallas kernels for 22%

profile of v4, /device:TPU:1, one launch (start us, length us, event | category | flops | bytes accessed | tf_op | source)
XLA Modules:
  0.0 142.3 jit_solution(5015031552076364079)
XLA Ops:
  0.7 0.8 bitcast_dynamic-update-slice_fusion.1
  1.5 2.2 %collective-permute-start = (bf16[14,8,256]{2,1,0:T(8,128)(2,1)S(1)}, bf16[14,8,256]{2,1,0:T(8,128)(2,1)S(1)}, u32[]{:S(2)}, u32[]{:S(2)}) collective-permute-start(bf16[14,8,256]{2,1,0:T(8,128)(2,1)S(1)} %get-tuple-element.65), channel_id=1, source_target_pairs={{0,16},{1,17},{2,18},{3,19},{4,20},{5,21},{6,22},{7,23},{8,24},{9,... | collective-permute-start | bytes 172040 | tf_op jit(solution)/shard_map/ppermute | solution.py:464
  3.7 0.8 bitcast_select_fusion.slots_ref
  4.6 1.2 copy-done
  5.8 3.1 %shard_map.104 = (bf16[1024,256]{1,0:T(8,128)(2,1)}, bf16[1024,256]{1,0:T(8,128)(2,1)S(1)}) custom-call(s32[2]{0:T(128)S(1)} %get-tuple-element.88.scalars_ref, s32[4,8,128]{2,1,0:T(8,128)S(1)} %bitcast_select_fusion.slots_ref, bf16[2048,256]{1,0:T(8,128)(2,1)S(1)} %copy-done), custom_call_target="tpu_custom_call" | custom-call | flops 1 | bytes 1 | tf_op jit(solution)/shard_map/pallas_call | solution.py:37
  8.9 1.4 broadcast_in_dim.30
  10.4 7.8 %all-to-all-start = ((bf16[16,2,14,8,256]{4,3,1,2,0:T(8,128)(2,1)}), bf16[16,2,14,8,256]{4,3,1,2,0:T(8,128)(2,1)}, u32[]{:S(2)}, u32[]{:S(2)}) async-start(bf16[16,2,14,8,256]{4,3,1,2,0:T(8,128)(2,1)} %broadcast_in_dim.30), calls=%async_computation | async-start | bytes 3670016 | tf_op jit(solution)/shard_map/all_to_all | solution.py:528
  18.2 3.9 %shard_map.105 = (bf16[1024,256]{1,0:T(8,128)(2,1)S(1)}, bf16[1024,256]{1,0:T(8,128)(2,1)}) custom-call(s32[2]{0:T(128)S(1)} %get-tuple-element.36.scalars_ref, s32[4,8,128]{2,1,0:T(8,128)S(1)} %bitcast_select_fusion.slots_ref, bf16[2048,256]{1,0:T(8,128)(2,1)S(1)} %copy-done.1), custom_call_target="tpu_custom_call" | custom-call | flops 1 | bytes 1 | tf_op jit(solution)/shard_map/pallas_call | solution.py:37
  22.1 1.3 collective-permute-start.1
  23.3 2.6 %collective-permute-start.2 = (bf16[1024,256]{1,0:T(8,128)(2,1)}, bf16[1024,256]{1,0:T(8,128)(2,1)S(1)}, u32[]{:S(2)}, u32[]{:S(2)}) collective-permute-start(bf16[1024,256]{1,0:T(8,128)(2,1)} %get-tuple-element.35), channel_id=1, source_target_pairs={{0,64},{32,96},{64,0},{96,32},{1,65},{33,97},{65,1},{97,33},{2,66}... | collective-permute-start | bytes 1572872 | tf_op jit(solution)/shard_map/ppermute | solution.py:525
  25.9 0.5 collective-permute-start.3
  26.6 13.5 %shard_map.106 = (bf16[2048,2048]{1,0:T(8,128)(2,1)S(1)}, f32[2048,256]{1,0:T(8,128)S(1)}, f32[2048,128]{1,0:T(8,128)S(1)}) custom-call(s32[4,32]{1,0:T(4,128)S(1)} %bitcast.93, s32[4,32,128]{2,1,0:T(8,128)S(1)} %broadcast_xor_fusion.near_ref, f32[4,3,32,128]{3,2,1,0:T(8,128)S(1)} %bitcast.92, bf16[1024,256]{1,0:T(8,128)(2,1)S(1)} %get-tuple-element.37.t0, ...), custom_call_target="tpu_custom_call" | custom-call | tf_op jit(solution)/shard_map/pallas_call | solution.py:99
  40.1 9.8 %collective-permute-done.3.t1 = bf16[1024,256]{1,0:T(8,128)(2,1)S(1)} collective-permute-done((bf16[1024,256]{1,0:T(8,128)(2,1)S(1)}, bf16[1024,256]{1,0:T(8,128)(2,1)S(1)}, u32[]{:S(2)}, u32[]{:S(2)}) %collective-permute-start.3) | collective-permute-done | bytes 524320 | tf_op jit(solution)/shard_map/ppermute | solution.py:526
  49.9 4.4 %shard_map.107 = (bf16[4,4,128,256]{3,2,1,0:T(8,128)(2,1)S(1)}, bf16[1,4,128,256]{3,2,1,0:T(8,128)(2,1)S(1)}, bf16[1,4,128,256]{3,2,1,0:T(8,128)(2,1)S(1)}, bf16...) custom-call(s32[4]{0:T(128)S(1)} %pad_add_fusion.flags_ref, ...), custom_call_target="tpu_custom_call" | custom-call | tf_op jit(solution)/shard_map/pallas_call | solution.py:171
  54.9 2.8 %collective-permute-start.4 = (bf16[1,4,128,256]{3,2,1,0:T(8,128)(2,1)S(1)}, bf16[1,4,128,256]{3,2,1,0:T(8,128)(2,1)S(1)}, u32[]{:S(2)}, u32[]{:S(2)}) collective-permute-start(bf16[1,4,128,256]{3,2,1,0:T(8,128)(2,1)S(1)} %get-tuple-element.44), channel_id=1, source_target_pairs={{0,96},{32,64},{64,32},{96,0},{1,97},{33,65},{65,33},{97,1},{2,98}... | collective-permute-start | bytes 786440 | tf_op jit(solution)/shard_map/ppermute | solution.py:552
  57.7 1.6 %collective-permute-start.7 = (bf16[4,1,128,256]{3,2,1,0:T(8,128)(2,1)S(1)}, bf16[4,1,128,256]{3,2,1,0:T(8,128)(2,1)S(1)}, u32[]{:S(2)}, u32[]{:S(2)}) collective-permute-start(bf16[4,1,128,256]{3,2,1,0:T(8,128)(2,1)S(1)} %get-tuple-element.53), channel_id=1, source_target_pairs={{0,1},{1,0},{2,3},{3,2},{4,5},{5,4},{6,7},{7,6},{8,9},{9,8},{10,11... | collective-permute-start | bytes 786440 | tf_op jit(solution)/shard_map/ppermute | solution.py:558
  59.3 3.5 %collective-permute-start.8 = (bf16[4,1,128,256]{3,2,1,0:T(8,128)(2,1)S(1)}, bf16[4,1,128,256]{3,2,1,0:T(8,128)(2,1)S(1)}, u32[]{:S(2)}, u32[]{:S(2)}) collective-permute-start(bf16[4,1,128,256]{3,2,1,0:T(8,128)(2,1)S(1)} %get-tuple-element.54), channel_id=1, source_target_pairs={{0,31},{1,2},{2,1},{3,4},{4,3},{5,6},{6,5},{7,8},{8,7},{9,10},{10,... | collective-permute-start | bytes 786440 | tf_op jit(solution)/shard_map/ppermute | solution.py:559
  62.8 2.3 %select_bitcast_fusion.1 = (bf16[1,16,2,14,8,256]{5,4,2,3,1,0:T(8,128)(2,1)S(1)}, bf16[1,16,2,14,8,256]{5,4,2,3,1,0:T(8,128)(2,1)S(1)}) fusion(bf16[16,2,14,8,256]{4,3,1,2,0:T(8,128)(2,1)} %all-to-all-done, bf16[16,2,14,8,256]{4,3,1,2,0:T(8,128)(2,1)} %collective-permute-done.6, pred[]{:T(512)S(6)} %eq.14), kind=kLoop, calls=%fused_computation.3 | loop fusion | flops 1835008 | bytes 7340033 | tf_op jit(solution)/shard_map/stack | solution.py:555
  65.5 0.5 copy.14
  65.9 2.0 %shard_map.108.middle_ref = f32[1,4,128,256]{3,2,1,0:T(8,128)S(1)} custom-call(bf16[4,4,128,256]{3,2,1,0:T(8,128)(2,1)S(1)} %get-tuple-element.52.latent_ref, bf16[28,256,256]{2,1,0:T(8,128)(2,1)S(1)} %bitcast.89), custom_call_target="tpu_custom_call" | custom-call | flops 1 | bytes 1 | tf_op jit(solution)/shard_map/pallas_call | solution.py:246
  68.2 2.5 %collective-permute-start.10 = (bf16[2,128,256]{2,1,0:T(8,128)(2,1)S(1)}, bf16[2,128,256]{2,1,0:T(8,128)(2,1)S(1)}, u32[]{:S(2)}, u32[]{:S(2)}) collective-permute-start(bf16[2,128,256]{2,1,0:T(8,128)(2,1)S(1)} %pad_maximum_fusion), channel_id=1, source_target_pairs={{0,31},{1,2},{2,1},{3,4},{4,3},{5,6},{6,5},{7,8},{8,7},{9,10},{10,... | collective-permute-start | bytes 393224 | tf_op jit(solution)/shard_map/ppermute | solution.py:571
  70.6 4.4 %shard_map.109.edge_ref = f32[3,4,128,256]{3,2,1,0:T(8,128)S(1)} custom-call(bf16[4,4,128,256]{3,2,1,0:T(8,128)(2,1)S(1)} %get-tuple-element.52.latent_ref, bf16[28,256,256]{2,1,0:T(8,128)(2,1)S(1)} %bitcast.90), custom_call_target="tpu_custom_call" | custom-call | flops 1 | bytes 1 | tf_op jit(solution)/shard_map/pallas_call | solution.py:246
  75.1 1.8 %collective-permute-done.10.second_end_ref = bf16[2,128,256]{2,1,0:T(8,128)(2,1)S(1)} collective-permute-done((bf16[2,128,256]{2,1,0:T(8,128)(2,1)S(1)}, bf16[2,128,256]{2,1,0:T(8,128)(2,1)S(1)}, u32[]{:S(2)}, u32[]{:S(2)}) %collective-permute-start.10) | collective-permute-done | bytes 131104 | tf_op jit(solution)/shard_map/ppermute | solution.py:571
  76.9 12.4 %shard_map.110 = (bf16[4,4,128,256]{3,2,1,0:T(8,128)(2,1)}, bf16[6,256,768]{2,1,0:T(8,128)(2,1)S(1)}, bf16[2048,768]{1,0:T(8,128)(2,1)S(1)}, bf16[32,8,16,128]{3...) custom-call(s32[4]{0:T(128)S(1)} %pad_add_fusion.flags_ref, f32[1,4,128,256]{3,2,1,0:T(8,128)S(1)} %shard_map.108.middle_ref, ...), custom_call_target="tpu_custom_call" | custom-call | tf_op jit(solution)/shard_map/pallas_call | solution.py:405
  89.3 1.7 %collective-permute-start.11 = (bf16[32,8,16,128]{3,2,1,0:T(8,128)(2,1)S(1)}, bf16[32,8,16,128]{3,2,1,0:T(8,128)(2,1)S(1)}, u32[]{:S(2)}, u32[]{:S(2)}) collective-permute-start(bf16[32,8,16,128]{3,2,1,0:T(8,128)(2,1)S(1)} %get-tuple-element.57), channel_id=1, source_target_pairs={{0,32},{32,0},{64,96},{96,64},{1,33},{33,1},{65,97},{97,65},{2,34}... | collective-permute-start | bytes 3145736 | tf_op jit(solution)/shard_map/ppermute | solution.py:445
  91.0 2.3 %collective-permute-done.11 = bf16[32,8,16,128]{3,2,1,0:T(8,128)(2,1)S(1)} collective-permute-done((bf16[32,8,16,128]{3,2,1,0:T(8,128)(2,1)S(1)}, bf16[32,8,16,128]{3,2,1,0:T(8,128)(2,1)S(1)}, u32[]{:S(2)}, u32[]{:S(2)}) %collective-permute-start.11) | collective-permute-done | bytes 1048608 | tf_op jit(solution)/shard_map/ppermute | solution.py:445
  93.7 4.8 %shard_map.111 = (bf16[32,6,16,128]{3,2,1,0:T(8,128)(2,1)S(1)}, bf16[32,6,16,128]{3,2,1,0:T(8,128)(2,1)S(1)}) custom-call(s32[4]{0:T(128)S(1)} %pad_add_fusion.flags_ref, bf16[6,256,768]{2,1,0:T(8,128)(2,1)S(1)} %get-tuple-element.60.turned, bf16[2048,768]{1,0:T(8,128)(2,1)S(1)} %get-tuple-element.61.shifted), custom_call_target="tpu_custom_call" | custom-call | tf_op jit(solution)/shard_map/pallas_call | solution.py:435
  99.1 1.3 collective-permute-start.12
  100.4 2.9 %collective-permute-start.13 = (bf16[2,4,8,16,128]{4,3,2,1,0:T(8,128)(2,1)S(1)}, bf16[2,4,8,16,128]{4,3,2,1,0:T(8,128)(2,1)S(1)}, u32[]{:S(2)}, u32[]{:S(2)}) collective-permute-start(bf16[2,4,8,16,128]{4,3,2,1,0:T(8,128)(2,1)S(1)} %get-tuple-element.70), channel_id=1, source_target_pairs={{0,2},{1,3},{2,0},{3,1},{4,6},{5,7},{6,4},{7,5},{8,10},{9,11},{10,... | collective-permute-start | bytes 786440 | tf_op jit(solution)/shard_map/ppermute | solution.py:455
  103.6 1.1 collective-permute-start.19
  104.7 1.6 %collective-permute-start.20 = (bf16[2,4,6,16,128]{4,3,2,1,0:T(8,128)(2,1)S(1)}, bf16[2,4,6,16,128]{4,3,2,1,0:T(8,128)(2,1)S(1)}, u32[]{:S(2)}, u32[]{:S(2)}) collective-permute-start(bf16[2,4,6,16,128]{4,3,2,1,0:T(8,128)(2,1)S(1)} %get-tuple-element.73), channel_id=1, source_target_pairs={{0,8},{1,9},{2,10},{3,11},{4,12},{5,13},{6,14},{7,15},{8,0},{9,1},... | collective-permute-start | bytes 589832 | tf_op jit(solution)/shard_map/ppermute | solution.py:455
  106.3 0.6 collective-permute-done.12
  106.9 1.7 %collective-permute-start.21 = (bf16[2,4,6,16,128]{4,3,2,1,0:T(8,128)(2,1)S(1)}, bf16[2,4,6,16,128]{4,3,2,1,0:T(8,128)(2,1)S(1)}, u32[]{:S(2)}, u32[]{:S(2)}) collective-permute-start(bf16[2,4,6,16,128]{4,3,2,1,0:T(8,128)(2,1)S(1)} %get-tuple-element.72), channel_id=1, source_target_pairs={{0,12},{1,13},{2,14},{3,15},{4,8},{5,9},{6,10},{7,11},{8,4},{9,5},... | collective-permute-start | bytes 589832 | tf_op jit(solution)/shard_map/ppermute | solution.py:455
  108.7 6.6 %collective-permute-done.13 = bf16[2,4,8,16,128]{4,3,2,1,0:T(8,128)(2,1)S(1)} collective-permute-done((bf16[2,4,8,16,128]{4,3,2,1,0:T(8,128)(2,1)S(1)}, bf16[2,4,8,16,128]{4,3,2,1,0:T(8,128)(2,1)S(1)}, u32[]{:S(2)}, u32[]{:S(2)}) %collective-permute-start.13) | collective-permute-done | bytes 262176 | tf_op jit(solution)/shard_map/ppermute | solution.py:455
  115.3 2.0 %collective-permute-done.14 = bf16[2,4,8,16,128]{4,3,2,1,0:T(8,128)(2,1)S(1)} collective-permute-done((bf16[2,4,8,16,128]{4,3,2,1,0:T(8,128)(2,1)S(1)}, bf16[2,4,8,16,128]{4,3,2,1,0:T(8,128)(2,1)S(1)}, u32[]{:S(2)}, u32[]{:S(2)}) %collective-permute-start.14) | collective-permute-done | bytes 262176 | tf_op jit(solution)/shard_map/ppermute | solution.py:455
  117.6 0.6 collective-permute-start.16
  118.2 3.2 %collective-permute-start.17 = (bf16[2,8,16,128]{3,2,1,0:T(8,128)(2,1)S(1)}, bf16[2,8,16,128]{3,2,1,0:T(8,128)(2,1)S(1)}, u32[]{:S(2)}, u32[]{:S(2)}) collective-permute-start(bf16[2,8,16,128]{3,2,1,0:T(8,128)(2,1)S(1)} %get-tuple-element.75), channel_id=1, source_target_pairs={{0,12},{1,13},{2,14},{3,15},{4,8},{5,9},{6,10},{7,11},{8,4},{9,5},... | collective-permute-start | bytes 196616 | tf_op jit(solution)/shard_map/ppermute | solution.py:455
  121.7 1.5 %collective-permute-start.23 = (bf16[2,6,16,128]{3,2,1,0:T(8,128)(2,1)S(1)}, bf16[2,6,16,128]{3,2,1,0:T(8,128)(2,1)S(1)}, u32[]{:S(2)}, u32[]{:S(2)}) collective-permute-start(bf16[2,6,16,128]{3,2,1,0:T(8,128)(2,1)S(1)} %get-tuple-element.87), channel_id=1, source_target_pairs={{0,2},{1,3},{2,0},{3,1},{4,6},{5,7},{6,4},{7,5},{8,10},{9,11},{10,... | collective-permute-start | bytes 147464 | tf_op jit(solution)/shard_map/ppermute | solution.py:455
  123.1 2.4 %collective-permute-start.24 = (bf16[2,6,16,128]{3,2,1,0:T(8,128)(2,1)S(1)}, bf16[2,6,16,128]{3,2,1,0:T(8,128)(2,1)S(1)}, u32[]{:S(2)}, u32[]{:S(2)}) collective-permute-start(bf16[2,6,16,128]{3,2,1,0:T(8,128)(2,1)S(1)} %get-tuple-element.86), channel_id=1, source_target_pairs={{0,3},{1,2},{2,1},{3,0},{4,7},{5,6},{6,5},{7,4},{8,11},{9,10},{10,... | collective-permute-start | bytes 147464 | tf_op jit(solution)/shard_map/ppermute | solution.py:455
  125.6 0.6 collective-permute-done.23
  126.2 1.1 collective-permute-done.24
  127.4 1.1 collective-permute-start.25
  128.4 1.9 %collective-permute-start.26 = (bf16[14,16,128]{2,1,0:T(8,128)(2,1)S(1)}, bf16[14,16,128]{2,1,0:T(8,128)(2,1)S(1)}, u32[]{:S(2)}, u32[]{:S(2)}) collective-permute-start(bf16[14,16,128]{2,1,0:T(8,128)(2,1)S(1)} %get-tuple-element.83), channel_id=1, source_target_pairs={{0,80},{1,81},{2,82},{3,83},{4,84},{5,85},{6,86},{7,87},{8,88},{9,... | collective-permute-start | bytes 172040 | tf_op jit(solution)/shard_map/ppermute | solution.py:595
  130.7 1.9 %collective-permute-done.26 = bf16[14,16,128]{2,1,0:T(8,128)(2,1)S(1)} collective-permute-done((bf16[14,16,128]{2,1,0:T(8,128)(2,1)S(1)}, bf16[14,16,128]{2,1,0:T(8,128)(2,1)S(1)}, u32[]{:S(2)}, u32[]{:S(2)}) %collective-permute-start.26) | collective-permute-done | bytes 57376 | tf_op jit(solution)/shard_map/ppermute | solution.py:595
  132.7 2.2 %collective-permute-done.27 = bf16[14,16,128]{2,1,0:T(8,128)(2,1)S(1)} collective-permute-done((bf16[14,16,128]{2,1,0:T(8,128)(2,1)S(1)}, bf16[14,16,128]{2,1,0:T(8,128)(2,1)S(1)}, u32[]{:S(2)}, u32[]{:S(2)}) %collective-permute-start.27) | collective-permute-done | bytes 57376 | tf_op jit(solution)/shard_map/ppermute | solution.py:596
  134.9 5.6 %collective-permute-start.28 = (f32[14,16,128]{2,1,0:T(8,128)S(1)}, f32[14,16,128]{2,1,0:T(8,128)S(1)}, u32[]{:S(2)}, u32[]{:S(2)}) collective-permute-start(f32[14,16,128]{2,1,0:T(8,128)S(1)} %convert_add_fusion.3), channel_id=1, source_target_pairs={{0,32},{32,0},{64,96},{96,64},{1,33},{33,1},{65,97},{97,65},{2,34}... | collective-permute-start | bytes 344072 | tf_op jit(solution)/shard_map/ppermute | solution.py:598
  140.5 1.0 collective-permute-done.28
  141.6 0.7 fusion.6
  (69 shorter events, 3.6 us)
Async XLA Ops:
  1.5 7.4 %collective-permute-start = (bf16[14,8,256]{2,1,0:T(8,128)(2,1)S(1)}, bf16[14,8,256]{2,1,0:T(8,128)(2,1)S(1)}, u32[]{:S(2)}, u32[]{:S(2)}) collective-permute-start(bf16[14,8,256]{2,1,0:T(8,128)(2,1)S(1)} %get-tuple-element.65), channel_id=1, source_target_pairs={{0,16},{1,17},{2,18},{3,19},{4,20},{5,21},{6,22},{7,23},{8,24},{9,... | collective-permute-start | bytes 172040 | tf_op jit(solution)/shard_map/ppermute | solution.py:464
  4.6 1.2 copy-start
  10.4 7.8 %copy-start.1 = (bf16[2048,256]{1,0:T(8,128)(2,1)S(1)}, bf16[2048,256]{1,0:T(8,128)(2,1)}, u32[]{:S(2)}) copy-start(bf16[2048,256]{1,0:T(8,128)(2,1)} %feats_ref.3) | copy-start | bytes 3145732
  10.4 16.2 %copy-start.5 = (s32[4,1,32,128]{3,2,1,0:T(8,128)S(1)}, s32[4,1,32,128]{3,2,1,0:T(8,128)}, u32[]{:S(2)}) copy-start(s32[4,1,32,128]{3,2,1,0:T(8,128)} %param.12) | copy-start | bytes 196612
  10.4 16.2 %copy-start.3 = (f32[4,1,32,3,128]{4,2,3,1,0:T(8,128)S(1)}, f32[4,1,32,3,128]{4,2,3,1,0:T(8,128)}, u32[]{:S(2)}) copy-start(f32[4,1,32,3,128]{4,2,3,1,0:T(8,128)} %param.14) | copy-start | bytes 589828
  10.4 16.2 %copy-start.4 = (s32[4,1,32]{2,1,0:T(1,128)S(1)}, s32[4,1,32]{2,1,0:T(1,128)}, u32[]{:S(2)}) copy-start(s32[4,1,32]{2,1,0:T(1,128)} %param.13) | copy-start | bytes 1540
  10.4 44.0 %all-to-all-start = ((bf16[16,2,14,8,256]{4,3,1,2,0:T(8,128)(2,1)}), bf16[16,2,14,8,256]{4,3,1,2,0:T(8,128)(2,1)}, u32[]{:S(2)}, u32[]{:S(2)}) async-start(bf16[16,2,14,8,256]{4,3,1,2,0:T(8,128)(2,1)} %broadcast_in_dim.30), calls=%async_computation | async-start | bytes 3670016 | tf_op jit(solution)/shard_map/all_to_all | solution.py:528
  22.1 4.5 %collective-permute-start.1 = (bf16[1024,256]{1,0:T(8,128)(2,1)}, bf16[1024,256]{1,0:T(8,128)(2,1)S(1)}, u32[]{:S(2)}, u32[]{:S(2)}) collective-permute-start(bf16[1024,256]{1,0:T(8,128)(2,1)} %get-tuple-element.39), channel_id=1, source_target_pairs={{0,32},{32,0},{64,96},{96,64},{1,33},{33,1},{65,97},{97,65},{2,34}... | collective-permute-start | bytes 1572872 | tf_op jit(solution)/shard_map/ppermute | solution.py:538
  23.3 16.8 %collective-permute-start.2 = (bf16[1024,256]{1,0:T(8,128)(2,1)}, bf16[1024,256]{1,0:T(8,128)(2,1)S(1)}, u32[]{:S(2)}, u32[]{:S(2)}) collective-permute-start(bf16[1024,256]{1,0:T(8,128)(2,1)} %get-tuple-element.35), channel_id=1, source_target_pairs={{0,64},{32,96},{64,0},{96,32},{1,65},{33,97},{65,1},{97,33},{2,66}... | collective-permute-start | bytes 1572872 | tf_op jit(solution)/shard_map/ppermute | solution.py:525
  25.9 24.0 %collective-permute-start.3 = (bf16[1024,256]{1,0:T(8,128)(2,1)S(1)}, bf16[1024,256]{1,0:T(8,128)(2,1)S(1)}, u32[]{:S(2)}, u32[]{:S(2)}) collective-permute-start(bf16[1024,256]{1,0:T(8,128)(2,1)S(1)} %get-tuple-element.43), channel_id=1, source_target_pairs={{0,96},{32,64},{64,32},{96,0},{1,97},{33,65},{65,33},{97,1},{2,98}... | collective-permute-start | bytes 1572872 | tf_op jit(solution)/shard_map/ppermute | solution.py:526
  54.3 8.5 %collective-permute-start.6 = (bf16[16,2,14,8,256]{4,3,1,2,0:T(8,128)(2,1)}, bf16[16,2,14,8,256]{4,3,1,2,0:T(8,128)(2,1)}, u32[]{:S(2)}, u32[]{:S(2)}) collective-permute-start(bf16[16,2,14,8,256]{4,3,1,2,0:T(8,128)(2,1)} %all-to-all-done), channel_id=1, source_target_pairs={{0,32},{32,0},{64,96},{96,64},{1,33},{33,1},{65,97},{97,65},{2,34}... | collective-permute-start | bytes 5505032 | tf_op jit(solution)/shard_map/ppermute | solution.py:555
  54.7 13.2 %collective-permute-start.5 = (bf16[1,4,128,256]{3,2,1,0:T(8,128)(2,1)S(1)}, bf16[1,4,128,256]{3,2,1,0:T(8,128)(2,1)S(1)}, u32[]{:S(2)}, u32[]{:S(2)}) collective-permute-start(bf16[1,4,128,256]{3,2,1,0:T(8,128)(2,1)S(1)} %get-tuple-element.45), channel_id=1, source_target_pairs={{0,32},{32,0},{64,96},{96,64},{1,33},{33,1},{65,97},{97,65},{2,34}... | collective-permute-start | bytes 786440 | tf_op jit(solution)/shard_map/ppermute | solution.py:553
  54.9 13.0 %collective-permute-start.4 = (bf16[1,4,128,256]{3,2,1,0:T(8,128)(2,1)S(1)}, bf16[1,4,128,256]{3,2,1,0:T(8,128)(2,1)S(1)}, u32[]{:S(2)}, u32[]{:S(2)}) collective-permute-start(bf16[1,4,128,256]{3,2,1,0:T(8,128)(2,1)S(1)} %get-tuple-element.44), channel_id=1, source_target_pairs={{0,96},{32,64},{64,32},{96,0},{1,97},{33,65},{65,33},{97,1},{2,98}... | collective-permute-start | bytes 786440 | tf_op jit(solution)/shard_map/ppermute | solution.py:552
  57.7 17.3 %collective-permute-start.7 = (bf16[4,1,128,256]{3,2,1,0:T(8,128)(2,1)S(1)}, bf16[4,1,128,256]{3,2,1,0:T(8,128)(2,1)S(1)}, u32[]{:S(2)}, u32[]{:S(2)}) collective-permute-start(bf16[4,1,128,256]{3,2,1,0:T(8,128)(2,1)S(1)} %get-tuple-element.53), channel_id=1, source_target_pairs={{0,1},{1,0},{2,3},{3,2},{4,5},{5,4},{6,7},{7,6},{8,9},{9,8},{10,11... | collective-permute-start | bytes 786440 | tf_op jit(solution)/shard_map/ppermute | solution.py:558
  59.3 15.8 %collective-permute-start.8 = (bf16[4,1,128,256]{3,2,1,0:T(8,128)(2,1)S(1)}, bf16[4,1,128,256]{3,2,1,0:T(8,128)(2,1)S(1)}, u32[]{:S(2)}, u32[]{:S(2)}) collective-permute-start(bf16[4,1,128,256]{3,2,1,0:T(8,128)(2,1)S(1)} %get-tuple-element.54), channel_id=1, source_target_pairs={{0,31},{1,2},{2,1},{3,4},{4,3},{5,6},{6,5},{7,8},{8,7},{9,10},{10,... | collective-permute-start | bytes 786440 | tf_op jit(solution)/shard_map/ppermute | solution.py:559
  65.9 4.7 %copy-start.6 = (bf16[256]{0:T(256)(128)(2,1)S(1)}, bf16[256]{0:T(256)(128)(2,1)}, u32[]{:S(2)}) copy-start(bf16[256]{0:T(256)(128)(2,1)} %param.16) | copy-start | bytes 1540
  68.0 7.1 %collective-permute-start.9 = (bf16[2,128,256]{2,1,0:T(8,128)(2,1)S(1)}, bf16[2,128,256]{2,1,0:T(8,128)(2,1)S(1)}, u32[]{:S(2)}, u32[]{:S(2)}) collective-permute-start(bf16[2,128,256]{2,1,0:T(8,128)(2,1)S(1)} %pad_maximum_fusion.1), channel_id=1, source_target_pairs={{0,1},{1,0},{2,3},{3,2},{4,5},{5,4},{6,7},{7,6},{8,9},{9,8},{10,11... | collective-permute-start | bytes 393224 | tf_op jit(solution)/shard_map/ppermute | solution.py:571
  68.2 8.7 %collective-permute-start.10 = (bf16[2,128,256]{2,1,0:T(8,128)(2,1)S(1)}, bf16[2,128,256]{2,1,0:T(8,128)(2,1)S(1)}, u32[]{:S(2)}, u32[]{:S(2)}) collective-permute-start(bf16[2,128,256]{2,1,0:T(8,128)(2,1)S(1)} %pad_maximum_fusion), channel_id=1, source_target_pairs={{0,31},{1,2},{2,1},{3,4},{4,3},{5,6},{6,5},{7,8},{8,7},{9,10},{10,... | collective-permute-start | bytes 393224 | tf_op jit(solution)/shard_map/ppermute | solution.py:571
  70.6 6.3 %copy-start.2 = (bf16[4,4,128,256]{3,2,1,0:T(8,128)(2,1)S(1)}, bf16[4,4,128,256]{3,2,1,0:T(8,128)(2,1)}, u32[]{:S(2)}) copy-start(bf16[4,4,128,256]{3,2,1,0:T(8,128)(2,1)} %cotangent_ref.1) | copy-start | bytes 3145732
  89.3 4.0 %collective-permute-start.11 = (bf16[32,8,16,128]{3,2,1,0:T(8,128)(2,1)S(1)}, bf16[32,8,16,128]{3,2,1,0:T(8,128)(2,1)S(1)}, u32[]{:S(2)}, u32[]{:S(2)}) collective-permute-start(bf16[32,8,16,128]{3,2,1,0:T(8,128)(2,1)S(1)} %get-tuple-element.57), channel_id=1, source_target_pairs={{0,32},{32,0},{64,96},{96,64},{1,33},{33,1},{65,97},{97,65},{2,34}... | collective-permute-start | bytes 3145736 | tf_op jit(solution)/shard_map/ppermute | solution.py:445
  98.5 4.8 %collective-permute-start.18 = (bf16[32,6,16,128]{3,2,1,0:T(8,128)(2,1)S(1)}, bf16[32,6,16,128]{3,2,1,0:T(8,128)(2,1)S(1)}, u32[]{:S(2)}, u32[]{:S(2)}) collective-permute-start(bf16[32,6,16,128]{3,2,1,0:T(8,128)(2,1)S(1)} %get-tuple-element.63), channel_id=1, source_target_pairs={{0,32},{32,0},{64,96},{96,64},{1,33},{33,1},{65,97},{97,65},{2,34}... | collective-permute-start | bytes 2359304 | tf_op jit(solution)/shard_map/ppermute | solution.py:445
  99.1 7.9 %collective-permute-start.12 = (bf16[2,4,8,16,128]{4,3,2,1,0:T(8,128)(2,1)S(1)}, bf16[2,4,8,16,128]{4,3,2,1,0:T(8,128)(2,1)S(1)}, u32[]{:S(2)}, u32[]{:S(2)}) collective-permute-start(bf16[2,4,8,16,128]{4,3,2,1,0:T(8,128)(2,1)S(1)} %get-tuple-element.68), channel_id=1, source_target_pairs={{0,1},{1,0},{2,3},{3,2},{4,5},{5,4},{6,7},{7,6},{8,9},{9,8},{10,11... | collective-permute-start | bytes 786440 | tf_op jit(solution)/shard_map/ppermute | solution.py:455
  100.4 14.9 %collective-permute-start.13 = (bf16[2,4,8,16,128]{4,3,2,1,0:T(8,128)(2,1)S(1)}, bf16[2,4,8,16,128]{4,3,2,1,0:T(8,128)(2,1)S(1)}, u32[]{:S(2)}, u32[]{:S(2)}) collective-permute-start(bf16[2,4,8,16,128]{4,3,2,1,0:T(8,128)(2,1)S(1)} %get-tuple-element.70), channel_id=1, source_target_pairs={{0,2},{1,3},{2,0},{3,1},{4,6},{5,7},{6,4},{7,5},{8,10},{9,11},{10,... | collective-permute-start | bytes 786440 | tf_op jit(solution)/shard_map/ppermute | solution.py:455
  103.3 14.0 %collective-permute-start.14 = (bf16[2,4,8,16,128]{4,3,2,1,0:T(8,128)(2,1)S(1)}, bf16[2,4,8,16,128]{4,3,2,1,0:T(8,128)(2,1)S(1)}, u32[]{:S(2)}, u32[]{:S(2)}) collective-permute-start(bf16[2,4,8,16,128]{4,3,2,1,0:T(8,128)(2,1)S(1)} %get-tuple-element.69), channel_id=1, source_target_pairs={{0,3},{1,2},{2,1},{3,0},{4,7},{5,6},{6,5},{7,4},{8,11},{9,10},{10,... | collective-permute-start | bytes 786440 | tf_op jit(solution)/shard_map/ppermute | solution.py:455
  103.6 14.6 %collective-permute-start.19 = (bf16[2,4,6,16,128]{4,3,2,1,0:T(8,128)(2,1)S(1)}, bf16[2,4,6,16,128]{4,3,2,1,0:T(8,128)(2,1)S(1)}, u32[]{:S(2)}, u32[]{:S(2)}) collective-permute-start(bf16[2,4,6,16,128]{4,3,2,1,0:T(8,128)(2,1)S(1)} %get-tuple-element.71), channel_id=1, source_target_pairs={{0,4},{1,5},{2,6},{3,7},{4,0},{5,1},{6,2},{7,3},{8,12},{9,13},{10,... | collective-permute-start | bytes 589832 | tf_op jit(solution)/shard_map/ppermute | solution.py:455
  104.7 16.7 %collective-permute-start.20 = (bf16[2,4,6,16,128]{4,3,2,1,0:T(8,128)(2,1)S(1)}, bf16[2,4,6,16,128]{4,3,2,1,0:T(8,128)(2,1)S(1)}, u32[]{:S(2)}, u32[]{:S(2)}) collective-permute-start(bf16[2,4,6,16,128]{4,3,2,1,0:T(8,128)(2,1)S(1)} %get-tuple-element.73), channel_id=1, source_target_pairs={{0,8},{1,9},{2,10},{3,11},{4,12},{5,13},{6,14},{7,15},{8,0},{9,1},... | collective-permute-start | bytes 589832 | tf_op jit(solution)/shard_map/ppermute | solution.py:455
  106.9 14.5 %collective-permute-start.21 = (bf16[2,4,6,16,128]{4,3,2,1,0:T(8,128)(2,1)S(1)}, bf16[2,4,6,16,128]{4,3,2,1,0:T(8,128)(2,1)S(1)}, u32[]{:S(2)}, u32[]{:S(2)}) collective-permute-start(bf16[2,4,6,16,128]{4,3,2,1,0:T(8,128)(2,1)S(1)} %get-tuple-element.72), channel_id=1, source_target_pairs={{0,12},{1,13},{2,14},{3,15},{4,8},{5,9},{6,10},{7,11},{8,4},{9,5},... | collective-permute-start | bytes 589832 | tf_op jit(solution)/shard_map/ppermute | solution.py:455
  117.5 5.7 %collective-permute-start.15 = (bf16[2,8,16,128]{3,2,1,0:T(8,128)(2,1)S(1)}, bf16[2,8,16,128]{3,2,1,0:T(8,128)(2,1)S(1)}, u32[]{:S(2)}, u32[]{:S(2)}) collective-permute-start(bf16[2,8,16,128]{3,2,1,0:T(8,128)(2,1)S(1)} %get-tuple-element.74), channel_id=1, source_target_pairs={{0,4},{1,5},{2,6},{3,7},{4,0},{5,1},{6,2},{7,3},{8,12},{9,13},{10,... | collective-permute-start | bytes 196616 | tf_op jit(solution)/shard_map/ppermute | solution.py:455
  117.6 7.9 %collective-permute-start.16 = (bf16[2,8,16,128]{3,2,1,0:T(8,128)(2,1)S(1)}, bf16[2,8,16,128]{3,2,1,0:T(8,128)(2,1)S(1)}, u32[]{:S(2)}, u32[]{:S(2)}) collective-permute-start(bf16[2,8,16,128]{3,2,1,0:T(8,128)(2,1)S(1)} %get-tuple-element.76), channel_id=1, source_target_pairs={{0,8},{1,9},{2,10},{3,11},{4,12},{5,13},{6,14},{7,15},{8,0},{9,1},... | collective-permute-start | bytes 196616 | tf_op jit(solution)/shard_map/ppermute | solution.py:455
  118.2 7.3 %collective-permute-start.17 = (bf16[2,8,16,128]{3,2,1,0:T(8,128)(2,1)S(1)}, bf16[2,8,16,128]{3,2,1,0:T(8,128)(2,1)S(1)}, u32[]{:S(2)}, u32[]{:S(2)}) collective-permute-start(bf16[2,8,16,128]{3,2,1,0:T(8,128)(2,1)S(1)} %get-tuple-element.75), channel_id=1, source_target_pairs={{0,12},{1,13},{2,14},{3,15},{4,8},{5,9},{6,10},{7,11},{8,4},{9,5},... | collective-permute-start | bytes 196616 | tf_op jit(solution)/shard_map/ppermute | solution.py:455
  121.6 4.0 %collective-permute-start.22 = (bf16[2,6,16,128]{3,2,1,0:T(8,128)(2,1)S(1)}, bf16[2,6,16,128]{3,2,1,0:T(8,128)(2,1)S(1)}, u32[]{:S(2)}, u32[]{:S(2)}) collective-permute-start(bf16[2,6,16,128]{3,2,1,0:T(8,128)(2,1)S(1)} %get-tuple-element.85), channel_id=1, source_target_pairs={{0,1},{1,0},{2,3},{3,2},{4,5},{5,4},{6,7},{7,6},{8,9},{9,8},{10,11... | collective-permute-start | bytes 147464 | tf_op jit(solution)/shard_map/ppermute | solution.py:455
  121.7 4.5 %collective-permute-start.23 = (bf16[2,6,16,128]{3,2,1,0:T(8,128)(2,1)S(1)}, bf16[2,6,16,128]{3,2,1,0:T(8,128)(2,1)S(1)}, u32[]{:S(2)}, u32[]{:S(2)}) collective-permute-start(bf16[2,6,16,128]{3,2,1,0:T(8,128)(2,1)S(1)} %get-tuple-element.87), channel_id=1, source_target_pairs={{0,2},{1,3},{2,0},{3,1},{4,6},{5,7},{6,4},{7,5},{8,10},{9,11},{10,... | collective-permute-start | bytes 147464 | tf_op jit(solution)/shard_map/ppermute | solution.py:455
  123.1 4.2 %collective-permute-start.24 = (bf16[2,6,16,128]{3,2,1,0:T(8,128)(2,1)S(1)}, bf16[2,6,16,128]{3,2,1,0:T(8,128)(2,1)S(1)}, u32[]{:S(2)}, u32[]{:S(2)}) collective-permute-start(bf16[2,6,16,128]{3,2,1,0:T(8,128)(2,1)S(1)} %get-tuple-element.86), channel_id=1, source_target_pairs={{0,3},{1,2},{2,1},{3,0},{4,7},{5,6},{6,5},{7,4},{8,11},{9,10},{10,... | collective-permute-start | bytes 147464 | tf_op jit(solution)/shard_map/ppermute | solution.py:455
  127.4 3.4 %collective-permute-start.25 = (bf16[14,16,128]{2,1,0:T(8,128)(2,1)S(1)}, bf16[14,16,128]{2,1,0:T(8,128)(2,1)S(1)}, u32[]{:S(2)}, u32[]{:S(2)}) collective-permute-start(bf16[14,16,128]{2,1,0:T(8,128)(2,1)S(1)} %get-tuple-element.83), channel_id=1, source_target_pairs={{0,16},{1,17},{2,18},{3,19},{4,20},{5,21},{6,22},{7,23},{8,24},{9,... | collective-permute-start | bytes 172040 | tf_op jit(solution)/shard_map/ppermute | solution.py:594
  128.4 4.2 %collective-permute-start.26 = (bf16[14,16,128]{2,1,0:T(8,128)(2,1)S(1)}, bf16[14,16,128]{2,1,0:T(8,128)(2,1)S(1)}, u32[]{:S(2)}, u32[]{:S(2)}) collective-permute-start(bf16[14,16,128]{2,1,0:T(8,128)(2,1)S(1)} %get-tuple-element.83), channel_id=1, source_target_pairs={{0,80},{1,81},{2,82},{3,83},{4,84},{5,85},{6,86},{7,87},{8,88},{9,... | collective-permute-start | bytes 172040 | tf_op jit(solution)/shard_map/ppermute | solution.py:595
  130.3 4.5 %collective-permute-start.27 = (bf16[14,16,128]{2,1,0:T(8,128)(2,1)S(1)}, bf16[14,16,128]{2,1,0:T(8,128)(2,1)S(1)}, u32[]{:S(2)}, u32[]{:S(2)}) collective-permute-start(bf16[14,16,128]{2,1,0:T(8,128)(2,1)S(1)} %get-tuple-element.84), channel_id=1, source_target_pairs={{0,64},{32,96},{64,0},{96,32},{1,65},{33,97},{65,1},{97,33},{2,66}... | collective-permute-start | bytes 172040 | tf_op jit(solution)/shard_map/ppermute | solution.py:596
  134.9 6.6 %collective-permute-start.28 = (f32[14,16,128]{2,1,0:T(8,128)S(1)}, f32[14,16,128]{2,1,0:T(8,128)S(1)}, u32[]{:S(2)}, u32[]{:S(2)}) collective-permute-start(f32[14,16,128]{2,1,0:T(8,128)S(1)} %convert_add_fusion.3), channel_id=1, source_target_pairs={{0,32},{32,0},{64,96},{96,64},{1,33},{33,1},{65,97},{97,65},{2,34}... | collective-permute-start | bytes 344072 | tf_op jit(solution)/shard_map/ppermute | solution.py:598

commit v5 on v4

--- a/solution.py
+++ b/solution.py
@@ -13,44 +13,54 @@
 BRIEF = pl.CostEstimate(flops=1, bytes_accessed=1, transcendentals=0)
 
 
-def send_kernel(scalars_ref, slots_ref, feats_ref, *out_refs):
+def listed_rows(slots, feats_ref, out_ref):
     points = feats_ref.shape[0]
     point_ids = lax.broadcasted_iota(jnp.int32, (128, points), 1)
+    columns = slots.T
+    for half in range(2):
+        hot = [
+            jnp.where(point_ids == columns[:, r : r + 1], 1.0, 0.0).astype(BF)
+            for r in range(half * 4, half * 4 + 4)
+        ]
+        rows = jnp.dot(
+            jnp.concatenate(hot, axis=0), feats_ref[...], preferred_element_type=F32
+        )
+        out_ref[half * 512 : half * 512 + 512, :] = rows.astype(BF)
+
+
+def send_kernel(owners_ref, slots_ref, feats_ref, *out_refs):
     for place, out_ref in enumerate(out_refs):
-        owner = scalars_ref[place]
-        columns = slots_ref[owner].T
-        for half in range(2):
-            hot = [
-                jnp.where(point_ids == columns[:, r : r + 1], 1.0, 0.0).astype(BF)
-                for r in range(half * 4, half * 4 + 4)
-            ]
-            rows = jnp.dot(
-                jnp.concatenate(hot, axis=0), feats_ref[...], preferred_element_type=F32
-            )
-            out_ref[half * 512 : half * 512 + 512, :] = rows.astype(BF)
-
-
-def gather_listed(feats, slots, scalars):
-    capacity = slots.shape[1] * slots.shape[2]
-    channels = feats.shape[1]
+        listed_rows(slots_ref[owners_ref[place + 1]], feats_ref, out_ref)
+
+
+def gather_listed(feats, slots, owners):
+    count, rows, lanes = slots.shape
     whole = pl.BlockSpec(memory_space=pltpu.VMEM)
     return pl.pallas_call(
         send_kernel,
         in_specs=[pl.BlockSpec(memory_space=pltpu.SMEM), whole, whole],
-        out_specs=[whole] * 2,
-        out_shape=[jax.ShapeDtypeStruct((capacity, channels), BF)] * 2,
+        out_specs=[whole] * (count - 1),
+        out_shape=[jax.ShapeDtypeStruct((rows * lanes, feats.shape[1]), BF)] * (count - 1),
         compiler_params=pltpu.CompilerParams(vmem_limit_bytes=16 << 20),
         cost_estimate=BRIEF,
-    )(scalars, slots, feats)
-
-
-def spread_kernel(fill_ref, near_ref, place_ref, t0, t1, out_ref, part_ref, denom_ref, close):
+    )(owners, slots, feats)
+
+
+def spread_kernel(
+    fill_ref, owners_ref, near_ref, place_ref, slots_ref, feats_ref, t1,
+    out_ref, part_ref, denom_ref, close, t0,
+):
     plane = pl.program_id(0)
     tiles = near_ref.shape[1]
     slots = near_ref.shape[2]
     groups = (out_ref.shape[1] + close.shape[1]) // 256
     split = close.shape[1]
     capacity = t0.shape[0]
+
+    @pl.when(plane == 0)
+    def _():
+        listed_rows(slots_ref[owners_ref[0]], feats_ref, t0)
+
     cell = lax.broadcasted_iota(jnp.int32, (16, slots), 0)
     centre_x = (cell // 4).astype(F32) - 1.5
     centre_y = (cell % 4).astype(F32) - 1.5
@@ -92,19 +102,24 @@
     ) + jnp.dot(close[:, capacity:], t1[...], preferred_element_type=F32)
 
 
-def spread_weights(near, fill, place, tables):
+def spread_weights(near, fill, place, owners, listed, feats, table):
     planes, tiles, slots = near.shape
-    capacity, channels = tables[0].shape
+    capacity, channels = table.shape
     rows = 2 * capacity
     return pl.pallas_call(
         spread_kernel,
         grid=(planes,),
         in_specs=[
             pl.BlockSpec(memory_space=pltpu.SMEM),
+            pl.BlockSpec(memory_space=pltpu.SMEM),
             pl.BlockSpec((1, tiles, slots), lambda z: (z, 0, 0)),
             pl.BlockSpec((1, 3, tiles, slots), lambda z: (z, 0, 0, 0)),
         ]
-        + [pl.BlockSpec((capacity, channels), lambda z: (0, 0))] * 2,
+        + [
+            pl.BlockSpec(listed.shape, lambda z: (0, 0, 0)),
+            pl.BlockSpec(feats.shape, lambda z: (0, 0)),
+            pl.BlockSpec((capacity, channels), lambda z: (0, 0)),
+        ],
         out_specs=[
             pl.BlockSpec((tiles * 16, rows), lambda z: (z, 0)),
             pl.BlockSpec((tiles * 16, channels), lambda z: (z, 0)),
@@ -115,9 +130,12 @@
             jax.ShapeDtypeStruct((planes * tiles * 16, channels), F32),
             jax.ShapeDtypeStruct((planes * tiles * 16, 128), F32),
         ],
-        scratch_shapes=[pltpu.VMEM((tiles * 16, rows), BF)],
-        compiler_params=pltpu.CompilerParams(vmem_limit_bytes=16 << 20),
-    )(fill, near, place, *tables)
+        scratch_shapes=[
+            pltpu.VMEM((tiles * 16, rows), BF),
+            pltpu.VMEM((capacity, channels), BF),
+        ],
+        compiler_params=pltpu.CompilerParams(vmem_limit_bytes=22 << 20),
+    )(fill, owners, near, place, listed, feats, table)
 
 
 def latent_kernel(
@@ -519,11 +537,12 @@
     capacity = slots.shape[1]
     listed = jnp.arange(capacity, dtype=jnp.int32) < counts[:, None]
     slots = jnp.where(listed, slots, -1).reshape(spaces, capacity // 128, 128)
-    scalars = (space ^ jnp.arange(spaces, dtype=jnp.int32)).reshape(2, 2)
-    to_far, to_cross = gather_listed(point_feats, slots, scalars[1])
+    owners = space ^ jnp.arange(spaces, dtype=jnp.int32)
+    to_other, to_far, to_cross = gather_listed(point_feats, slots, owners)
     to_far, to_cross, gathered = lax.optimization_barrier((to_far, to_cross, gathered))
     from_far = lax.ppermute(to_far, "space", far)
     from_cross = lax.ppermute(to_cross, "space", cross)
+    from_other = lax.ppermute(to_other, "space", swap)
     gathered = jnp.broadcast_to(gathered[None], (16,) + gathered.shape)
     gathered = lax.all_to_all(
         gathered,
@@ -533,16 +552,15 @@
         axis_index_groups=[[16 * y + i for i in range(16)] for y in range(chans // 16)],
         tiled=True,
     )
-    held_scalars, _ = lax.optimization_barrier((scalars[0], to_far))
-    to_self, to_other = gather_listed(point_feats, slots, held_scalars)
-    from_other = lax.ppermute(to_other, "space", swap)
-
-    near, _ = lax.optimization_barrier((neighbors[:, 0], to_self))
+    near, _ = lax.optimization_barrier((neighbors[:, 0], to_far))
     spread, close_part, denom = spread_weights(
         near ^ (space * capacity),
         tile_fill[:, 0],
         offsets[:, 0].transpose(0, 2, 1, 3),
-        (to_self, from_other),
+        owners,
+        slots,
+        point_feats,
+        from_other,
     )
 
     latent, near_plane, far_plane, first_row, second_row = latent_block(

time: 143 us -> 140 us (0.979)
    pallas_call x2 -> x1, Pallas kernels: 6.99 us -> 4.25 us  [gather_listed(): pl.pallas_call(send_kernel, in_specs=[pl.BlockSpec(memory_space=pltpu.SME...]
    ppermute x1, waiting for transfers between devices: 9.81 us -> 8.32 us  [on_device(): from_cross = lax.ppermute(to_cross, 'space', cross)]
where the time goes in v5:
time: 140 us
  starting transfers between devices  52.9 us (38%)
  Pallas kernels  47.4 us (34%)
  waiting for transfers between devices  28.6 us (20%)
  other arithmetic  5.26 us (4%)
  local copies, waits for them, and re-layouts  4.34 us (3%)
    ppermute x12, starting transfers between devices, sum_over(): lax.ppermute(part, 'chan', [(i, i ^ offset * step) for i in range(chans)])  16.4 us
    pallas_call x1, Pallas kernels, spread_weights(): pl.pallas_call(spread_kernel, grid=(planes,), in_specs=[pl.BlockSpec(memo...  14.9 us
    pallas_call x1, Pallas kernels, outer_conv(): pl.pallas_call(outer_kernel, in_specs=[pl.BlockSpec(memory_space=pltpu.SM...  12.5 us
    ppermute x12, waiting for transfers between devices, sum_over(): lax.ppermute(part, 'chan', [(i, i ^ offset * step) for i in range(chans)])  11.2 us
    ppermute x1, waiting for transfers between devices, on_device(): from_cross = lax.ppermute(to_cross, 'space', cross)  8.32 us
    all_to_all x1, starting transfers between devices, on_device(): lax.all_to_all(gathered, 'chan', split_axis=0, concat_axis=0, axis_index_...  7.78 us
    pallas_call x2, Pallas kernels, inner_conv(): pl.pallas_call(functools.partial(inner_kernel, chosen), in_specs=[whole]...  6.49 us
    ppermute x1, starting transfers between devices, on_device(): lax.ppermute(own_sum, 'space', swap)  5.61 us
  transfers between devices with their start and end apart: 30, of which 11 were waited for; matrix products, arithmetic and copies ran while one was open for 3% of the time, Pallas kernels for 22%

profile of v5, /device:TPU:1, one launch (start us, length us, event | category | flops | bytes accessed | tf_op | source)
XLA Modules:
  0.0 139.6 jit_solution(1586362925822777461)
XLA Ops:
  0.7 0.8 bitcast_dynamic-update-slice_fusion.1
  1.5 2.2 %collective-permute-start = (bf16[14,8,256]{2,1,0:T(8,128)(2,1)S(1)}, bf16[14,8,256]{2,1,0:T(8,128)(2,1)S(1)}, u32[]{:S(2)}, u32[]{:S(2)}) collective-permute-start(bf16[14,8,256]{2,1,0:T(8,128)(2,1)S(1)} %get-tuple-element.61), channel_id=1, source_target_pairs={{0,16},{1,17},{2,18},{3,19},{4,20},{5,21},{6,22},{7,23},{8,24},{9,... | collective-permute-start | bytes 172040 | tf_op jit(solution)/shard_map/ppermute | solution.py:482
  3.7 0.8 bitcast_select_fusion.slots_ref
  4.5 1.2 copy-done
  5.7 4.2 %shard_map.104 = (bf16[1024,256]{1,0:T(8,128)(2,1)}, bf16[1024,256]{1,0:T(8,128)(2,1)}, bf16[1024,256]{1,0:T(8,128)(2,1)S(1)}) custom-call(s32[4]{0:T(128)S(1)} %iota_xor_fusion.owners_ref, s32[4,8,128]{2,1,0:T(8,128)S(1)} %bitcast_select_fusion.slots_ref, bf16[2048,256]{1,0:T(8,128)(2,1)S(1)} %copy-done), custom_call_target="tpu_custom_call" | custom-call | flops 1 | bytes 1 | tf_op jit(solution)/shard_map/pallas_call | solution.py:39
  10.0 1.4 %broadcast_in_dim.30 = bf16[16,2,14,8,256]{4,3,1,2,0:T(8,128)(2,1)} broadcast(bf16[2,14,8,256]{3,2,0,1:T(8,128)(2,1)S(1)} %bitcast_dynamic-update-slice_fusion), dimensions={1,2,3,4} | broadcast | bytes 1949696 | tf_op jit(solution)/shard_map/broadcast_in_dim | solution.py:546
  11.5 7.8 %all-to-all-start = ((bf16[16,2,14,8,256]{4,3,1,2,0:T(8,128)(2,1)}), bf16[16,2,14,8,256]{4,3,1,2,0:T(8,128)(2,1)}, u32[]{:S(2)}, u32[]{:S(2)}) async-start(bf16[16,2,14,8,256]{4,3,1,2,0:T(8,128)(2,1)} %broadcast_in_dim.30), calls=%async_computation | async-start | bytes 3670016 | tf_op jit(solution)/shard_map/all_to_all | solution.py:547
  19.2 1.3 collective-permute-start.1
  20.6 2.6 %collective-permute-start.2 = (bf16[1024,256]{1,0:T(8,128)(2,1)}, bf16[1024,256]{1,0:T(8,128)(2,1)S(1)}, u32[]{:S(2)}, u32[]{:S(2)}) collective-permute-start(bf16[1024,256]{1,0:T(8,128)(2,1)} %get-tuple-element.33), channel_id=1, source_target_pairs={{0,64},{32,96},{64,0},{96,32},{1,65},{33,97},{65,1},{97,33},{2,66}... | collective-permute-start | bytes 1572872 | tf_op jit(solution)/shard_map/ppermute | solution.py:543
  23.2 0.6 collective-permute-start.3
  23.9 14.9 %shard_map.105 = (bf16[2048,2048]{1,0:T(8,128)(2,1)S(1)}, f32[2048,256]{1,0:T(8,128)S(1)}, f32[2048,128]{1,0:T(8,128)S(1)}) custom-call(s32[4,32]{1,0:T(4,128)S(1)} %bitcast.93, s32[4]{0:T(128)S(1)} %iota_xor_fusion.owners_ref, s32[4,32,128]{2,1,0:T(8,128)S(1)} %broadcast_xor_fusion.near_ref, f32[4,3,32,128]{3,2,1,0:T(8,128)S(1)} %bitcast.92, ...), custom_call_target="tpu_custom_call" | custom-call | tf_op jit(solution)/shard_map/pallas_call | solution.py:109
  38.9 8.3 %collective-permute-done.3.t1 = bf16[1024,256]{1,0:T(8,128)(2,1)S(1)} collective-permute-done((bf16[1024,256]{1,0:T(8,128)(2,1)S(1)}, bf16[1024,256]{1,0:T(8,128)(2,1)S(1)}, u32[]{:S(2)}, u32[]{:S(2)}) %collective-permute-start.3) | collective-permute-done | bytes 524320 | tf_op jit(solution)/shard_map/ppermute | solution.py:544
  47.2 4.5 %shard_map.106 = (bf16[4,4,128,256]{3,2,1,0:T(8,128)(2,1)S(1)}, bf16[1,4,128,256]{3,2,1,0:T(8,128)(2,1)S(1)}, bf16[1,4,128,256]{3,2,1,0:T(8,128)(2,1)S(1)}, bf16...) custom-call(s32[4]{0:T(128)S(1)} %pad_add_fusion.flags_ref, ...), custom_call_target="tpu_custom_call" | custom-call | tf_op jit(solution)/shard_map/pallas_call | solution.py:189
  52.2 2.7 %collective-permute-start.4 = (bf16[1,4,128,256]{3,2,1,0:T(8,128)(2,1)S(1)}, bf16[1,4,128,256]{3,2,1,0:T(8,128)(2,1)S(1)}, u32[]{:S(2)}, u32[]{:S(2)}) collective-permute-start(bf16[1,4,128,256]{3,2,1,0:T(8,128)(2,1)S(1)} %get-tuple-element.40), channel_id=1, source_target_pairs={{0,96},{32,64},{64,32},{96,0},{1,97},{33,65},{65,33},{97,1},{2,98}... | collective-permute-start | bytes 786440 | tf_op jit(solution)/shard_map/ppermute | solution.py:570
  54.9 1.5 %collective-permute-start.7 = (bf16[4,1,128,256]{3,2,1,0:T(8,128)(2,1)S(1)}, bf16[4,1,128,256]{3,2,1,0:T(8,128)(2,1)S(1)}, u32[]{:S(2)}, u32[]{:S(2)}) collective-permute-start(bf16[4,1,128,256]{3,2,1,0:T(8,128)(2,1)S(1)} %get-tuple-element.49), channel_id=1, source_target_pairs={{0,1},{1,0},{2,3},{3,2},{4,5},{5,4},{6,7},{7,6},{8,9},{9,8},{10,11... | collective-permute-start | bytes 786440 | tf_op jit(solution)/shard_map/ppermute | solution.py:576
  56.5 3.5 %collective-permute-start.8 = (bf16[4,1,128,256]{3,2,1,0:T(8,128)(2,1)S(1)}, bf16[4,1,128,256]{3,2,1,0:T(8,128)(2,1)S(1)}, u32[]{:S(2)}, u32[]{:S(2)}) collective-permute-start(bf16[4,1,128,256]{3,2,1,0:T(8,128)(2,1)S(1)} %get-tuple-element.50), channel_id=1, source_target_pairs={{0,31},{1,2},{2,1},{3,4},{4,3},{5,6},{6,5},{7,8},{8,7},{9,10},{10,... | collective-permute-start | bytes 786440 | tf_op jit(solution)/shard_map/ppermute | solution.py:577
  60.0 2.3 %select_bitcast_fusion.1 = (bf16[1,16,2,14,8,256]{5,4,2,3,1,0:T(8,128)(2,1)S(1)}, bf16[1,16,2,14,8,256]{5,4,2,3,1,0:T(8,128)(2,1)S(1)}) fusion(bf16[16,2,14,8,256]{4,3,1,2,0:T(8,128)(2,1)} %all-to-all-done, bf16[16,2,14,8,256]{4,3,1,2,0:T(8,128)(2,1)} %collective-permute-done.6, pred[]{:T(512)S(6)} %eq.14), kind=kLoop, calls=%fused_computation.3 | loop fusion | flops 1835008 | bytes 7340033 | tf_op jit(solution)/shard_map/stack | solution.py:573
  62.6 0.5 copy.14
  63.1 2.0 %shard_map.107.middle_ref = f32[1,4,128,256]{3,2,1,0:T(8,128)S(1)} custom-call(bf16[4,4,128,256]{3,2,1,0:T(8,128)(2,1)S(1)} %get-tuple-element.48.latent_ref, bf16[28,256,256]{2,1,0:T(8,128)(2,1)S(1)} %bitcast.89), custom_call_target="tpu_custom_call" | custom-call | flops 1 | bytes 1 | tf_op jit(solution)/shard_map/pallas_call | solution.py:264
  65.3 2.5 %collective-permute-start.10 = (bf16[2,128,256]{2,1,0:T(8,128)(2,1)S(1)}, bf16[2,128,256]{2,1,0:T(8,128)(2,1)S(1)}, u32[]{:S(2)}, u32[]{:S(2)}) collective-permute-start(bf16[2,128,256]{2,1,0:T(8,128)(2,1)S(1)} %pad_maximum_fusion), channel_id=1, source_target_pairs={{0,31},{1,2},{2,1},{3,4},{4,3},{5,6},{6,5},{7,8},{8,7},{9,10},{10,... | collective-permute-start | bytes 393224 | tf_op jit(solution)/shard_map/ppermute | solution.py:589
  67.8 4.5 %shard_map.108.edge_ref = f32[3,4,128,256]{3,2,1,0:T(8,128)S(1)} custom-call(bf16[4,4,128,256]{3,2,1,0:T(8,128)(2,1)S(1)} %get-tuple-element.48.latent_ref, bf16[28,256,256]{2,1,0:T(8,128)(2,1)S(1)} %bitcast.90), custom_call_target="tpu_custom_call" | custom-call | flops 1 | bytes 1 | tf_op jit(solution)/shard_map/pallas_call | solution.py:264
  72.3 1.6 %collective-permute-done.10.second_end_ref = bf16[2,128,256]{2,1,0:T(8,128)(2,1)S(1)} collective-permute-done((bf16[2,128,256]{2,1,0:T(8,128)(2,1)S(1)}, bf16[2,128,256]{2,1,0:T(8,128)(2,1)S(1)}, u32[]{:S(2)}, u32[]{:S(2)}) %collective-permute-start.10) | collective-permute-done | bytes 131104 | tf_op jit(solution)/shard_map/ppermute | solution.py:589
  73.9 12.5 %shard_map.109 = (bf16[4,4,128,256]{3,2,1,0:T(8,128)(2,1)}, bf16[6,256,768]{2,1,0:T(8,128)(2,1)S(1)}, bf16[2048,768]{1,0:T(8,128)(2,1)S(1)}, bf16[32,8,16,128]{3...) custom-call(s32[4]{0:T(128)S(1)} %pad_add_fusion.flags_ref, f32[1,4,128,256]{3,2,1,0:T(8,128)S(1)} %shard_map.107.middle_ref, ...), custom_call_target="tpu_custom_call" | custom-call | tf_op jit(solution)/shard_map/pallas_call | solution.py:423
  86.4 1.8 %collective-permute-start.11 = (bf16[32,8,16,128]{3,2,1,0:T(8,128)(2,1)S(1)}, bf16[32,8,16,128]{3,2,1,0:T(8,128)(2,1)S(1)}, u32[]{:S(2)}, u32[]{:S(2)}) collective-permute-start(bf16[32,8,16,128]{3,2,1,0:T(8,128)(2,1)S(1)} %get-tuple-element.53), channel_id=1, source_target_pairs={{0,32},{32,0},{64,96},{96,64},{1,33},{33,1},{65,97},{97,65},{2,34}... | collective-permute-start | bytes 3145736 | tf_op jit(solution)/shard_map/ppermute | solution.py:463
  88.2 2.3 %collective-permute-done.11 = bf16[32,8,16,128]{3,2,1,0:T(8,128)(2,1)S(1)} collective-permute-done((bf16[32,8,16,128]{3,2,1,0:T(8,128)(2,1)S(1)}, bf16[32,8,16,128]{3,2,1,0:T(8,128)(2,1)S(1)}, u32[]{:S(2)}, u32[]{:S(2)}) %collective-permute-start.11) | collective-permute-done | bytes 1048608 | tf_op jit(solution)/shard_map/ppermute | solution.py:463
  90.9 4.8 %shard_map.110 = (bf16[32,6,16,128]{3,2,1,0:T(8,128)(2,1)S(1)}, bf16[32,6,16,128]{3,2,1,0:T(8,128)(2,1)S(1)}) custom-call(s32[4]{0:T(128)S(1)} %pad_add_fusion.flags_ref, bf16[6,256,768]{2,1,0:T(8,128)(2,1)S(1)} %get-tuple-element.56.turned, bf16[2048,768]{1,0:T(8,128)(2,1)S(1)} %get-tuple-element.57.shifted), custom_call_target="tpu_custom_call" | custom-call | tf_op jit(solution)/shard_map/pallas_call | solution.py:453
  95.7 0.5 collective-permute-start.18
  96.4 1.3 collective-permute-start.12
  97.7 3.0 %collective-permute-start.13 = (bf16[2,4,8,16,128]{4,3,2,1,0:T(8,128)(2,1)S(1)}, bf16[2,4,8,16,128]{4,3,2,1,0:T(8,128)(2,1)S(1)}, u32[]{:S(2)}, u32[]{:S(2)}) collective-permute-start(bf16[2,4,8,16,128]{4,3,2,1,0:T(8,128)(2,1)S(1)} %get-tuple-element.66), channel_id=1, source_target_pairs={{0,2},{1,3},{2,0},{3,1},{4,6},{5,7},{6,4},{7,5},{8,10},{9,11},{10,... | collective-permute-start | bytes 786440 | tf_op jit(solution)/shard_map/ppermute | solution.py:473
  100.9 1.0 collective-permute-start.19
  101.9 1.6 %collective-permute-start.20 = (bf16[2,4,6,16,128]{4,3,2,1,0:T(8,128)(2,1)S(1)}, bf16[2,4,6,16,128]{4,3,2,1,0:T(8,128)(2,1)S(1)}, u32[]{:S(2)}, u32[]{:S(2)}) collective-permute-start(bf16[2,4,6,16,128]{4,3,2,1,0:T(8,128)(2,1)S(1)} %get-tuple-element.69), channel_id=1, source_target_pairs={{0,8},{1,9},{2,10},{3,11},{4,12},{5,13},{6,14},{7,15},{8,0},{9,1},... | collective-permute-start | bytes 589832 | tf_op jit(solution)/shard_map/ppermute | solution.py:473
  103.5 0.7 collective-permute-done.12
  104.2 1.7 %collective-permute-start.21 = (bf16[2,4,6,16,128]{4,3,2,1,0:T(8,128)(2,1)S(1)}, bf16[2,4,6,16,128]{4,3,2,1,0:T(8,128)(2,1)S(1)}, u32[]{:S(2)}, u32[]{:S(2)}) collective-permute-start(bf16[2,4,6,16,128]{4,3,2,1,0:T(8,128)(2,1)S(1)} %get-tuple-element.68), channel_id=1, source_target_pairs={{0,12},{1,13},{2,14},{3,15},{4,8},{5,9},{6,10},{7,11},{8,4},{9,5},... | collective-permute-start | bytes 589832 | tf_op jit(solution)/shard_map/ppermute | solution.py:473
  105.9 6.7 %collective-permute-done.13 = bf16[2,4,8,16,128]{4,3,2,1,0:T(8,128)(2,1)S(1)} collective-permute-done((bf16[2,4,8,16,128]{4,3,2,1,0:T(8,128)(2,1)S(1)}, bf16[2,4,8,16,128]{4,3,2,1,0:T(8,128)(2,1)S(1)}, u32[]{:S(2)}, u32[]{:S(2)}) %collective-permute-start.13) | collective-permute-done | bytes 262176 | tf_op jit(solution)/shard_map/ppermute | solution.py:473
  112.6 2.0 %collective-permute-done.14 = bf16[2,4,8,16,128]{4,3,2,1,0:T(8,128)(2,1)S(1)} collective-permute-done((bf16[2,4,8,16,128]{4,3,2,1,0:T(8,128)(2,1)S(1)}, bf16[2,4,8,16,128]{4,3,2,1,0:T(8,128)(2,1)S(1)}, u32[]{:S(2)}, u32[]{:S(2)}) %collective-permute-start.14) | collective-permute-done | bytes 262176 | tf_op jit(solution)/shard_map/ppermute | solution.py:473
  114.9 0.6 collective-permute-start.16
  115.5 3.2 %collective-permute-start.17 = (bf16[2,8,16,128]{3,2,1,0:T(8,128)(2,1)S(1)}, bf16[2,8,16,128]{3,2,1,0:T(8,128)(2,1)S(1)}, u32[]{:S(2)}, u32[]{:S(2)}) collective-permute-start(bf16[2,8,16,128]{3,2,1,0:T(8,128)(2,1)S(1)} %get-tuple-element.71), channel_id=1, source_target_pairs={{0,12},{1,13},{2,14},{3,15},{4,8},{5,9},{6,10},{7,11},{8,4},{9,5},... | collective-permute-start | bytes 196616 | tf_op jit(solution)/shard_map/ppermute | solution.py:473
  118.9 1.5 %collective-permute-start.23 = (bf16[2,6,16,128]{3,2,1,0:T(8,128)(2,1)S(1)}, bf16[2,6,16,128]{3,2,1,0:T(8,128)(2,1)S(1)}, u32[]{:S(2)}, u32[]{:S(2)}) collective-permute-start(bf16[2,6,16,128]{3,2,1,0:T(8,128)(2,1)S(1)} %get-tuple-element.83), channel_id=1, source_target_pairs={{0,2},{1,3},{2,0},{3,1},{4,6},{5,7},{6,4},{7,5},{8,10},{9,11},{10,... | collective-permute-start | bytes 147464 | tf_op jit(solution)/shard_map/ppermute | solution.py:473
  120.4 2.4 %collective-permute-start.24 = (bf16[2,6,16,128]{3,2,1,0:T(8,128)(2,1)S(1)}, bf16[2,6,16,128]{3,2,1,0:T(8,128)(2,1)S(1)}, u32[]{:S(2)}, u32[]{:S(2)}) collective-permute-start(bf16[2,6,16,128]{3,2,1,0:T(8,128)(2,1)S(1)} %get-tuple-element.82), channel_id=1, source_target_pairs={{0,3},{1,2},{2,1},{3,0},{4,7},{5,6},{6,5},{7,4},{8,11},{9,10},{10,... | collective-permute-start | bytes 147464 | tf_op jit(solution)/shard_map/ppermute | solution.py:473
  122.9 0.6 collective-permute-done.23
  123.5 1.1 collective-permute-done.24
  124.7 1.1 collective-permute-start.25
  125.7 1.9 %collective-permute-start.26 = (bf16[14,16,128]{2,1,0:T(8,128)(2,1)S(1)}, bf16[14,16,128]{2,1,0:T(8,128)(2,1)S(1)}, u32[]{:S(2)}, u32[]{:S(2)}) collective-permute-start(bf16[14,16,128]{2,1,0:T(8,128)(2,1)S(1)} %get-tuple-element.79), channel_id=1, source_target_pairs={{0,80},{1,81},{2,82},{3,83},{4,84},{5,85},{6,86},{7,87},{8,88},{9,... | collective-permute-start | bytes 172040 | tf_op jit(solution)/shard_map/ppermute | solution.py:613
  128.0 1.9 %collective-permute-done.26 = bf16[14,16,128]{2,1,0:T(8,128)(2,1)S(1)} collective-permute-done((bf16[14,16,128]{2,1,0:T(8,128)(2,1)S(1)}, bf16[14,16,128]{2,1,0:T(8,128)(2,1)S(1)}, u32[]{:S(2)}, u32[]{:S(2)}) %collective-permute-start.26) | collective-permute-done | bytes 57376 | tf_op jit(solution)/shard_map/ppermute | solution.py:613
  130.0 2.2 %collective-permute-done.27 = bf16[14,16,128]{2,1,0:T(8,128)(2,1)S(1)} collective-permute-done((bf16[14,16,128]{2,1,0:T(8,128)(2,1)S(1)}, bf16[14,16,128]{2,1,0:T(8,128)(2,1)S(1)}, u32[]{:S(2)}, u32[]{:S(2)}) %collective-permute-start.27) | collective-permute-done | bytes 57376 | tf_op jit(solution)/shard_map/ppermute | solution.py:614
  132.2 5.6 %collective-permute-start.28 = (f32[14,16,128]{2,1,0:T(8,128)S(1)}, f32[14,16,128]{2,1,0:T(8,128)S(1)}, u32[]{:S(2)}, u32[]{:S(2)}) collective-permute-start(f32[14,16,128]{2,1,0:T(8,128)S(1)} %convert_add_fusion.3), channel_id=1, source_target_pairs={{0,32},{32,0},{64,96},{96,64},{1,33},{33,1},{65,97},{97,65},{2,34}... | collective-permute-start | bytes 344072 | tf_op jit(solution)/shard_map/ppermute | solution.py:616
  137.8 1.0 collective-permute-done.28
  138.9 0.7 fusion.6
  (67 shorter events, 3.2 us)
Async XLA Ops:
  1.5 8.5 %collective-permute-start = (bf16[14,8,256]{2,1,0:T(8,128)(2,1)S(1)}, bf16[14,8,256]{2,1,0:T(8,128)(2,1)S(1)}, u32[]{:S(2)}, u32[]{:S(2)}) collective-permute-start(bf16[14,8,256]{2,1,0:T(8,128)(2,1)S(1)} %get-tuple-element.61), channel_id=1, source_target_pairs={{0,16},{1,17},{2,18},{3,19},{4,20},{5,21},{6,22},{7,23},{8,24},{9,... | collective-permute-start | bytes 172040 | tf_op jit(solution)/shard_map/ppermute | solution.py:482
  4.5 1.2 copy-start
  11.4 12.4 %copy-start.5 = (s32[4,1,32,128]{3,2,1,0:T(8,128)S(1)}, s32[4,1,32,128]{3,2,1,0:T(8,128)}, u32[]{:S(2)}) copy-start(s32[4,1,32,128]{3,2,1,0:T(8,128)} %param.12) | copy-start | bytes 196612
  11.4 12.4 %copy-start.1 = (bf16[2048,256]{1,0:T(8,128)(2,1)S(1)}, bf16[2048,256]{1,0:T(8,128)(2,1)}, u32[]{:S(2)}) copy-start(bf16[2048,256]{1,0:T(8,128)(2,1)} %feats_ref.3) | copy-start | bytes 3145732
  11.4 12.5 %copy-start.3 = (f32[4,1,32,3,128]{4,2,3,1,0:T(8,128)S(1)}, f32[4,1,32,3,128]{4,2,3,1,0:T(8,128)}, u32[]{:S(2)}) copy-start(f32[4,1,32,3,128]{4,2,3,1,0:T(8,128)} %param.14) | copy-start | bytes 589828
  11.4 12.5 %copy-start.4 = (s32[4,1,32]{2,1,0:T(1,128)S(1)}, s32[4,1,32]{2,1,0:T(1,128)}, u32[]{:S(2)}) copy-start(s32[4,1,32]{2,1,0:T(1,128)} %param.13) | copy-start | bytes 1540
  11.5 40.2 %all-to-all-start = ((bf16[16,2,14,8,256]{4,3,1,2,0:T(8,128)(2,1)}), bf16[16,2,14,8,256]{4,3,1,2,0:T(8,128)(2,1)}, u32[]{:S(2)}, u32[]{:S(2)}) async-start(bf16[16,2,14,8,256]{4,3,1,2,0:T(8,128)(2,1)} %broadcast_in_dim.30), calls=%async_computation | async-start | bytes 3670016 | tf_op jit(solution)/shard_map/all_to_all | solution.py:547
  19.2 4.6 %collective-permute-start.1 = (bf16[1024,256]{1,0:T(8,128)(2,1)}, bf16[1024,256]{1,0:T(8,128)(2,1)S(1)}, u32[]{:S(2)}, u32[]{:S(2)}) collective-permute-start(bf16[1024,256]{1,0:T(8,128)(2,1)} %get-tuple-element.35), channel_id=1, source_target_pairs={{0,32},{32,0},{64,96},{96,64},{1,33},{33,1},{65,97},{97,65},{2,34}... | collective-permute-start | bytes 1572872 | tf_op jit(solution)/shard_map/ppermute | solution.py:545
  20.6 18.3 %collective-permute-start.2 = (bf16[1024,256]{1,0:T(8,128)(2,1)}, bf16[1024,256]{1,0:T(8,128)(2,1)S(1)}, u32[]{:S(2)}, u32[]{:S(2)}) collective-permute-start(bf16[1024,256]{1,0:T(8,128)(2,1)} %get-tuple-element.33), channel_id=1, source_target_pairs={{0,64},{32,96},{64,0},{96,32},{1,65},{33,97},{65,1},{97,33},{2,66}... | collective-permute-start | bytes 1572872 | tf_op jit(solution)/shard_map/ppermute | solution.py:543
  23.2 24.0 %collective-permute-start.3 = (bf16[1024,256]{1,0:T(8,128)(2,1)S(1)}, bf16[1024,256]{1,0:T(8,128)(2,1)S(1)}, u32[]{:S(2)}, u32[]{:S(2)}) collective-permute-start(bf16[1024,256]{1,0:T(8,128)(2,1)S(1)} %get-tuple-element.39), channel_id=1, source_target_pairs={{0,96},{32,64},{64,32},{96,0},{1,97},{33,65},{65,33},{97,1},{2,98}... | collective-permute-start | bytes 1572872 | tf_op jit(solution)/shard_map/ppermute | solution.py:544
  51.6 8.3 %collective-permute-start.6 = (bf16[16,2,14,8,256]{4,3,1,2,0:T(8,128)(2,1)}, bf16[16,2,14,8,256]{4,3,1,2,0:T(8,128)(2,1)}, u32[]{:S(2)}, u32[]{:S(2)}) collective-permute-start(bf16[16,2,14,8,256]{4,3,1,2,0:T(8,128)(2,1)} %all-to-all-done), channel_id=1, source_target_pairs={{0,32},{32,0},{64,96},{96,64},{1,33},{33,1},{65,97},{97,65},{2,34}... | collective-permute-start | bytes 5505032 | tf_op jit(solution)/shard_map/ppermute | solution.py:573
  51.9 13.2 %collective-permute-start.5 = (bf16[1,4,128,256]{3,2,1,0:T(8,128)(2,1)S(1)}, bf16[1,4,128,256]{3,2,1,0:T(8,128)(2,1)S(1)}, u32[]{:S(2)}, u32[]{:S(2)}) collective-permute-start(bf16[1,4,128,256]{3,2,1,0:T(8,128)(2,1)S(1)} %get-tuple-element.41), channel_id=1, source_target_pairs={{0,32},{32,0},{64,96},{96,64},{1,33},{33,1},{65,97},{97,65},{2,34}... | collective-permute-start | bytes 786440 | tf_op jit(solution)/shard_map/ppermute | solution.py:571
  52.2 12.9 %collective-permute-start.4 = (bf16[1,4,128,256]{3,2,1,0:T(8,128)(2,1)S(1)}, bf16[1,4,128,256]{3,2,1,0:T(8,128)(2,1)S(1)}, u32[]{:S(2)}, u32[]{:S(2)}) collective-permute-start(bf16[1,4,128,256]{3,2,1,0:T(8,128)(2,1)S(1)} %get-tuple-element.40), channel_id=1, source_target_pairs={{0,96},{32,64},{64,32},{96,0},{1,97},{33,65},{65,33},{97,1},{2,98}... | collective-permute-start | bytes 786440 | tf_op jit(solution)/shard_map/ppermute | solution.py:570
  54.9 17.3 %collective-permute-start.7 = (bf16[4,1,128,256]{3,2,1,0:T(8,128)(2,1)S(1)}, bf16[4,1,128,256]{3,2,1,0:T(8,128)(2,1)S(1)}, u32[]{:S(2)}, u32[]{:S(2)}) collective-permute-start(bf16[4,1,128,256]{3,2,1,0:T(8,128)(2,1)S(1)} %get-tuple-element.49), channel_id=1, source_target_pairs={{0,1},{1,0},{2,3},{3,2},{4,5},{5,4},{6,7},{7,6},{8,9},{9,8},{10,11... | collective-permute-start | bytes 786440 | tf_op jit(solution)/shard_map/ppermute | solution.py:576
  56.5 15.8 %collective-permute-start.8 = (bf16[4,1,128,256]{3,2,1,0:T(8,128)(2,1)S(1)}, bf16[4,1,128,256]{3,2,1,0:T(8,128)(2,1)S(1)}, u32[]{:S(2)}, u32[]{:S(2)}) collective-permute-start(bf16[4,1,128,256]{3,2,1,0:T(8,128)(2,1)S(1)} %get-tuple-element.50), channel_id=1, source_target_pairs={{0,31},{1,2},{2,1},{3,4},{4,3},{5,6},{6,5},{7,8},{8,7},{9,10},{10,... | collective-permute-start | bytes 786440 | tf_op jit(solution)/shard_map/ppermute | solution.py:577
  63.1 4.7 %copy-start.6 = (bf16[256]{0:T(256)(128)(2,1)S(1)}, bf16[256]{0:T(256)(128)(2,1)}, u32[]{:S(2)}) copy-start(bf16[256]{0:T(256)(128)(2,1)} %param.16) | copy-start | bytes 1540
  65.2 7.1 %collective-permute-start.9 = (bf16[2,128,256]{2,1,0:T(8,128)(2,1)S(1)}, bf16[2,128,256]{2,1,0:T(8,128)(2,1)S(1)}, u32[]{:S(2)}, u32[]{:S(2)}) collective-permute-start(bf16[2,128,256]{2,1,0:T(8,128)(2,1)S(1)} %pad_maximum_fusion.1), channel_id=1, source_target_pairs={{0,1},{1,0},{2,3},{3,2},{4,5},{5,4},{6,7},{7,6},{8,9},{9,8},{10,11... | collective-permute-start | bytes 393224 | tf_op jit(solution)/shard_map/ppermute | solution.py:589
  65.3 8.6 %collective-permute-start.10 = (bf16[2,128,256]{2,1,0:T(8,128)(2,1)S(1)}, bf16[2,128,256]{2,1,0:T(8,128)(2,1)S(1)}, u32[]{:S(2)}, u32[]{:S(2)}) collective-permute-start(bf16[2,128,256]{2,1,0:T(8,128)(2,1)S(1)} %pad_maximum_fusion), channel_id=1, source_target_pairs={{0,31},{1,2},{2,1},{3,4},{4,3},{5,6},{6,5},{7,8},{8,7},{9,10},{10,... | collective-permute-start | bytes 393224 | tf_op jit(solution)/shard_map/ppermute | solution.py:589
  67.8 6.2 %copy-start.2 = (bf16[4,4,128,256]{3,2,1,0:T(8,128)(2,1)S(1)}, bf16[4,4,128,256]{3,2,1,0:T(8,128)(2,1)}, u32[]{:S(2)}) copy-start(bf16[4,4,128,256]{3,2,1,0:T(8,128)(2,1)} %cotangent_ref.1) | copy-start | bytes 3145732
  86.4 4.0 %collective-permute-start.11 = (bf16[32,8,16,128]{3,2,1,0:T(8,128)(2,1)S(1)}, bf16[32,8,16,128]{3,2,1,0:T(8,128)(2,1)S(1)}, u32[]{:S(2)}, u32[]{:S(2)}) collective-permute-start(bf16[32,8,16,128]{3,2,1,0:T(8,128)(2,1)S(1)} %get-tuple-element.53), channel_id=1, source_target_pairs={{0,32},{32,0},{64,96},{96,64},{1,33},{33,1},{65,97},{97,65},{2,34}... | collective-permute-start | bytes 3145736 | tf_op jit(solution)/shard_map/ppermute | solution.py:463
  95.7 4.9 %collective-permute-start.18 = (bf16[32,6,16,128]{3,2,1,0:T(8,128)(2,1)S(1)}, bf16[32,6,16,128]{3,2,1,0:T(8,128)(2,1)S(1)}, u32[]{:S(2)}, u32[]{:S(2)}) collective-permute-start(bf16[32,6,16,128]{3,2,1,0:T(8,128)(2,1)S(1)} %get-tuple-element.59), channel_id=1, source_target_pairs={{0,32},{32,0},{64,96},{96,64},{1,33},{33,1},{65,97},{97,65},{2,34}... | collective-permute-start | bytes 2359304 | tf_op jit(solution)/shard_map/ppermute | solution.py:463
  96.4 7.8 %collective-permute-start.12 = (bf16[2,4,8,16,128]{4,3,2,1,0:T(8,128)(2,1)S(1)}, bf16[2,4,8,16,128]{4,3,2,1,0:T(8,128)(2,1)S(1)}, u32[]{:S(2)}, u32[]{:S(2)}) collective-permute-start(bf16[2,4,8,16,128]{4,3,2,1,0:T(8,128)(2,1)S(1)} %get-tuple-element.64), channel_id=1, source_target_pairs={{0,1},{1,0},{2,3},{3,2},{4,5},{5,4},{6,7},{7,6},{8,9},{9,8},{10,11... | collective-permute-start | bytes 786440 | tf_op jit(solution)/shard_map/ppermute | solution.py:473
  97.7 14.9 %collective-permute-start.13 = (bf16[2,4,8,16,128]{4,3,2,1,0:T(8,128)(2,1)S(1)}, bf16[2,4,8,16,128]{4,3,2,1,0:T(8,128)(2,1)S(1)}, u32[]{:S(2)}, u32[]{:S(2)}) collective-permute-start(bf16[2,4,8,16,128]{4,3,2,1,0:T(8,128)(2,1)S(1)} %get-tuple-element.66), channel_id=1, source_target_pairs={{0,2},{1,3},{2,0},{3,1},{4,6},{5,7},{6,4},{7,5},{8,10},{9,11},{10,... | collective-permute-start | bytes 786440 | tf_op jit(solution)/shard_map/ppermute | solution.py:473
  100.6 14.0 %collective-permute-start.14 = (bf16[2,4,8,16,128]{4,3,2,1,0:T(8,128)(2,1)S(1)}, bf16[2,4,8,16,128]{4,3,2,1,0:T(8,128)(2,1)S(1)}, u32[]{:S(2)}, u32[]{:S(2)}) collective-permute-start(bf16[2,4,8,16,128]{4,3,2,1,0:T(8,128)(2,1)S(1)} %get-tuple-element.65), channel_id=1, source_target_pairs={{0,3},{1,2},{2,1},{3,0},{4,7},{5,6},{6,5},{7,4},{8,11},{9,10},{10,... | collective-permute-start | bytes 786440 | tf_op jit(solution)/shard_map/ppermute | solution.py:473
  100.9 14.6 %collective-permute-start.19 = (bf16[2,4,6,16,128]{4,3,2,1,0:T(8,128)(2,1)S(1)}, bf16[2,4,6,16,128]{4,3,2,1,0:T(8,128)(2,1)S(1)}, u32[]{:S(2)}, u32[]{:S(2)}) collective-permute-start(bf16[2,4,6,16,128]{4,3,2,1,0:T(8,128)(2,1)S(1)} %get-tuple-element.67), channel_id=1, source_target_pairs={{0,4},{1,5},{2,6},{3,7},{4,0},{5,1},{6,2},{7,3},{8,12},{9,13},{10,... | collective-permute-start | bytes 589832 | tf_op jit(solution)/shard_map/ppermute | solution.py:473
  101.9 16.8 %collective-permute-start.20 = (bf16[2,4,6,16,128]{4,3,2,1,0:T(8,128)(2,1)S(1)}, bf16[2,4,6,16,128]{4,3,2,1,0:T(8,128)(2,1)S(1)}, u32[]{:S(2)}, u32[]{:S(2)}) collective-permute-start(bf16[2,4,6,16,128]{4,3,2,1,0:T(8,128)(2,1)S(1)} %get-tuple-element.69), channel_id=1, source_target_pairs={{0,8},{1,9},{2,10},{3,11},{4,12},{5,13},{6,14},{7,15},{8,0},{9,1},... | collective-permute-start | bytes 589832 | tf_op jit(solution)/shard_map/ppermute | solution.py:473
  104.2 14.5 %collective-permute-start.21 = (bf16[2,4,6,16,128]{4,3,2,1,0:T(8,128)(2,1)S(1)}, bf16[2,4,6,16,128]{4,3,2,1,0:T(8,128)(2,1)S(1)}, u32[]{:S(2)}, u32[]{:S(2)}) collective-permute-start(bf16[2,4,6,16,128]{4,3,2,1,0:T(8,128)(2,1)S(1)} %get-tuple-element.68), channel_id=1, source_target_pairs={{0,12},{1,13},{2,14},{3,15},{4,8},{5,9},{6,10},{7,11},{8,4},{9,5},... | collective-permute-start | bytes 589832 | tf_op jit(solution)/shard_map/ppermute | solution.py:473
  114.8 5.7 %collective-permute-start.15 = (bf16[2,8,16,128]{3,2,1,0:T(8,128)(2,1)S(1)}, bf16[2,8,16,128]{3,2,1,0:T(8,128)(2,1)S(1)}, u32[]{:S(2)}, u32[]{:S(2)}) collective-permute-start(bf16[2,8,16,128]{3,2,1,0:T(8,128)(2,1)S(1)} %get-tuple-element.70), channel_id=1, source_target_pairs={{0,4},{1,5},{2,6},{3,7},{4,0},{5,1},{6,2},{7,3},{8,12},{9,13},{10,... | collective-permute-start | bytes 196616 | tf_op jit(solution)/shard_map/ppermute | solution.py:473
  114.9 7.9 %collective-permute-start.16 = (bf16[2,8,16,128]{3,2,1,0:T(8,128)(2,1)S(1)}, bf16[2,8,16,128]{3,2,1,0:T(8,128)(2,1)S(1)}, u32[]{:S(2)}, u32[]{:S(2)}) collective-permute-start(bf16[2,8,16,128]{3,2,1,0:T(8,128)(2,1)S(1)} %get-tuple-element.72), channel_id=1, source_target_pairs={{0,8},{1,9},{2,10},{3,11},{4,12},{5,13},{6,14},{7,15},{8,0},{9,1},... | collective-permute-start | bytes 196616 | tf_op jit(solution)/shard_map/ppermute | solution.py:473
  115.5 7.3 %collective-permute-start.17 = (bf16[2,8,16,128]{3,2,1,0:T(8,128)(2,1)S(1)}, bf16[2,8,16,128]{3,2,1,0:T(8,128)(2,1)S(1)}, u32[]{:S(2)}, u32[]{:S(2)}) collective-permute-start(bf16[2,8,16,128]{3,2,1,0:T(8,128)(2,1)S(1)} %get-tuple-element.71), channel_id=1, source_target_pairs={{0,12},{1,13},{2,14},{3,15},{4,8},{5,9},{6,10},{7,11},{8,4},{9,5},... | collective-permute-start | bytes 196616 | tf_op jit(solution)/shard_map/ppermute | solution.py:473
  118.9 4.0 %collective-permute-start.22 = (bf16[2,6,16,128]{3,2,1,0:T(8,128)(2,1)S(1)}, bf16[2,6,16,128]{3,2,1,0:T(8,128)(2,1)S(1)}, u32[]{:S(2)}, u32[]{:S(2)}) collective-permute-start(bf16[2,6,16,128]{3,2,1,0:T(8,128)(2,1)S(1)} %get-tuple-element.81), channel_id=1, source_target_pairs={{0,1},{1,0},{2,3},{3,2},{4,5},{5,4},{6,7},{7,6},{8,9},{9,8},{10,11... | collective-permute-start | bytes 147464 | tf_op jit(solution)/shard_map/ppermute | solution.py:473
  118.9 4.5 %collective-permute-start.23 = (bf16[2,6,16,128]{3,2,1,0:T(8,128)(2,1)S(1)}, bf16[2,6,16,128]{3,2,1,0:T(8,128)(2,1)S(1)}, u32[]{:S(2)}, u32[]{:S(2)}) collective-permute-start(bf16[2,6,16,128]{3,2,1,0:T(8,128)(2,1)S(1)} %get-tuple-element.83), channel_id=1, source_target_pairs={{0,2},{1,3},{2,0},{3,1},{4,6},{5,7},{6,4},{7,5},{8,10},{9,11},{10,... | collective-permute-start | bytes 147464 | tf_op jit(solution)/shard_map/ppermute | solution.py:473
  120.4 4.2 %collective-permute-start.24 = (bf16[2,6,16,128]{3,2,1,0:T(8,128)(2,1)S(1)}, bf16[2,6,16,128]{3,2,1,0:T(8,128)(2,1)S(1)}, u32[]{:S(2)}, u32[]{:S(2)}) collective-permute-start(bf16[2,6,16,128]{3,2,1,0:T(8,128)(2,1)S(1)} %get-tuple-element.82), channel_id=1, source_target_pairs={{0,3},{1,2},{2,1},{3,0},{4,7},{5,6},{6,5},{7,4},{8,11},{9,10},{10,... | collective-permute-start | bytes 147464 | tf_op jit(solution)/shard_map/ppermute | solution.py:473
  124.7 3.4 %collective-permute-start.25 = (bf16[14,16,128]{2,1,0:T(8,128)(2,1)S(1)}, bf16[14,16,128]{2,1,0:T(8,128)(2,1)S(1)}, u32[]{:S(2)}, u32[]{:S(2)}) collective-permute-start(bf16[14,16,128]{2,1,0:T(8,128)(2,1)S(1)} %get-tuple-element.79), channel_id=1, source_target_pairs={{0,16},{1,17},{2,18},{3,19},{4,20},{5,21},{6,22},{7,23},{8,24},{9,... | collective-permute-start | bytes 172040 | tf_op jit(solution)/shard_map/ppermute | solution.py:612
  125.7 4.2 %collective-permute-start.26 = (bf16[14,16,128]{2,1,0:T(8,128)(2,1)S(1)}, bf16[14,16,128]{2,1,0:T(8,128)(2,1)S(1)}, u32[]{:S(2)}, u32[]{:S(2)}) collective-permute-start(bf16[14,16,128]{2,1,0:T(8,128)(2,1)S(1)} %get-tuple-element.79), channel_id=1, source_target_pairs={{0,80},{1,81},{2,82},{3,83},{4,84},{5,85},{6,86},{7,87},{8,88},{9,... | collective-permute-start | bytes 172040 | tf_op jit(solution)/shard_map/ppermute | solution.py:613
  127.6 4.5 %collective-permute-start.27 = (bf16[14,16,128]{2,1,0:T(8,128)(2,1)S(1)}, bf16[14,16,128]{2,1,0:T(8,128)(2,1)S(1)}, u32[]{:S(2)}, u32[]{:S(2)}) collective-permute-start(bf16[14,16,128]{2,1,0:T(8,128)(2,1)S(1)} %get-tuple-element.80), channel_id=1, source_target_pairs={{0,64},{32,96},{64,0},{96,32},{1,65},{33,97},{65,1},{97,33},{2,66}... | collective-permute-start | bytes 172040 | tf_op jit(solution)/shard_map/ppermute | solution.py:614
  132.2 6.6 %collective-permute-start.28 = (f32[14,16,128]{2,1,0:T(8,128)S(1)}, f32[14,16,128]{2,1,0:T(8,128)S(1)}, u32[]{:S(2)}, u32[]{:S(2)}) collective-permute-start(f32[14,16,128]{2,1,0:T(8,128)S(1)} %convert_add_fusion.3), channel_id=1, source_target_pairs={{0,32},{32,0},{64,96},{96,64},{1,33},{33,1},{65,97},{97,65},{2,34}... | collective-permute-start | bytes 344072 | tf_op jit(solution)/shard_map/ppermute | solution.py:616

commit v6 on v5

--- a/solution.py
+++ b/solution.py
@@ -313,7 +313,7 @@
 
         return carry
 
-    lax.fori_loop(0, count, one_tap, 0)
+    lax.fori_loop(0, count, one_tap, 0, unroll=True)
     if 3 * count < 2 * half_size:
         unused = jnp.zeros((channels // 8, 16, 128), BF)
 

time: 140 us -> 141 us (level)
  transfers between devices with their start and end apart: 30 -> 30, of which waited for: 11 -> 11; matrix products, arithmetic and copies ran while one was open for 3% -> 3% of each run, Pallas kernels for 22% -> 21%
where the time goes in v6:
time: 141 us
  starting transfers between devices  52.9 us (38%)
  Pallas kernels  48.8 us (35%)
  waiting for transfers between devices  28.6 us (20%)
  other arithmetic  5.26 us (4%)
  local copies, waits for them, and re-layouts  4.34 us (3%)
    ppermute x12, starting transfers between devices, sum_over(): lax.ppermute(part, 'chan', [(i, i ^ offset * step) for i in range(chans)])  16.4 us
    pallas_call x1, Pallas kernels, spread_weights(): pl.pallas_call(spread_kernel, grid=(planes,), in_specs=[pl.BlockSpec(memo...  14.9 us
    pallas_call x1, Pallas kernels, outer_conv(): pl.pallas_call(outer_kernel, in_specs=[pl.BlockSpec(memory_space=pltpu.SM...  13 us
    ppermute x12, waiting for transfers between devices, sum_over(): lax.ppermute(part, 'chan', [(i, i ^ offset * step) for i in range(chans)])  11.1 us
    ppermute x1, waiting for transfers between devices, on_device(): from_cross = lax.ppermute(to_cross, 'space', cross)  8.32 us
    all_to_all x1, starting transfers between devices, on_device(): lax.all_to_all(gathered, 'chan', split_axis=0, concat_axis=0, axis_index_...  7.78 us
    pallas_call x2, Pallas kernels, inner_conv(): pl.pallas_call(functools.partial(inner_kernel, chosen), in_specs=[whole]...  6.49 us
    pallas_call x1, Pallas kernels, rest_terms(): pl.pallas_call(rest_kernel, in_specs=[pl.BlockSpec(memory_space=pltpu.SME...  5.68 us
  transfers between devices with their start and end apart: 30, of which 11 were waited for; matrix products, arithmetic and copies ran while one was open for 3% of the time, Pallas kernels for 21%

profile of v6, /device:TPU:1, one launch (start us, length us, event | category | flops | bytes accessed | tf_op | source)
XLA Modules:
  0.0 140.9 jit_solution(9693860130289916786)
XLA Ops:
  0.7 0.8 bitcast_dynamic-update-slice_fusion.1
  1.5 2.2 %collective-permute-start = (bf16[14,8,256]{2,1,0:T(8,128)(2,1)S(1)}, bf16[14,8,256]{2,1,0:T(8,128)(2,1)S(1)}, u32[]{:S(2)}, u32[]{:S(2)}) collective-permute-start(bf16[14,8,256]{2,1,0:T(8,128)(2,1)S(1)} %get-tuple-element.61), channel_id=1, source_target_pairs={{0,16},{1,17},{2,18},{3,19},{4,20},{5,21},{6,22},{7,23},{8,24},{9,... | collective-permute-start | bytes 172040 | tf_op jit(solution)/shard_map/ppermute | solution.py:482
  3.7 0.8 bitcast_select_fusion.slots_ref
  4.5 1.2 copy-done
  5.7 4.2 %shard_map.104 = (bf16[1024,256]{1,0:T(8,128)(2,1)}, bf16[1024,256]{1,0:T(8,128)(2,1)}, bf16[1024,256]{1,0:T(8,128)(2,1)S(1)}) custom-call(s32[4]{0:T(128)S(1)} %iota_xor_fusion.owners_ref, s32[4,8,128]{2,1,0:T(8,128)S(1)} %bitcast_select_fusion.slots_ref, bf16[2048,256]{1,0:T(8,128)(2,1)S(1)} %copy-done), custom_call_target="tpu_custom_call" | custom-call | flops 1 | bytes 1 | tf_op jit(solution)/shard_map/pallas_call | solution.py:39
  10.0 1.4 %broadcast_in_dim.30 = bf16[16,2,14,8,256]{4,3,1,2,0:T(8,128)(2,1)} broadcast(bf16[2,14,8,256]{3,2,0,1:T(8,128)(2,1)S(1)} %bitcast_dynamic-update-slice_fusion), dimensions={1,2,3,4} | broadcast | bytes 1949696 | tf_op jit(solution)/shard_map/broadcast_in_dim | solution.py:546
  11.5 7.8 %all-to-all-start = ((bf16[16,2,14,8,256]{4,3,1,2,0:T(8,128)(2,1)}), bf16[16,2,14,8,256]{4,3,1,2,0:T(8,128)(2,1)}, u32[]{:S(2)}, u32[]{:S(2)}) async-start(bf16[16,2,14,8,256]{4,3,1,2,0:T(8,128)(2,1)} %broadcast_in_dim.30), calls=%async_computation | async-start | bytes 3670016 | tf_op jit(solution)/shard_map/all_to_all | solution.py:547
  19.2 1.3 collective-permute-start.1
  20.6 2.6 %collective-permute-start.2 = (bf16[1024,256]{1,0:T(8,128)(2,1)}, bf16[1024,256]{1,0:T(8,128)(2,1)S(1)}, u32[]{:S(2)}, u32[]{:S(2)}) collective-permute-start(bf16[1024,256]{1,0:T(8,128)(2,1)} %get-tuple-element.33), channel_id=1, source_target_pairs={{0,64},{32,96},{64,0},{96,32},{1,65},{33,97},{65,1},{97,33},{2,66}... | collective-permute-start | bytes 1572872 | tf_op jit(solution)/shard_map/ppermute | solution.py:543
  23.2 0.6 collective-permute-start.3
  23.9 14.9 %shard_map.105 = (bf16[2048,2048]{1,0:T(8,128)(2,1)S(1)}, f32[2048,256]{1,0:T(8,128)S(1)}, f32[2048,128]{1,0:T(8,128)S(1)}) custom-call(s32[4,32]{1,0:T(4,128)S(1)} %bitcast.93, s32[4]{0:T(128)S(1)} %iota_xor_fusion.owners_ref, s32[4,32,128]{2,1,0:T(8,128)S(1)} %broadcast_xor_fusion.near_ref, f32[4,3,32,128]{3,2,1,0:T(8,128)S(1)} %bitcast.92, ...), custom_call_target="tpu_custom_call" | custom-call | tf_op jit(solution)/shard_map/pallas_call | solution.py:109
  38.9 8.3 %collective-permute-done.3.t1 = bf16[1024,256]{1,0:T(8,128)(2,1)S(1)} collective-permute-done((bf16[1024,256]{1,0:T(8,128)(2,1)S(1)}, bf16[1024,256]{1,0:T(8,128)(2,1)S(1)}, u32[]{:S(2)}, u32[]{:S(2)}) %collective-permute-start.3) | collective-permute-done | bytes 524320 | tf_op jit(solution)/shard_map/ppermute | solution.py:544
  47.2 4.5 %shard_map.106 = (bf16[4,4,128,256]{3,2,1,0:T(8,128)(2,1)S(1)}, bf16[1,4,128,256]{3,2,1,0:T(8,128)(2,1)S(1)}, bf16[1,4,128,256]{3,2,1,0:T(8,128)(2,1)S(1)}, bf16...) custom-call(s32[4]{0:T(128)S(1)} %pad_add_fusion.flags_ref, ...), custom_call_target="tpu_custom_call" | custom-call | tf_op jit(solution)/shard_map/pallas_call | solution.py:189
  52.2 2.7 %collective-permute-start.4 = (bf16[1,4,128,256]{3,2,1,0:T(8,128)(2,1)S(1)}, bf16[1,4,128,256]{3,2,1,0:T(8,128)(2,1)S(1)}, u32[]{:S(2)}, u32[]{:S(2)}) collective-permute-start(bf16[1,4,128,256]{3,2,1,0:T(8,128)(2,1)S(1)} %get-tuple-element.40), channel_id=1, source_target_pairs={{0,96},{32,64},{64,32},{96,0},{1,97},{33,65},{65,33},{97,1},{2,98}... | collective-permute-start | bytes 786440 | tf_op jit(solution)/shard_map/ppermute | solution.py:570
  54.9 1.5 %collective-permute-start.7 = (bf16[4,1,128,256]{3,2,1,0:T(8,128)(2,1)S(1)}, bf16[4,1,128,256]{3,2,1,0:T(8,128)(2,1)S(1)}, u32[]{:S(2)}, u32[]{:S(2)}) collective-permute-start(bf16[4,1,128,256]{3,2,1,0:T(8,128)(2,1)S(1)} %get-tuple-element.49), channel_id=1, source_target_pairs={{0,1},{1,0},{2,3},{3,2},{4,5},{5,4},{6,7},{7,6},{8,9},{9,8},{10,11... | collective-permute-start | bytes 786440 | tf_op jit(solution)/shard_map/ppermute | solution.py:576
  56.5 3.5 %collective-permute-start.8 = (bf16[4,1,128,256]{3,2,1,0:T(8,128)(2,1)S(1)}, bf16[4,1,128,256]{3,2,1,0:T(8,128)(2,1)S(1)}, u32[]{:S(2)}, u32[]{:S(2)}) collective-permute-start(bf16[4,1,128,256]{3,2,1,0:T(8,128)(2,1)S(1)} %get-tuple-element.50), channel_id=1, source_target_pairs={{0,31},{1,2},{2,1},{3,4},{4,3},{5,6},{6,5},{7,8},{8,7},{9,10},{10,... | collective-permute-start | bytes 786440 | tf_op jit(solution)/shard_map/ppermute | solution.py:577
  60.0 2.3 %select_bitcast_fusion.1 = (bf16[1,16,2,14,8,256]{5,4,2,3,1,0:T(8,128)(2,1)S(1)}, bf16[1,16,2,14,8,256]{5,4,2,3,1,0:T(8,128)(2,1)S(1)}) fusion(bf16[16,2,14,8,256]{4,3,1,2,0:T(8,128)(2,1)} %all-to-all-done, bf16[16,2,14,8,256]{4,3,1,2,0:T(8,128)(2,1)} %collective-permute-done.6, pred[]{:T(512)S(6)} %eq.14), kind=kLoop, calls=%fused_computation.3 | loop fusion | flops 1835008 | bytes 7340033 | tf_op jit(solution)/shard_map/stack | solution.py:573
  62.6 0.5 copy.14
  63.1 2.0 %shard_map.107.middle_ref = f32[1,4,128,256]{3,2,1,0:T(8,128)S(1)} custom-call(bf16[4,4,128,256]{3,2,1,0:T(8,128)(2,1)S(1)} %get-tuple-element.48.latent_ref, bf16[28,256,256]{2,1,0:T(8,128)(2,1)S(1)} %bitcast.89), custom_call_target="tpu_custom_call" | custom-call | flops 1 | bytes 1 | tf_op jit(solution)/shard_map/pallas_call | solution.py:264
  65.3 2.5 %collective-permute-start.10 = (bf16[2,128,256]{2,1,0:T(8,128)(2,1)S(1)}, bf16[2,128,256]{2,1,0:T(8,128)(2,1)S(1)}, u32[]{:S(2)}, u32[]{:S(2)}) collective-permute-start(bf16[2,128,256]{2,1,0:T(8,128)(2,1)S(1)} %pad_maximum_fusion), channel_id=1, source_target_pairs={{0,31},{1,2},{2,1},{3,4},{4,3},{5,6},{6,5},{7,8},{8,7},{9,10},{10,... | collective-permute-start | bytes 393224 | tf_op jit(solution)/shard_map/ppermute | solution.py:589
  67.8 4.5 %shard_map.108.edge_ref = f32[3,4,128,256]{3,2,1,0:T(8,128)S(1)} custom-call(bf16[4,4,128,256]{3,2,1,0:T(8,128)(2,1)S(1)} %get-tuple-element.48.latent_ref, bf16[28,256,256]{2,1,0:T(8,128)(2,1)S(1)} %bitcast.90), custom_call_target="tpu_custom_call" | custom-call | flops 1 | bytes 1 | tf_op jit(solution)/shard_map/pallas_call | solution.py:264
  72.3 1.6 %collective-permute-done.10.second_end_ref = bf16[2,128,256]{2,1,0:T(8,128)(2,1)S(1)} collective-permute-done((bf16[2,128,256]{2,1,0:T(8,128)(2,1)S(1)}, bf16[2,128,256]{2,1,0:T(8,128)(2,1)S(1)}, u32[]{:S(2)}, u32[]{:S(2)}) %collective-permute-start.10) | collective-permute-done | bytes 131104 | tf_op jit(solution)/shard_map/ppermute | solution.py:589
  73.9 13.0 %shard_map.109 = (bf16[4,4,128,256]{3,2,1,0:T(8,128)(2,1)}, bf16[6,256,768]{2,1,0:T(8,128)(2,1)S(1)}, bf16[2048,768]{1,0:T(8,128)(2,1)S(1)}, bf16[32,8,16,128]{3...) custom-call(s32[4]{0:T(128)S(1)} %pad_add_fusion.flags_ref, f32[1,4,128,256]{3,2,1,0:T(8,128)S(1)} %shard_map.107.middle_ref, ...), custom_call_target="tpu_custom_call" | custom-call | tf_op jit(solution)/shard_map/pallas_call | solution.py:423
  86.9 1.8 %collective-permute-start.11 = (bf16[32,8,16,128]{3,2,1,0:T(8,128)(2,1)S(1)}, bf16[32,8,16,128]{3,2,1,0:T(8,128)(2,1)S(1)}, u32[]{:S(2)}, u32[]{:S(2)}) collective-permute-start(bf16[32,8,16,128]{3,2,1,0:T(8,128)(2,1)S(1)} %get-tuple-element.53), channel_id=1, source_target_pairs={{0,32},{32,0},{64,96},{96,64},{1,33},{33,1},{65,97},{97,65},{2,34}... | collective-permute-start | bytes 3145736 | tf_op jit(solution)/shard_map/ppermute | solution.py:463
  88.7 2.3 %collective-permute-done.11 = bf16[32,8,16,128]{3,2,1,0:T(8,128)(2,1)S(1)} collective-permute-done((bf16[32,8,16,128]{3,2,1,0:T(8,128)(2,1)S(1)}, bf16[32,8,16,128]{3,2,1,0:T(8,128)(2,1)S(1)}, u32[]{:S(2)}, u32[]{:S(2)}) %collective-permute-start.11) | collective-permute-done | bytes 1048608 | tf_op jit(solution)/shard_map/ppermute | solution.py:463
  91.4 5.7 %shard_map.110 = (bf16[32,6,16,128]{3,2,1,0:T(8,128)(2,1)S(1)}, bf16[32,6,16,128]{3,2,1,0:T(8,128)(2,1)S(1)}) custom-call(s32[4]{0:T(128)S(1)} %pad_add_fusion.flags_ref, bf16[6,256,768]{2,1,0:T(8,128)(2,1)S(1)} %get-tuple-element.56.turned, bf16[2048,768]{1,0:T(8,128)(2,1)S(1)} %get-tuple-element.57.shifted), custom_call_target="tpu_custom_call" | custom-call | tf_op jit(solution)/shard_map/pallas_call | solution.py:453
  97.1 0.5 collective-permute-start.18
  97.8 1.3 collective-permute-start.12
  99.0 3.0 %collective-permute-start.13 = (bf16[2,4,8,16,128]{4,3,2,1,0:T(8,128)(2,1)S(1)}, bf16[2,4,8,16,128]{4,3,2,1,0:T(8,128)(2,1)S(1)}, u32[]{:S(2)}, u32[]{:S(2)}) collective-permute-start(bf16[2,4,8,16,128]{4,3,2,1,0:T(8,128)(2,1)S(1)} %get-tuple-element.66), channel_id=1, source_target_pairs={{0,2},{1,3},{2,0},{3,1},{4,6},{5,7},{6,4},{7,5},{8,10},{9,11},{10,... | collective-permute-start | bytes 786440 | tf_op jit(solution)/shard_map/ppermute | solution.py:473
  102.3 1.0 collective-permute-start.19
  103.3 1.6 %collective-permute-start.20 = (bf16[2,4,6,16,128]{4,3,2,1,0:T(8,128)(2,1)S(1)}, bf16[2,4,6,16,128]{4,3,2,1,0:T(8,128)(2,1)S(1)}, u32[]{:S(2)}, u32[]{:S(2)}) collective-permute-start(bf16[2,4,6,16,128]{4,3,2,1,0:T(8,128)(2,1)S(1)} %get-tuple-element.69), channel_id=1, source_target_pairs={{0,8},{1,9},{2,10},{3,11},{4,12},{5,13},{6,14},{7,15},{8,0},{9,1},... | collective-permute-start | bytes 589832 | tf_op jit(solution)/shard_map/ppermute | solution.py:473
  104.9 0.7 collective-permute-done.12
  105.6 1.7 %collective-permute-start.21 = (bf16[2,4,6,16,128]{4,3,2,1,0:T(8,128)(2,1)S(1)}, bf16[2,4,6,16,128]{4,3,2,1,0:T(8,128)(2,1)S(1)}, u32[]{:S(2)}, u32[]{:S(2)}) collective-permute-start(bf16[2,4,6,16,128]{4,3,2,1,0:T(8,128)(2,1)S(1)} %get-tuple-element.68), channel_id=1, source_target_pairs={{0,12},{1,13},{2,14},{3,15},{4,8},{5,9},{6,10},{7,11},{8,4},{9,5},... | collective-permute-start | bytes 589832 | tf_op jit(solution)/shard_map/ppermute | solution.py:473
  107.3 6.7 %collective-permute-done.13 = bf16[2,4,8,16,128]{4,3,2,1,0:T(8,128)(2,1)S(1)} collective-permute-done((bf16[2,4,8,16,128]{4,3,2,1,0:T(8,128)(2,1)S(1)}, bf16[2,4,8,16,128]{4,3,2,1,0:T(8,128)(2,1)S(1)}, u32[]{:S(2)}, u32[]{:S(2)}) %collective-permute-start.13) | collective-permute-done | bytes 262176 | tf_op jit(solution)/shard_map/ppermute | solution.py:473
  113.9 2.0 %collective-permute-done.14 = bf16[2,4,8,16,128]{4,3,2,1,0:T(8,128)(2,1)S(1)} collective-permute-done((bf16[2,4,8,16,128]{4,3,2,1,0:T(8,128)(2,1)S(1)}, bf16[2,4,8,16,128]{4,3,2,1,0:T(8,128)(2,1)S(1)}, u32[]{:S(2)}, u32[]{:S(2)}) %collective-permute-start.14) | collective-permute-done | bytes 262176 | tf_op jit(solution)/shard_map/ppermute | solution.py:473
  116.2 0.6 collective-permute-start.16
  116.8 3.2 %collective-permute-start.17 = (bf16[2,8,16,128]{3,2,1,0:T(8,128)(2,1)S(1)}, bf16[2,8,16,128]{3,2,1,0:T(8,128)(2,1)S(1)}, u32[]{:S(2)}, u32[]{:S(2)}) collective-permute-start(bf16[2,8,16,128]{3,2,1,0:T(8,128)(2,1)S(1)} %get-tuple-element.71), channel_id=1, source_target_pairs={{0,12},{1,13},{2,14},{3,15},{4,8},{5,9},{6,10},{7,11},{8,4},{9,5},... | collective-permute-start | bytes 196616 | tf_op jit(solution)/shard_map/ppermute | solution.py:473
  120.3 1.5 %collective-permute-start.23 = (bf16[2,6,16,128]{3,2,1,0:T(8,128)(2,1)S(1)}, bf16[2,6,16,128]{3,2,1,0:T(8,128)(2,1)S(1)}, u32[]{:S(2)}, u32[]{:S(2)}) collective-permute-start(bf16[2,6,16,128]{3,2,1,0:T(8,128)(2,1)S(1)} %get-tuple-element.83), channel_id=1, source_target_pairs={{0,2},{1,3},{2,0},{3,1},{4,6},{5,7},{6,4},{7,5},{8,10},{9,11},{10,... | collective-permute-start | bytes 147464 | tf_op jit(solution)/shard_map/ppermute | solution.py:473
  121.8 2.4 %collective-permute-start.24 = (bf16[2,6,16,128]{3,2,1,0:T(8,128)(2,1)S(1)}, bf16[2,6,16,128]{3,2,1,0:T(8,128)(2,1)S(1)}, u32[]{:S(2)}, u32[]{:S(2)}) collective-permute-start(bf16[2,6,16,128]{3,2,1,0:T(8,128)(2,1)S(1)} %get-tuple-element.82), channel_id=1, source_target_pairs={{0,3},{1,2},{2,1},{3,0},{4,7},{5,6},{6,5},{7,4},{8,11},{9,10},{10,... | collective-permute-start | bytes 147464 | tf_op jit(solution)/shard_map/ppermute | solution.py:473
  124.2 0.6 collective-permute-done.23
  124.8 1.1 collective-permute-done.24
  126.0 1.1 collective-permute-start.25
  127.1 1.9 %collective-permute-start.26 = (bf16[14,16,128]{2,1,0:T(8,128)(2,1)S(1)}, bf16[14,16,128]{2,1,0:T(8,128)(2,1)S(1)}, u32[]{:S(2)}, u32[]{:S(2)}) collective-permute-start(bf16[14,16,128]{2,1,0:T(8,128)(2,1)S(1)} %get-tuple-element.79), channel_id=1, source_target_pairs={{0,80},{1,81},{2,82},{3,83},{4,84},{5,85},{6,86},{7,87},{8,88},{9,... | collective-permute-start | bytes 172040 | tf_op jit(solution)/shard_map/ppermute | solution.py:613
  129.4 1.9 %collective-permute-done.26 = bf16[14,16,128]{2,1,0:T(8,128)(2,1)S(1)} collective-permute-done((bf16[14,16,128]{2,1,0:T(8,128)(2,1)S(1)}, bf16[14,16,128]{2,1,0:T(8,128)(2,1)S(1)}, u32[]{:S(2)}, u32[]{:S(2)}) %collective-permute-start.26) | collective-permute-done | bytes 57376 | tf_op jit(solution)/shard_map/ppermute | solution.py:613
  131.3 2.2 %collective-permute-done.27 = bf16[14,16,128]{2,1,0:T(8,128)(2,1)S(1)} collective-permute-done((bf16[14,16,128]{2,1,0:T(8,128)(2,1)S(1)}, bf16[14,16,128]{2,1,0:T(8,128)(2,1)S(1)}, u32[]{:S(2)}, u32[]{:S(2)}) %collective-permute-start.27) | collective-permute-done | bytes 57376 | tf_op jit(solution)/shard_map/ppermute | solution.py:614
  133.6 5.6 %collective-permute-start.28 = (f32[14,16,128]{2,1,0:T(8,128)S(1)}, f32[14,16,128]{2,1,0:T(8,128)S(1)}, u32[]{:S(2)}, u32[]{:S(2)}) collective-permute-start(f32[14,16,128]{2,1,0:T(8,128)S(1)} %convert_add_fusion.3), channel_id=1, source_target_pairs={{0,32},{32,0},{64,96},{96,64},{1,33},{33,1},{65,97},{97,65},{2,34}... | collective-permute-start | bytes 344072 | tf_op jit(solution)/shard_map/ppermute | solution.py:616
  139.2 1.0 collective-permute-done.28
  140.2 0.7 fusion.6
  (67 shorter events, 3.2 us)
Async XLA Ops:
  1.5 8.5 %collective-permute-start = (bf16[14,8,256]{2,1,0:T(8,128)(2,1)S(1)}, bf16[14,8,256]{2,1,0:T(8,128)(2,1)S(1)}, u32[]{:S(2)}, u32[]{:S(2)}) collective-permute-start(bf16[14,8,256]{2,1,0:T(8,128)(2,1)S(1)} %get-tuple-element.61), channel_id=1, source_target_pairs={{0,16},{1,17},{2,18},{3,19},{4,20},{5,21},{6,22},{7,23},{8,24},{9,... | collective-permute-start | bytes 172040 | tf_op jit(solution)/shard_map/ppermute | solution.py:482
  4.5 1.2 copy-start
  11.4 12.4 %copy-start.5 = (s32[4,1,32,128]{3,2,1,0:T(8,128)S(1)}, s32[4,1,32,128]{3,2,1,0:T(8,128)}, u32[]{:S(2)}) copy-start(s32[4,1,32,128]{3,2,1,0:T(8,128)} %param.12) | copy-start | bytes 196612
  11.4 12.4 %copy-start.1 = (bf16[2048,256]{1,0:T(8,128)(2,1)S(1)}, bf16[2048,256]{1,0:T(8,128)(2,1)}, u32[]{:S(2)}) copy-start(bf16[2048,256]{1,0:T(8,128)(2,1)} %feats_ref.3) | copy-start | bytes 3145732
  11.4 12.5 %copy-start.3 = (f32[4,1,32,3,128]{4,2,3,1,0:T(8,128)S(1)}, f32[4,1,32,3,128]{4,2,3,1,0:T(8,128)}, u32[]{:S(2)}) copy-start(f32[4,1,32,3,128]{4,2,3,1,0:T(8,128)} %param.14) | copy-start | bytes 589828
  11.4 12.5 %copy-start.4 = (s32[4,1,32]{2,1,0:T(1,128)S(1)}, s32[4,1,32]{2,1,0:T(1,128)}, u32[]{:S(2)}) copy-start(s32[4,1,32]{2,1,0:T(1,128)} %param.13) | copy-start | bytes 1540
  11.5 40.2 %all-to-all-start = ((bf16[16,2,14,8,256]{4,3,1,2,0:T(8,128)(2,1)}), bf16[16,2,14,8,256]{4,3,1,2,0:T(8,128)(2,1)}, u32[]{:S(2)}, u32[]{:S(2)}) async-start(bf16[16,2,14,8,256]{4,3,1,2,0:T(8,128)(2,1)} %broadcast_in_dim.30), calls=%async_computation | async-start | bytes 3670016 | tf_op jit(solution)/shard_map/all_to_all | solution.py:547
  19.2 4.6 %collective-permute-start.1 = (bf16[1024,256]{1,0:T(8,128)(2,1)}, bf16[1024,256]{1,0:T(8,128)(2,1)S(1)}, u32[]{:S(2)}, u32[]{:S(2)}) collective-permute-start(bf16[1024,256]{1,0:T(8,128)(2,1)} %get-tuple-element.35), channel_id=1, source_target_pairs={{0,32},{32,0},{64,96},{96,64},{1,33},{33,1},{65,97},{97,65},{2,34}... | collective-permute-start | bytes 1572872 | tf_op jit(solution)/shard_map/ppermute | solution.py:545
  20.6 18.3 %collective-permute-start.2 = (bf16[1024,256]{1,0:T(8,128)(2,1)}, bf16[1024,256]{1,0:T(8,128)(2,1)S(1)}, u32[]{:S(2)}, u32[]{:S(2)}) collective-permute-start(bf16[1024,256]{1,0:T(8,128)(2,1)} %get-tuple-element.33), channel_id=1, source_target_pairs={{0,64},{32,96},{64,0},{96,32},{1,65},{33,97},{65,1},{97,33},{2,66}... | collective-permute-start | bytes 1572872 | tf_op jit(solution)/shard_map/ppermute | solution.py:543
  23.2 24.0 %collective-permute-start.3 = (bf16[1024,256]{1,0:T(8,128)(2,1)S(1)}, bf16[1024,256]{1,0:T(8,128)(2,1)S(1)}, u32[]{:S(2)}, u32[]{:S(2)}) collective-permute-start(bf16[1024,256]{1,0:T(8,128)(2,1)S(1)} %get-tuple-element.39), channel_id=1, source_target_pairs={{0,96},{32,64},{64,32},{96,0},{1,97},{33,65},{65,33},{97,1},{2,98}... | collective-permute-start | bytes 1572872 | tf_op jit(solution)/shard_map/ppermute | solution.py:544
  51.6 8.3 %collective-permute-start.6 = (bf16[16,2,14,8,256]{4,3,1,2,0:T(8,128)(2,1)}, bf16[16,2,14,8,256]{4,3,1,2,0:T(8,128)(2,1)}, u32[]{:S(2)}, u32[]{:S(2)}) collective-permute-start(bf16[16,2,14,8,256]{4,3,1,2,0:T(8,128)(2,1)} %all-to-all-done), channel_id=1, source_target_pairs={{0,32},{32,0},{64,96},{96,64},{1,33},{33,1},{65,97},{97,65},{2,34}... | collective-permute-start | bytes 5505032 | tf_op jit(solution)/shard_map/ppermute | solution.py:573
  51.9 13.2 %collective-permute-start.5 = (bf16[1,4,128,256]{3,2,1,0:T(8,128)(2,1)S(1)}, bf16[1,4,128,256]{3,2,1,0:T(8,128)(2,1)S(1)}, u32[]{:S(2)}, u32[]{:S(2)}) collective-permute-start(bf16[1,4,128,256]{3,2,1,0:T(8,128)(2,1)S(1)} %get-tuple-element.41), channel_id=1, source_target_pairs={{0,32},{32,0},{64,96},{96,64},{1,33},{33,1},{65,97},{97,65},{2,34}... | collective-permute-start | bytes 786440 | tf_op jit(solution)/shard_map/ppermute | solution.py:571
  52.2 12.9 %collective-permute-start.4 = (bf16[1,4,128,256]{3,2,1,0:T(8,128)(2,1)S(1)}, bf16[1,4,128,256]{3,2,1,0:T(8,128)(2,1)S(1)}, u32[]{:S(2)}, u32[]{:S(2)}) collective-permute-start(bf16[1,4,128,256]{3,2,1,0:T(8,128)(2,1)S(1)} %get-tuple-element.40), channel_id=1, source_target_pairs={{0,96},{32,64},{64,32},{96,0},{1,97},{33,65},{65,33},{97,1},{2,98}... | collective-permute-start | bytes 786440 | tf_op jit(solution)/shard_map/ppermute | solution.py:570
  54.9 17.3 %collective-permute-start.7 = (bf16[4,1,128,256]{3,2,1,0:T(8,128)(2,1)S(1)}, bf16[4,1,128,256]{3,2,1,0:T(8,128)(2,1)S(1)}, u32[]{:S(2)}, u32[]{:S(2)}) collective-permute-start(bf16[4,1,128,256]{3,2,1,0:T(8,128)(2,1)S(1)} %get-tuple-element.49), channel_id=1, source_target_pairs={{0,1},{1,0},{2,3},{3,2},{4,5},{5,4},{6,7},{7,6},{8,9},{9,8},{10,11... | collective-permute-start | bytes 786440 | tf_op jit(solution)/shard_map/ppermute | solution.py:576
  56.5 15.8 %collective-permute-start.8 = (bf16[4,1,128,256]{3,2,1,0:T(8,128)(2,1)S(1)}, bf16[4,1,128,256]{3,2,1,0:T(8,128)(2,1)S(1)}, u32[]{:S(2)}, u32[]{:S(2)}) collective-permute-start(bf16[4,1,128,256]{3,2,1,0:T(8,128)(2,1)S(1)} %get-tuple-element.50), channel_id=1, source_target_pairs={{0,31},{1,2},{2,1},{3,4},{4,3},{5,6},{6,5},{7,8},{8,7},{9,10},{10,... | collective-permute-start | bytes 786440 | tf_op jit(solution)/shard_map/ppermute | solution.py:577
  63.1 4.7 %copy-start.6 = (bf16[256]{0:T(256)(128)(2,1)S(1)}, bf16[256]{0:T(256)(128)(2,1)}, u32[]{:S(2)}) copy-start(bf16[256]{0:T(256)(128)(2,1)} %param.16) | copy-start | bytes 1540
  65.2 7.1 %collective-permute-start.9 = (bf16[2,128,256]{2,1,0:T(8,128)(2,1)S(1)}, bf16[2,128,256]{2,1,0:T(8,128)(2,1)S(1)}, u32[]{:S(2)}, u32[]{:S(2)}) collective-permute-start(bf16[2,128,256]{2,1,0:T(8,128)(2,1)S(1)} %pad_maximum_fusion.1), channel_id=1, source_target_pairs={{0,1},{1,0},{2,3},{3,2},{4,5},{5,4},{6,7},{7,6},{8,9},{9,8},{10,11... | collective-permute-start | bytes 393224 | tf_op jit(solution)/shard_map/ppermute | solution.py:589
  65.3 8.6 %collective-permute-start.10 = (bf16[2,128,256]{2,1,0:T(8,128)(2,1)S(1)}, bf16[2,128,256]{2,1,0:T(8,128)(2,1)S(1)}, u32[]{:S(2)}, u32[]{:S(2)}) collective-permute-start(bf16[2,128,256]{2,1,0:T(8,128)(2,1)S(1)} %pad_maximum_fusion), channel_id=1, source_target_pairs={{0,31},{1,2},{2,1},{3,4},{4,3},{5,6},{6,5},{7,8},{8,7},{9,10},{10,... | collective-permute-start | bytes 393224 | tf_op jit(solution)/shard_map/ppermute | solution.py:589
  67.8 6.2 %copy-start.2 = (bf16[4,4,128,256]{3,2,1,0:T(8,128)(2,1)S(1)}, bf16[4,4,128,256]{3,2,1,0:T(8,128)(2,1)}, u32[]{:S(2)}) copy-start(bf16[4,4,128,256]{3,2,1,0:T(8,128)(2,1)} %cotangent_ref.1) | copy-start | bytes 3145732
  86.9 4.0 %collective-permute-start.11 = (bf16[32,8,16,128]{3,2,1,0:T(8,128)(2,1)S(1)}, bf16[32,8,16,128]{3,2,1,0:T(8,128)(2,1)S(1)}, u32[]{:S(2)}, u32[]{:S(2)}) collective-permute-start(bf16[32,8,16,128]{3,2,1,0:T(8,128)(2,1)S(1)} %get-tuple-element.53), channel_id=1, source_target_pairs={{0,32},{32,0},{64,96},{96,64},{1,33},{33,1},{65,97},{97,65},{2,34}... | collective-permute-start | bytes 3145736 | tf_op jit(solution)/shard_map/ppermute | solution.py:463
  97.1 4.9 %collective-permute-start.18 = (bf16[32,6,16,128]{3,2,1,0:T(8,128)(2,1)S(1)}, bf16[32,6,16,128]{3,2,1,0:T(8,128)(2,1)S(1)}, u32[]{:S(2)}, u32[]{:S(2)}) collective-permute-start(bf16[32,6,16,128]{3,2,1,0:T(8,128)(2,1)S(1)} %get-tuple-element.59), channel_id=1, source_target_pairs={{0,32},{32,0},{64,96},{96,64},{1,33},{33,1},{65,97},{97,65},{2,34}... | collective-permute-start | bytes 2359304 | tf_op jit(solution)/shard_map/ppermute | solution.py:463
  97.8 7.8 %collective-permute-start.12 = (bf16[2,4,8,16,128]{4,3,2,1,0:T(8,128)(2,1)S(1)}, bf16[2,4,8,16,128]{4,3,2,1,0:T(8,128)(2,1)S(1)}, u32[]{:S(2)}, u32[]{:S(2)}) collective-permute-start(bf16[2,4,8,16,128]{4,3,2,1,0:T(8,128)(2,1)S(1)} %get-tuple-element.64), channel_id=1, source_target_pairs={{0,1},{1,0},{2,3},{3,2},{4,5},{5,4},{6,7},{7,6},{8,9},{9,8},{10,11... | collective-permute-start | bytes 786440 | tf_op jit(solution)/shard_map/ppermute | solution.py:473
  99.0 14.9 %collective-permute-start.13 = (bf16[2,4,8,16,128]{4,3,2,1,0:T(8,128)(2,1)S(1)}, bf16[2,4,8,16,128]{4,3,2,1,0:T(8,128)(2,1)S(1)}, u32[]{:S(2)}, u32[]{:S(2)}) collective-permute-start(bf16[2,4,8,16,128]{4,3,2,1,0:T(8,128)(2,1)S(1)} %get-tuple-element.66), channel_id=1, source_target_pairs={{0,2},{1,3},{2,0},{3,1},{4,6},{5,7},{6,4},{7,5},{8,10},{9,11},{10,... | collective-permute-start | bytes 786440 | tf_op jit(solution)/shard_map/ppermute | solution.py:473
  102.0 14.0 %collective-permute-start.14 = (bf16[2,4,8,16,128]{4,3,2,1,0:T(8,128)(2,1)S(1)}, bf16[2,4,8,16,128]{4,3,2,1,0:T(8,128)(2,1)S(1)}, u32[]{:S(2)}, u32[]{:S(2)}) collective-permute-start(bf16[2,4,8,16,128]{4,3,2,1,0:T(8,128)(2,1)S(1)} %get-tuple-element.65), channel_id=1, source_target_pairs={{0,3},{1,2},{2,1},{3,0},{4,7},{5,6},{6,5},{7,4},{8,11},{9,10},{10,... | collective-permute-start | bytes 786440 | tf_op jit(solution)/shard_map/ppermute | solution.py:473
  102.3 14.6 %collective-permute-start.19 = (bf16[2,4,6,16,128]{4,3,2,1,0:T(8,128)(2,1)S(1)}, bf16[2,4,6,16,128]{4,3,2,1,0:T(8,128)(2,1)S(1)}, u32[]{:S(2)}, u32[]{:S(2)}) collective-permute-start(bf16[2,4,6,16,128]{4,3,2,1,0:T(8,128)(2,1)S(1)} %get-tuple-element.67), channel_id=1, source_target_pairs={{0,4},{1,5},{2,6},{3,7},{4,0},{5,1},{6,2},{7,3},{8,12},{9,13},{10,... | collective-permute-start | bytes 589832 | tf_op jit(solution)/shard_map/ppermute | solution.py:473
  103.3 16.8 %collective-permute-start.20 = (bf16[2,4,6,16,128]{4,3,2,1,0:T(8,128)(2,1)S(1)}, bf16[2,4,6,16,128]{4,3,2,1,0:T(8,128)(2,1)S(1)}, u32[]{:S(2)}, u32[]{:S(2)}) collective-permute-start(bf16[2,4,6,16,128]{4,3,2,1,0:T(8,128)(2,1)S(1)} %get-tuple-element.69), channel_id=1, source_target_pairs={{0,8},{1,9},{2,10},{3,11},{4,12},{5,13},{6,14},{7,15},{8,0},{9,1},... | collective-permute-start | bytes 589832 | tf_op jit(solution)/shard_map/ppermute | solution.py:473
  105.6 14.5 %collective-permute-start.21 = (bf16[2,4,6,16,128]{4,3,2,1,0:T(8,128)(2,1)S(1)}, bf16[2,4,6,16,128]{4,3,2,1,0:T(8,128)(2,1)S(1)}, u32[]{:S(2)}, u32[]{:S(2)}) collective-permute-start(bf16[2,4,6,16,128]{4,3,2,1,0:T(8,128)(2,1)S(1)} %get-tuple-element.68), channel_id=1, source_target_pairs={{0,12},{1,13},{2,14},{3,15},{4,8},{5,9},{6,10},{7,11},{8,4},{9,5},... | collective-permute-start | bytes 589832 | tf_op jit(solution)/shard_map/ppermute | solution.py:473
  116.1 5.7 %collective-permute-start.15 = (bf16[2,8,16,128]{3,2,1,0:T(8,128)(2,1)S(1)}, bf16[2,8,16,128]{3,2,1,0:T(8,128)(2,1)S(1)}, u32[]{:S(2)}, u32[]{:S(2)}) collective-permute-start(bf16[2,8,16,128]{3,2,1,0:T(8,128)(2,1)S(1)} %get-tuple-element.70), channel_id=1, source_target_pairs={{0,4},{1,5},{2,6},{3,7},{4,0},{5,1},{6,2},{7,3},{8,12},{9,13},{10,... | collective-permute-start | bytes 196616 | tf_op jit(solution)/shard_map/ppermute | solution.py:473
  116.2 7.9 %collective-permute-start.16 = (bf16[2,8,16,128]{3,2,1,0:T(8,128)(2,1)S(1)}, bf16[2,8,16,128]{3,2,1,0:T(8,128)(2,1)S(1)}, u32[]{:S(2)}, u32[]{:S(2)}) collective-permute-start(bf16[2,8,16,128]{3,2,1,0:T(8,128)(2,1)S(1)} %get-tuple-element.72), channel_id=1, source_target_pairs={{0,8},{1,9},{2,10},{3,11},{4,12},{5,13},{6,14},{7,15},{8,0},{9,1},... | collective-permute-start | bytes 196616 | tf_op jit(solution)/shard_map/ppermute | solution.py:473
  116.8 7.3 %collective-permute-start.17 = (bf16[2,8,16,128]{3,2,1,0:T(8,128)(2,1)S(1)}, bf16[2,8,16,128]{3,2,1,0:T(8,128)(2,1)S(1)}, u32[]{:S(2)}, u32[]{:S(2)}) collective-permute-start(bf16[2,8,16,128]{3,2,1,0:T(8,128)(2,1)S(1)} %get-tuple-element.71), channel_id=1, source_target_pairs={{0,12},{1,13},{2,14},{3,15},{4,8},{5,9},{6,10},{7,11},{8,4},{9,5},... | collective-permute-start | bytes 196616 | tf_op jit(solution)/shard_map/ppermute | solution.py:473
  120.2 4.0 %collective-permute-start.22 = (bf16[2,6,16,128]{3,2,1,0:T(8,128)(2,1)S(1)}, bf16[2,6,16,128]{3,2,1,0:T(8,128)(2,1)S(1)}, u32[]{:S(2)}, u32[]{:S(2)}) collective-permute-start(bf16[2,6,16,128]{3,2,1,0:T(8,128)(2,1)S(1)} %get-tuple-element.81), channel_id=1, source_target_pairs={{0,1},{1,0},{2,3},{3,2},{4,5},{5,4},{6,7},{7,6},{8,9},{9,8},{10,11... | collective-permute-start | bytes 147464 | tf_op jit(solution)/shard_map/ppermute | solution.py:473
  120.3 4.5 %collective-permute-start.23 = (bf16[2,6,16,128]{3,2,1,0:T(8,128)(2,1)S(1)}, bf16[2,6,16,128]{3,2,1,0:T(8,128)(2,1)S(1)}, u32[]{:S(2)}, u32[]{:S(2)}) collective-permute-start(bf16[2,6,16,128]{3,2,1,0:T(8,128)(2,1)S(1)} %get-tuple-element.83), channel_id=1, source_target_pairs={{0,2},{1,3},{2,0},{3,1},{4,6},{5,7},{6,4},{7,5},{8,10},{9,11},{10,... | collective-permute-start | bytes 147464 | tf_op jit(solution)/shard_map/ppermute | solution.py:473
  121.8 4.2 %collective-permute-start.24 = (bf16[2,6,16,128]{3,2,1,0:T(8,128)(2,1)S(1)}, bf16[2,6,16,128]{3,2,1,0:T(8,128)(2,1)S(1)}, u32[]{:S(2)}, u32[]{:S(2)}) collective-permute-start(bf16[2,6,16,128]{3,2,1,0:T(8,128)(2,1)S(1)} %get-tuple-element.82), channel_id=1, source_target_pairs={{0,3},{1,2},{2,1},{3,0},{4,7},{5,6},{6,5},{7,4},{8,11},{9,10},{10,... | collective-permute-start | bytes 147464 | tf_op jit(solution)/shard_map/ppermute | solution.py:473
  126.0 3.4 %collective-permute-start.25 = (bf16[14,16,128]{2,1,0:T(8,128)(2,1)S(1)}, bf16[14,16,128]{2,1,0:T(8,128)(2,1)S(1)}, u32[]{:S(2)}, u32[]{:S(2)}) collective-permute-start(bf16[14,16,128]{2,1,0:T(8,128)(2,1)S(1)} %get-tuple-element.79), channel_id=1, source_target_pairs={{0,16},{1,17},{2,18},{3,19},{4,20},{5,21},{6,22},{7,23},{8,24},{9,... | collective-permute-start | bytes 172040 | tf_op jit(solution)/shard_map/ppermute | solution.py:612
  127.1 4.2 %collective-permute-start.26 = (bf16[14,16,128]{2,1,0:T(8,128)(2,1)S(1)}, bf16[14,16,128]{2,1,0:T(8,128)(2,1)S(1)}, u32[]{:S(2)}, u32[]{:S(2)}) collective-permute-start(bf16[14,16,128]{2,1,0:T(8,128)(2,1)S(1)} %get-tuple-element.79), channel_id=1, source_target_pairs={{0,80},{1,81},{2,82},{3,83},{4,84},{5,85},{6,86},{7,87},{8,88},{9,... | collective-permute-start | bytes 172040 | tf_op jit(solution)/shard_map/ppermute | solution.py:613
  129.0 4.5 %collective-permute-start.27 = (bf16[14,16,128]{2,1,0:T(8,128)(2,1)S(1)}, bf16[14,16,128]{2,1,0:T(8,128)(2,1)S(1)}, u32[]{:S(2)}, u32[]{:S(2)}) collective-permute-start(bf16[14,16,128]{2,1,0:T(8,128)(2,1)S(1)} %get-tuple-element.80), channel_id=1, source_target_pairs={{0,64},{32,96},{64,0},{96,32},{1,65},{33,97},{65,1},{97,33},{2,66}... | collective-permute-start | bytes 172040 | tf_op jit(solution)/shard_map/ppermute | solution.py:614
  133.6 6.6 %collective-permute-start.28 = (f32[14,16,128]{2,1,0:T(8,128)S(1)}, f32[14,16,128]{2,1,0:T(8,128)S(1)}, u32[]{:S(2)}, u32[]{:S(2)}) collective-permute-start(f32[14,16,128]{2,1,0:T(8,128)S(1)} %convert_add_fusion.3), channel_id=1, source_target_pairs={{0,32},{32,0},{64,96},{96,64},{1,33},{33,1},{65,97},{97,65},{2,34}... | collective-permute-start | bytes 344072 | tf_op jit(solution)/shard_map/ppermute | solution.py:616
